TPU v7x, 512 devices: a whole 4x8x8 slice. The times are simulated.
512 devices in a mesh: row: 16 (over x, y_hi), col: 32 (over y_lo, z, core).
Axes of the slice: x: 4, y: 8 (y_hi: 4, y_lo: 2; y = y_hi * 2 + y_lo), z: 8, core: 2. Of those that a mesh axis runs over, the one named last changes fastest.
Arguments:
- activations: bfloat16 [2048, 57344], P(('row', 'col')), as said below
Outputs:
- correlation: bfloat16 [8192, 57344], P('row', 'col')
Inputs may be any that keep to these rules, and one draw needn't show every extreme that they name: `activations`: finite values; each unit has a spread of order one or more over the tokens.
All inputs are finite; a program needn't handle non-finite values.
Results may differ from a plain program's by a relative error of at most 0.0039.
Values may be sent and summed in bfloat16 or wider, within the bound.
No kernel may reach another device: no remote copies, remote signals or barrier semaphores. Data moves between devices by JAX's collectives and lax.ppermute only.
A program may use at most 64 MiB of HBM per device.

v0:
```python
import jax
import jax.numpy as jnp
from jax import lax
from jax.sharding import PartitionSpec as P

ROWS_DEV = 512


EPS = 1e-06


def standard_local(values):
    widened = values.astype(jnp.float32)
    mean = jnp.mean(widened, axis=0)
    centered = widened - mean
    spread = jnp.sqrt(jnp.mean(centered * centered, axis=0) + EPS)
    return (centered / spread).astype(jnp.bfloat16)


def reorder_tokens(gathered, n_col, n_row, tok_dev):
    width = gathered.shape[1]
    split_up = gathered.reshape(n_col, n_row, tok_dev, width)
    return split_up.transpose(1, 0, 2, 3).reshape(n_col * n_row * tok_dev, width)


def per_device(activations):
    n_row = lax.axis_size("row")
    n_col = lax.axis_size("col")
    tok_dev = activations.shape[0]
    total = tok_dev * n_row * n_col
    slab = ROWS_DEV * n_row
    column_local = lax.all_to_all(activations, "col", split_axis=1, concat_axis=0, tiled=True)
    slab_local = lax.all_to_all(
        activations[:, :slab], "row", split_axis=1, concat_axis=0, tiled=True
    )
    slab_all = reorder_tokens(
        lax.all_gather(slab_local, "col", axis=0, tiled=True), n_col, n_row, tok_dev
    )
    dims = (((0,), (0,)), ((), ()))
    slab_standard = standard_local(slab_all)
    column_all = lax.all_gather(column_local, "row", axis=0, tiled=True)
    column_standard = standard_local(column_all)
    product = lax.dot_general(
        slab_standard, column_standard, dims, preferred_element_type=jnp.float32
    )
    return (product / total).astype(jnp.bfloat16)


def solution(mesh):
    in_specs = (P(("row", "col"), None),)
    out_specs = P("row", "col")
    return jax.shard_map(
        per_device, mesh=mesh, in_specs=in_specs, out_specs=out_specs, check_vma=False
    )
```

profile of v0, /device:TPU:6, one launch (start us, length us, event | category | flops | bytes accessed | tf_op | source)
XLA Modules:
  0.0 227.5 jit_solution(10187959690399844966)
XLA Ops:
  6.5 0.0 all-gather.3.cloned.1.call-start
  6.5 0.9 slice.3
  7.4 17.9 %all_to_all.38 = bf16[4,16,512]{2,0,1:T(4,128)(2,1)S(1)} all-to-all(bf16[4,16,512]{2,0,1:T(4,128)(2,1)S(1)} %bitcast.11), channel_id=1, replica_groups=mesh['row'=16,'col'=32] {'row'}, dimensions={1} | all-to-all | bytes 131072 | tf_op jit(solution)/shard_map/all_to_all | solution.py:33
  25.3 0.6 all_to_all.31
  25.9 0.0 all-gather.3.cloned.1.call-update
  26.0 0.0 all-gather.5.cloned.1.call-start
  26.0 26.5 %all_to_all.39 = bf16[4,32,1792]{2,0,1:T(4,128)(2,1)S(1)} all-to-all(bf16[4,32,1792]{2,0,1:T(4,128)(2,1)} %bitcast.9), channel_id=1, replica_groups=mesh['row'=16,'col'=32] {'col'}, dimensions={1} | all-to-all | bytes 917504 | tf_op jit(solution)/shard_map/all_to_all | solution.py:32
  52.5 0.9 all_to_all.35
  53.4 0.0 all-gather.5.cloned.1.call-update
  53.4 43.8 %all-gather.3.cloned.1.call-done = bf16[2048,512]{1,0:T(8,128)(2,1)} async-done(((bf16[64,512]{1,0:T(8,128)(2,1)}), bf16[2048,512]{1,0:T(8,128)(2,1)}) %all-gather.3.cloned.1.call-update) | async-done | bytes 2097168 | tf_op jit(solution)/shard_map/all_gather | solution.py:37
  97.2 4.7 %reshape.35 = f32[32,16,4,512]{3,2,1,0:T(4,128)} reshape(bf16[2048,512]{1,0:T(8,128)(2,1)} %all-gather.3.cloned.1.call-done) | data formatting | bytes 6291456 | tf_op jit(solution)/shard_map/convert_element_type | solution.py:13
  102.0 5.3 %copy.6 = f32[32,16,4,512]{3,2,0,1:T(4,128)} copy(f32[32,16,4,512]{3,2,1,0:T(4,128)} %reshape.35) | data formatting | bytes 8388608 | tf_op jit(solution)/shard_map/convert_element_type | solution.py:13
  107.2 0.0 copy-start.1
  107.2 5.4 %reshape.34 = f32[2048,512]{1,0:T(8,128)} reshape(f32[16,32,4,512]{3,2,1,0:T(4,128)} %bitcast.7) | data formatting | bytes 8388608 | tf_op jit(solution)/shard_map/convert_element_type | solution.py:13
  112.7 0.0 copy-done.1
  112.7 0.3 convert_reduce_fusion.1
  113.0 3.5 %multiply_reduce_fusion = f32[512]{0:T(512)S(1)} fusion(f32[32,16,4,512]{3,2,1,0:T(4,128)} %reshape.35, f32[512]{0:T(512)S(1)} %broadcast_multiply_fusion.1), kind=kLoop, calls=%fused_computation.9 | loop fusion | flops 3145216 | bytes 4198400 | tf_op jit(solution)/shard_map/reduce_sum | solution.py:16
  116.5 91.6 %all-gather.5.cloned.1.call-done = bf16[2048,1792]{1,0:T(8,128)(2,1)} async-done(((bf16[128,1792]{1,0:T(8,128)(2,1)}), bf16[2048,1792]{1,0:T(8,128)(2,1)}) %all-gather.5.cloned.1.call-update) | async-done | bytes 7340048 | tf_op jit(solution)/shard_map/all_gather | solution.py:41
  208.1 0.0 copy-start
  208.1 4.3 %convert_reduce_fusion = f32[1792]{0:T(1024)S(1)} fusion(bf16[2048,1792]{1,0:T(8,128)(2,1)} %all-gather.5.cloned.1.call-done), kind=kLoop, calls=%fused_computation.1 | loop fusion | flops 7338240 | bytes 7347200 | tf_op jit(solution)/shard_map/reduce_sum | solution.py:14
  212.4 0.9 copy-done
  213.2 2.0 fusion.2
  215.2 0.0 copy-done.2
  215.2 5.4 %multiply_convert_fusion = bf16[512,1792]{1,0:T(8,128)(2,1)} fusion(bf16[2048,1792]{1,0:T(8,128)(2,1)S(1)} %copy-done, f32[1792]{0:T(1024)S(1)} %add_sqrt_fusion, f32[1792]{0:T(1024)S(1)} %broadcast_multiply_fusion, f32[2048,512]{1,0:T(8,128)S(1)} %copy-done.2, f32[512]{0:T(512)S(1)} %add_sqrt_fusion.1, f32[512]{0:T(512)S(1)} %broadcast_multiply_fusion.1), kind=kOutput, calls=%fused_computation.10 | convolution fusion | flops 3777757184 | bytes 13387776 | tf_op jit(solution)/shard_map/dot_general | solution.py:43
  (5 shorter events, 0.0 us)
Async XLA Ops:
  6.5 90.7 %all-gather.3.cloned.1.call-start = ((), (), s32[]{:S(2)}) async-start(), calls=%async_computation.2 | async-start | bytes 2162688 | tf_op jit(solution)/shard_map/all_gather | solution.py:37
  26.0 182.1 %all-gather.5.cloned.1.call-start = ((), (), s32[]{:S(2)}) async-start(), calls=%async_computation.3 | async-start | bytes 7798784 | tf_op jit(solution)/shard_map/all_gather | solution.py:41
  107.2 5.4 %copy-start.1 = (bf16[2048,512]{1,0:T(8,128)(2,1)S(1)}, bf16[2048,512]{1,0:T(8,128)(2,1)}, u32[]{:S(2)}) copy-start(bf16[2048,512]{1,0:T(8,128)(2,1)} %all-gather.3.cloned.1.call-done) | copy-start | bytes 6291460
  208.1 5.2 %copy-start = (bf16[2048,1792]{1,0:T(8,128)(2,1)S(1)}, bf16[2048,1792]{1,0:T(8,128)(2,1)}, u32[]{:S(2)}) copy-start(bf16[2048,1792]{1,0:T(8,128)(2,1)} %all-gather.5.cloned.1.call-done) | copy-start | bytes 22020100
  212.4 2.8 %copy-start.2 = (f32[2048,512]{1,0:T(8,128)S(1)}, f32[2048,512]{1,0:T(8,128)}, u32[]{:S(2)}) copy-start(f32[2048,512]{1,0:T(8,128)} %reshape.34) | copy-start | bytes 12582916
Sparse Core Ops, SparseCore 0:
  26.1 71.0 all-gather.2
  100.3 107.7 all-gather.4
where the time goes:
time: 229 us; the launch traced here: 227 us
  waiting for transfers between devices  135 us (59%)
  blocking collectives  44.4 us (19%)
  local copies, waits for them, and re-layouts  18.7 us (8%)
  between operations  13.4 us (6%)
  other arithmetic  10.1 us (4%)
  matrix products  5.44 us (2%)
    all_gather x1, waiting for transfers between devices, per_device(): column_all = lax.all_gather(column_local, 'row', axis=0, tiled=True)  91.6 us
    all_gather x1, waiting for transfers between devices, per_device(): lax.all_gather(slab_local, 'col', axis=0, tiled=True)  43.8 us
    all_to_all x1, blocking collectives, per_device(): lax.all_to_all(activations, 'col', split_axis=1, concat_axis=0, tiled=True)  26.5 us
    all_to_all x1, blocking collectives, per_device(): lax.all_to_all(activations[:, :slab], 'row', split_axis=1, concat_axis=0,...  17.9 us
    convert_element_type x3, local copies, waits for them, and re-layouts, standard_local(): widened = values.astype(jnp.float32)  15.4 us
    dot_general x1, matrix products, per_device(): lax.dot_general(slab_standard, column_standard, dims, preferred_element_t...  5.44 us
    reduce_sum x2, other arithmetic, standard_local(): spread = jnp.sqrt(jnp.mean(centered * centered, axis=0) + EPS)  5.42 us
    reduce_sum x2, other arithmetic, standard_local(): mean = jnp.mean(widened, axis=0)  4.64 us
  transfers between devices with their start and end apart: 2, of which 2 were waited for; matrix products, arithmetic and copies ran while one was open for 8% of the time, Pallas kernels for 0%

commit v1 on v0

v1 whole, which is shorter than its diff:
```python
import jax
import jax.numpy as jnp
from jax import lax
from jax.experimental import pallas as pl
from jax.experimental.pallas import tpu as pltpu
from jax.sharding import Mesh, PartitionSpec as P

ROWS_DEV = 512
EPS = 1e-06
TOKENS = 2048
FIRST = 1280
PIECE = 128
TILE = 256


def pairs(core_first):
    perm = []
    for i in range(4):
        for core in range(2):
            flip = core_first if core == 0 else 4 - core_first
            perm.append((i * 2 + core, (i ^ flip) * 2 + core))
    return perm


def exchange(values, axis, step):
    return lax.ppermute(values, (axis, "c"), pairs(1 if step == 0 else 3))


def slab_kernel(order_ref, slab_ref, out_ref, wide, piece):
    n = TOKENS // PIECE
    for block in range(ROWS_DEV // 128):
        lanes = slice(block * 128, (block + 1) * 128)

        def widen(i, total):
            rows = pl.ds(pl.multiple_of(i * PIECE, PIECE), PIECE)
            values = slab_ref[rows, lanes].astype(jnp.float32)
            wide[block, rows, :] = values
            return total + jnp.sum(values.reshape(PIECE // 8, 8, 128), axis=0)

        def square(i, total):
            centered = wide[block, pl.ds(pl.multiple_of(i * PIECE, PIECE), PIECE), :] - mean
            return total + jnp.sum((centered * centered).reshape(PIECE // 8, 8, 128), axis=0)

        zero = jnp.zeros((8, 128), jnp.float32)
        mean = jnp.sum(lax.fori_loop(0, n, widen, zero), axis=0, keepdims=True) / TOKENS
        variance = jnp.sum(lax.fori_loop(0, n, square, zero), axis=0, keepdims=True) / TOKENS
        scale = 1.0 / jnp.sqrt(variance + EPS)
        for slot in range(n):
            first = order_ref[slot] * 8
            for half in range(2):
                for token in range(4):
                    rows = wide[block, pl.ds(first + half * 4 + token, 16, stride=128), :]
                    piece[pl.ds(half * 64 + token, 16, stride=4), :] = rows
            standard = (piece[...] - mean) * scale
            out_ref[lanes, slot * PIECE : (slot + 1) * PIECE] = standard.T.astype(jnp.bfloat16)


def slab_standard(slab, order):
    return pl.pallas_call(
        slab_kernel,
        out_shape=jax.ShapeDtypeStruct((ROWS_DEV, TOKENS), jnp.bfloat16),
        in_specs=[pl.BlockSpec(memory_space=pltpu.SMEM), pl.BlockSpec(memory_space=pltpu.VMEM)],
        out_specs=pl.BlockSpec(memory_space=pltpu.VMEM),
        scratch_shapes=[
            pltpu.VMEM((ROWS_DEV // 128, TOKENS, 128), jnp.float32),
            pltpu.VMEM((PIECE, 128), jnp.float32),
        ],
        compiler_params=pltpu.CompilerParams(vmem_limit_bytes=24 * 2**20),
        cost_estimate=pl.CostEstimate(flops=8 * TOKENS * ROWS_DEV, bytes_accessed=4 * TOKENS * ROWS_DEV, transcendentals=0),
    )(order, slab)


def columns_kernel(slab_ref, own, x1, x2, y1, y2, x3, x4, y3, y4, out_ref, standard):
    def tiles(pieces, n_tiles, offset):
        @pl.loop(0, n_tiles)
        def _(j):
            def load(slot):
                ref, row, shift = pieces[slot]
                lanes = pl.ds(pl.multiple_of(j * TILE + shift, TILE), TILE)
                return ref[row : row + PIECE, lanes].astype(jnp.float32)

            total = jnp.zeros((8, TILE), jnp.float32)
            for slot in range(16):
                total += jnp.sum(load(slot).reshape(PIECE // 8, 8, TILE), axis=0)
            mean = jnp.sum(total, axis=0, keepdims=True) / TOKENS
            total = jnp.zeros((8, TILE), jnp.float32)
            for slot in range(16):
                centered = load(slot) - mean
                total += jnp.sum((centered * centered).reshape(PIECE // 8, 8, TILE), axis=0)
            spread = jnp.sqrt(jnp.sum(total, axis=0, keepdims=True) / TOKENS + EPS)
            scale = 1.0 / spread
            for slot in range(16):
                standard[slot * PIECE : (slot + 1) * PIECE, :] = ((load(slot) - mean) * scale).astype(jnp.bfloat16)
            product = jnp.dot(slab_ref[...], standard[...], preferred_element_type=jnp.float32)
            lanes = pl.ds(pl.multiple_of(j * TILE + offset, TILE), TILE)
            out_ref[:, lanes] = (product / TOKENS).astype(jnp.bfloat16)

    def at(ref, i, shift=0):
        return (ref, i * PIECE, shift)

    tiles(
        [at(own, 0), at(x1, 0), at(x2, 0), at(x2, 1)]
        + [at(y1, 0), at(x3, 0), at(x4, 0), at(x4, 3)]
        + [at(y2, 0), at(x3, 1), at(x4, 1), at(x4, 4)]
        + [at(y2, 1), at(x3, 2), at(x4, 2), at(x4, 5)],
        FIRST // TILE,
        0,
    )
    width = own.shape[1]
    tiles(
        [at(own, 0, FIRST), at(x1, 0, FIRST), at(x2, 0, FIRST), at(x2, 1, FIRST)]
        + [at(y3, i) for i in range(4)]
        + [at(y4, i) for i in range(8)],
        (width - FIRST) // TILE,
        FIRST,
    )


def correlate(slab, pieces):
    width = pieces[0].shape[1]
    return pl.pallas_call(
        columns_kernel,
        out_shape=jax.ShapeDtypeStruct((ROWS_DEV, width), jnp.bfloat16),
        in_specs=[pl.BlockSpec(memory_space=pltpu.VMEM)] * (1 + len(pieces)),
        out_specs=pl.BlockSpec(memory_space=pltpu.VMEM),
        scratch_shapes=[pltpu.VMEM((TOKENS, TILE), jnp.bfloat16)],
        compiler_params=pltpu.CompilerParams(vmem_limit_bytes=24 * 2**20),
        cost_estimate=pl.CostEstimate(
            flops=2 * TOKENS * ROWS_DEV * width, bytes_accessed=2 * TOKENS * (ROWS_DEV + width), transcendentals=0
        ),
    )(slab, *pieces)


def per_device(activations):
    slab_width = ROWS_DEV * 16
    slab_own = activations[:, :slab_width]
    slab_other = lax.ppermute(slab_own, "yl", [(0, 1), (1, 0)])
    first = lax.axis_index("yl") == 0
    slab_pair = jnp.concatenate(
        [jnp.where(first, slab_own, slab_other), jnp.where(first, slab_other, slab_own)], axis=0
    )

    own = lax.all_to_all(activations, ("yl", "z", "c"), split_axis=1, concat_axis=0, tiled=True)
    x1 = exchange(own, "x", 0)
    own_first = own[:, :FIRST]
    y1 = exchange(own_first, "yh", 0)
    slab_local = lax.all_to_all(slab_pair, ("x", "yh"), split_axis=1, concat_axis=0, tiled=True)
    slab_all = lax.all_gather(slab_local, ("z", "c"), axis=0, tiled=True)
    x2 = exchange(jnp.concatenate([own, x1], axis=0), "x", 1)
    y2 = exchange(jnp.concatenate([own_first, y1], axis=0), "yh", 1)
    rest = jnp.concatenate([own[:, FIRST:], x1[:, FIRST:], x2[:, FIRST:]], axis=0)
    three = jnp.concatenate([y1, y2], axis=0)
    x3 = exchange(three, "x", 0)
    y3 = exchange(rest, "yh", 0)
    x4 = exchange(jnp.concatenate([three, x3], axis=0), "x", 1)
    y4 = exchange(jnp.concatenate([rest, y3], axis=0), "yh", 1)

    near = jnp.where(lax.axis_index("c") == 0, 1, 3)
    flips = jnp.stack([0 * near, near, 4 - near, 2 + 0 * near])
    x_of = lax.axis_index("x") ^ flips
    y_of = lax.axis_index("yh") ^ flips
    order = (x_of[None, :] * 4 + y_of[:, None]).reshape(16).astype(jnp.int32)
    slab = slab_standard(slab_all, order)
    return correlate(slab, [own, x1, x2, y1, y2, x3, x4, y3, y4])


def solution(mesh):
    fine = Mesh(mesh.devices.reshape(4, 4, 2, 8, 2), ("x", "yh", "yl", "z", "c"))
    in_specs = (P(("x", "yh", "yl", "z", "c"), None),)
    out_specs = P(("x", "yh"), ("yl", "z", "c"))
    return jax.shard_map(per_device, mesh=fine, in_specs=in_specs, out_specs=out_specs, check_vma=False)
```

time: 229 us -> 186 us (0.81)
  the two profiles are of different devices: /device:TPU:6 before, /device:TPU:16 now
where the time goes in v1:
time: 186 us; the launch traced here: 185 us
  waiting for transfers between devices  75.4 us (41%)
  starting transfers between devices  70 us (38%)
  Pallas kernels  18.4 us (10%)
  between operations  13.6 us (7%)
  other arithmetic  4.47 us (2%)
  local copies, waits for them, and re-layouts  3.4 us (2%)
    ppermute x8, waiting for transfers between devices, exchange(): return lax.ppermute(values, (axis, 'c'), pairs(1 if step == 0 else 3))  58.8 us
    ppermute x8, starting transfers between devices, exchange(): return lax.ppermute(values, (axis, 'c'), pairs(1 if step == 0 else 3))  45.5 us
    all_to_all x1, waiting for transfers between devices, per_device(): lax.all_to_all(activations, ('yl', 'z', 'c'), split_axis=1, concat_axis=0...  13.7 us
    pallas_call x1, Pallas kernels, correlate(): pl.pallas_call(columns_kernel, out_shape=jax.ShapeDtypeStruct((ROWS_DEV,...  11.9 us
    all_to_all x1, starting transfers between devices, per_device(): lax.all_to_all(activations, ('yl', 'z', 'c'), split_axis=1, concat_axis=0...  10.7 us
    all_to_all x1, starting transfers between devices, per_device(): lax.all_to_all(slab_pair, ('x', 'yh'), split_axis=1, concat_axis=0, tiled...  10.2 us
    pallas_call x1, Pallas kernels, slab_standard(): pl.pallas_call(slab_kernel, out_shape=jax.ShapeDtypeStruct((ROWS_DEV, TOK...  6.51 us
  transfers between devices with their start and end apart: 12, of which 6 were waited for; matrix products, arithmetic and copies ran while one was open for 2% of the time, Pallas kernels for 4%

profile of v1, /device:TPU:16, one launch (start us, length us, event | category | flops | bytes accessed | tf_op | source)
XLA Modules:
  0.0 185.3 jit_solution(4501762539946896039)
XLA Ops:
  6.5 0.9 slice.15
  7.4 3.5 %collective-permute-start = (bf16[4,8192]{1,0:T(4,128)(2,1)S(1)}, bf16[4,8192]{1,0:T(4,128)(2,1)S(1)}, u32[]{:S(2)}, u32[]{:S(2)}) collective-permute-start(bf16[4,8192]{1,0:T(4,128)(2,1)S(1)} %slice.15), channel_id=1, source_target_pairs={{0,16},{16,0},{1,17},{17,1},{2,18},{18,2},{3,19},{19,3},{4,20},{20... | collective-permute-start | bytes 196616 | tf_op jit(solution)/shard_map/ppermute | solution.py:137
  10.9 10.7 %all-to-all-start.1 = ((bf16[4,32,1792]{2,0,1:T(4,128)(2,1)}), bf16[4,32,1792]{2,0,1:T(4,128)(2,1)S(1)}, u32[]{:S(2)}, u32[]{:S(2)}) async-start(bf16[4,32,1792]{2,0,1:T(4,128)(2,1)} %bitcast.9), calls=%async_computation.1 | async-start | bytes 917504 | tf_op jit(solution)/shard_map/all_to_all | solution.py:143
  21.6 0.9 broadcast_select_fusion.1
  22.6 13.7 %all-to-all-done.1 = bf16[4,32,1792]{2,0,1:T(4,128)(2,1)S(1)} async-done(((bf16[4,32,1792]{2,0,1:T(4,128)(2,1)}), bf16[4,32,1792]{2,0,1:T(4,128)(2,1)S(1)}, u32[]{:S(2)}, u32[]{:S(2)}) %all-to-all-start.1) | async-done | bytes 458784 | tf_op jit(solution)/shard_map/all_to_all | solution.py:143
  36.4 2.2 %collective-permute-start.3 = (bf16[128,1280]{1,0:T(8,128)(2,1)S(1)}, bf16[128,1280]{1,0:T(8,128)(2,1)S(1)}, u32[]{:S(2)}, u32[]{:S(2)}) collective-permute-start(bf16[128,1280]{1,0:T(8,128)(2,1)S(1)} %slice.20), channel_id=1, source_target_pairs={{0,32},{1,97},{32,0},{33,65},{64,96},{65,33},{96,64},{97,1},{2,34}... | collective-permute-start | bytes 983048 | tf_op jit(solution)/shard_map/ppermute | solution.py:26
  39.4 10.2 %all-to-all-start = ((bf16[8,16,512]{2,0,1:T(8,128)(2,1)}), bf16[8,16,512]{2,0,1:T(8,128)(2,1)S(1)}, u32[]{:S(2)}, u32[]{:S(2)}) async-start(bf16[8,16,512]{2,0,1:T(8,128)(2,1)} %bitcast.2), calls=%async_computation | async-start | bytes 262144 | tf_op jit(solution)/shard_map/all_to_all | solution.py:147
  49.8 5.6 %collective-permute-start.4 = (bf16[256,1280]{1,0:T(8,128)(2,1)S(1)}, bf16[256,1280]{1,0:T(8,128)(2,1)S(1)}, u32[]{:S(2)}, u32[]{:S(2)}) collective-permute-start(bf16[256,1280]{1,0:T(8,128)(2,1)S(1)} %pad_maximum_fusion.4), channel_id=1, source_target_pairs={{0,96},{1,33},{32,64},{33,1},{64,32},{65,97},{96,0},{97,65},{2,98}... | collective-permute-start | bytes 1966088 | tf_op jit(solution)/shard_map/ppermute | solution.py:26
  55.3 2.9 %all-to-all-done = bf16[8,16,512]{2,0,1:T(8,128)(2,1)S(1)} async-done(((bf16[8,16,512]{2,0,1:T(8,128)(2,1)}), bf16[8,16,512]{2,0,1:T(8,128)(2,1)S(1)}, u32[]{:S(2)}, u32[]{:S(2)}) %all-to-all-start) | async-done | bytes 131104 | tf_op jit(solution)/shard_map/all_to_all | solution.py:147
  59.0 2.1 %collective-permute-start.1 = (bf16[128,1792]{1,0:T(8,128)(2,1)S(1)}, bf16[128,1792]{1,0:T(8,128)(2,1)S(1)}, u32[]{:S(2)}, u32[]{:S(2)}) collective-permute-start(bf16[128,1792]{1,0:T(8,128)(2,1)S(1)} %all_to_all.35.own), channel_id=1, source_target_pairs={{0,128},{1,385},{128,0},{129,257},{256,384},{257,129},{384,256},{3... | collective-permute-start | bytes 1376264 | tf_op jit(solution)/shard_map/ppermute | solution.py:26
  61.1 8.3 %collective-permute-done.4.y2 = bf16[256,1280]{1,0:T(8,128)(2,1)S(1)} collective-permute-done((bf16[256,1280]{1,0:T(8,128)(2,1)S(1)}, bf16[256,1280]{1,0:T(8,128)(2,1)S(1)}, u32[]{:S(2)}, u32[]{:S(2)}) %collective-permute-start.4) | collective-permute-done | bytes 655392 | tf_op jit(solution)/shard_map/ppermute | solution.py:26
  69.4 3.4 %collective-permute-start.5 = (bf16[384,1280]{1,0:T(8,128)(2,1)S(1)}, bf16[384,1280]{1,0:T(8,128)(2,1)S(1)}, u32[]{:S(2)}, u32[]{:S(2)}) collective-permute-start(bf16[384,1280]{1,0:T(8,128)(2,1)S(1)} %pad_maximum_fusion.2), channel_id=1, source_target_pairs={{0,128},{1,385},{128,0},{129,257},{256,384},{257,129},{384,256},{3... | collective-permute-start | bytes 2949128 | tf_op jit(solution)/shard_map/ppermute | solution.py:26
  72.9 4.0 %collective-permute-start.2 = (bf16[256,1792]{1,0:T(8,128)(2,1)S(1)}, bf16[256,1792]{1,0:T(8,128)(2,1)S(1)}, u32[]{:S(2)}, u32[]{:S(2)}) collective-permute-start(bf16[256,1792]{1,0:T(8,128)(2,1)S(1)} %pad_maximum_fusion.3), channel_id=1, source_target_pairs={{0,384},{1,129},{128,256},{129,1},{256,128},{257,385},{384,0},{385... | collective-permute-start | bytes 2752520 | tf_op jit(solution)/shard_map/ppermute | solution.py:26
  76.9 19.0 %collective-permute-done.5.x3 = bf16[384,1280]{1,0:T(8,128)(2,1)S(1)} collective-permute-done((bf16[384,1280]{1,0:T(8,128)(2,1)S(1)}, bf16[384,1280]{1,0:T(8,128)(2,1)S(1)}, u32[]{:S(2)}, u32[]{:S(2)}) %collective-permute-start.5) | collective-permute-done | bytes 983072 | tf_op jit(solution)/shard_map/ppermute | solution.py:26
  95.9 1.4 pad_maximum_fusion
  97.3 2.8 %collective-permute-start.6 = (bf16[768,1280]{1,0:T(8,128)(2,1)}, bf16[768,1280]{1,0:T(8,128)(2,1)}, u32[]{:S(2)}, u32[]{:S(2)}) collective-permute-start(bf16[768,1280]{1,0:T(8,128)(2,1)} %pad_maximum_fusion), channel_id=1, source_target_pairs={{0,384},{1,129},{128,256},{129,1},{256,128},{257,385},{384,0},{385... | collective-permute-start | bytes 5898248 | tf_op jit(solution)/shard_map/ppermute | solution.py:26
  100.3 1.9 %collective-permute-start.7 = (bf16[512,512]{1,0:T(8,128)(2,1)S(1)}, bf16[512,512]{1,0:T(8,128)(2,1)S(1)}, u32[]{:S(2)}, u32[]{:S(2)}) collective-permute-start(bf16[512,512]{1,0:T(8,128)(2,1)S(1)} %pad_maximum_fusion.5), channel_id=1, source_target_pairs={{0,32},{1,97},{32,0},{33,65},{64,96},{65,33},{96,64},{97,1},{2,34}... | collective-permute-start | bytes 1572872 | tf_op jit(solution)/shard_map/ppermute | solution.py:26
  102.2 15.7 %collective-permute-done.7.y3 = bf16[512,512]{1,0:T(8,128)(2,1)S(1)} collective-permute-done((bf16[512,512]{1,0:T(8,128)(2,1)S(1)}, bf16[512,512]{1,0:T(8,128)(2,1)S(1)}, u32[]{:S(2)}, u32[]{:S(2)}) %collective-permute-start.7) | collective-permute-done | bytes 524320 | tf_op jit(solution)/shard_map/ppermute | solution.py:26
  117.9 1.0 pad_maximum_fusion.1
  118.9 23.4 %collective-permute-start.8 = (bf16[1024,512]{1,0:T(8,128)(2,1)}, bf16[1024,512]{1,0:T(8,128)(2,1)}, u32[]{:S(2)}, u32[]{:S(2)}) collective-permute-start(bf16[1024,512]{1,0:T(8,128)(2,1)} %pad_maximum_fusion.1), channel_id=1, source_target_pairs={{0,96},{1,33},{32,64},{33,1},{64,32},{65,97},{96,0},{97,65},{2,98}... | collective-permute-start | bytes 3145736 | tf_op jit(solution)/shard_map/ppermute | solution.py:26
  142.6 1.6 copy-done
  144.2 6.5 %shard_map.17.slab_ref = bf16[512,2048]{1,0:T(8,128)(2,1)S(1)} custom-call(s32[16]{0:T(128)S(1)} %add.20.order_ref, bf16[2048,512]{1,0:T(8,128)(2,1)S(1)} %copy-done), custom_call_target="tpu_custom_call" | custom-call | flops 8388608 | bytes 4194304 | tf_op jit(solution)/shard_map/pallas_call | solution.py:59
  150.7 15.8 %collective-permute-done.8.y4 = bf16[1024,512]{1,0:T(8,128)(2,1)} collective-permute-done((bf16[1024,512]{1,0:T(8,128)(2,1)}, bf16[1024,512]{1,0:T(8,128)(2,1)}, u32[]{:S(2)}, u32[]{:S(2)}) %collective-permute-start.8) | collective-permute-done | bytes 1048608 | tf_op jit(solution)/shard_map/ppermute | solution.py:26
  166.6 11.9 %shard_map.18 = bf16[512,1792]{1,0:T(8,128)(2,1)} custom-call(bf16[512,2048]{1,0:T(8,128)(2,1)S(1)} %shard_map.17.slab_ref, bf16[128,1792]{1,0:T(8,128)(2,1)S(1)} %all_to_all.35.own, bf16[128,1792]{1,0:T(8,128)(2,1)S(1)} %collective-permute-done.1.x1, bf16[256,1792]{1,0:T(8,128)(2,1)S(1)} %copy-done.2, bf16[128,1280]{1,0:T(8,128)(2,1)S(1)} %collective-permute-done.3.y1, ...), custom_call_target="tpu_custom_call" | custom-call | flops 3758096384 | bytes 9437184 | tf_op jit(solution)/shard_map/pallas_call | solution.py:121
  (29 shorter events, 2.1 us)
Async XLA Ops:
  7.4 14.2 %collective-permute-start = (bf16[4,8192]{1,0:T(4,128)(2,1)S(1)}, bf16[4,8192]{1,0:T(4,128)(2,1)S(1)}, u32[]{:S(2)}, u32[]{:S(2)}) collective-permute-start(bf16[4,8192]{1,0:T(4,128)(2,1)S(1)} %slice.15), channel_id=1, source_target_pairs={{0,16},{16,0},{1,17},{17,1},{2,18},{18,2},{3,19},{19,3},{4,20},{20... | collective-permute-start | bytes 196616 | tf_op jit(solution)/shard_map/ppermute | solution.py:137
  10.9 25.4 %all-to-all-start.1 = ((bf16[4,32,1792]{2,0,1:T(4,128)(2,1)}), bf16[4,32,1792]{2,0,1:T(4,128)(2,1)S(1)}, u32[]{:S(2)}, u32[]{:S(2)}) async-start(bf16[4,32,1792]{2,0,1:T(4,128)(2,1)} %bitcast.9), calls=%async_computation.1 | async-start | bytes 917504 | tf_op jit(solution)/shard_map/all_to_all | solution.py:143
  36.4 13.3 %collective-permute-start.3 = (bf16[128,1280]{1,0:T(8,128)(2,1)S(1)}, bf16[128,1280]{1,0:T(8,128)(2,1)S(1)}, u32[]{:S(2)}, u32[]{:S(2)}) collective-permute-start(bf16[128,1280]{1,0:T(8,128)(2,1)S(1)} %slice.20), channel_id=1, source_target_pairs={{0,32},{1,97},{32,0},{33,65},{64,96},{65,33},{96,64},{97,1},{2,34}... | collective-permute-start | bytes 983048 | tf_op jit(solution)/shard_map/ppermute | solution.py:26
  39.4 18.8 %all-to-all-start = ((bf16[8,16,512]{2,0,1:T(8,128)(2,1)}), bf16[8,16,512]{2,0,1:T(8,128)(2,1)S(1)}, u32[]{:S(2)}, u32[]{:S(2)}) async-start(bf16[8,16,512]{2,0,1:T(8,128)(2,1)} %bitcast.2), calls=%async_computation | async-start | bytes 262144 | tf_op jit(solution)/shard_map/all_to_all | solution.py:147
  49.7 92.9 %all-gather.2.cloned.1.call-start = ((), (), s32[]{:S(2)}) async-start(), calls=%async_computation.2 | async-start | bytes 2228224 | tf_op jit(solution)/shard_map/all_gather | solution.py:148
  49.8 19.5 %collective-permute-start.4 = (bf16[256,1280]{1,0:T(8,128)(2,1)S(1)}, bf16[256,1280]{1,0:T(8,128)(2,1)S(1)}, u32[]{:S(2)}, u32[]{:S(2)}) collective-permute-start(bf16[256,1280]{1,0:T(8,128)(2,1)S(1)} %pad_maximum_fusion.4), channel_id=1, source_target_pairs={{0,96},{1,33},{32,64},{33,1},{64,32},{65,97},{96,0},{97,65},{2,98}... | collective-permute-start | bytes 1966088 | tf_op jit(solution)/shard_map/ppermute | solution.py:26
  58.3 0.7 copy-start.3
  59.0 13.9 %collective-permute-start.1 = (bf16[128,1792]{1,0:T(8,128)(2,1)S(1)}, bf16[128,1792]{1,0:T(8,128)(2,1)S(1)}, u32[]{:S(2)}, u32[]{:S(2)}) collective-permute-start(bf16[128,1792]{1,0:T(8,128)(2,1)S(1)} %all_to_all.35.own), channel_id=1, source_target_pairs={{0,128},{1,385},{128,0},{129,257},{256,384},{257,129},{384,256},{3... | collective-permute-start | bytes 1376264 | tf_op jit(solution)/shard_map/ppermute | solution.py:26
  69.4 26.5 %collective-permute-start.5 = (bf16[384,1280]{1,0:T(8,128)(2,1)S(1)}, bf16[384,1280]{1,0:T(8,128)(2,1)S(1)}, u32[]{:S(2)}, u32[]{:S(2)}) collective-permute-start(bf16[384,1280]{1,0:T(8,128)(2,1)S(1)} %pad_maximum_fusion.2), channel_id=1, source_target_pairs={{0,128},{1,385},{128,0},{129,257},{256,384},{257,129},{384,256},{3... | collective-permute-start | bytes 2949128 | tf_op jit(solution)/shard_map/ppermute | solution.py:26
  72.9 27.3 %collective-permute-start.2 = (bf16[256,1792]{1,0:T(8,128)(2,1)S(1)}, bf16[256,1792]{1,0:T(8,128)(2,1)S(1)}, u32[]{:S(2)}, u32[]{:S(2)}) collective-permute-start(bf16[256,1792]{1,0:T(8,128)(2,1)S(1)} %pad_maximum_fusion.3), channel_id=1, source_target_pairs={{0,384},{1,129},{128,256},{129,1},{256,128},{257,385},{384,0},{385... | collective-permute-start | bytes 2752520 | tf_op jit(solution)/shard_map/ppermute | solution.py:26
  97.3 69.2 %collective-permute-start.6 = (bf16[768,1280]{1,0:T(8,128)(2,1)}, bf16[768,1280]{1,0:T(8,128)(2,1)}, u32[]{:S(2)}, u32[]{:S(2)}) collective-permute-start(bf16[768,1280]{1,0:T(8,128)(2,1)} %pad_maximum_fusion), channel_id=1, source_target_pairs={{0,384},{1,129},{128,256},{129,1},{256,128},{257,385},{384,0},{385... | collective-permute-start | bytes 5898248 | tf_op jit(solution)/shard_map/ppermute | solution.py:26
  100.2 17.7 %copy-start.1 = (bf16[256,1792]{1,0:T(8,128)(2,1)}, bf16[256,1792]{1,0:T(8,128)(2,1)S(1)}, u32[]{:S(2)}) copy-start(bf16[256,1792]{1,0:T(8,128)(2,1)S(1)} %collective-permute-done.2.x2) | copy-start | bytes 2752516
  100.3 17.6 %collective-permute-start.7 = (bf16[512,512]{1,0:T(8,128)(2,1)S(1)}, bf16[512,512]{1,0:T(8,128)(2,1)S(1)}, u32[]{:S(2)}, u32[]{:S(2)}) collective-permute-start(bf16[512,512]{1,0:T(8,128)(2,1)S(1)} %pad_maximum_fusion.5), channel_id=1, source_target_pairs={{0,32},{1,97},{32,0},{33,65},{64,96},{65,33},{96,64},{97,1},{2,34}... | collective-permute-start | bytes 1572872 | tf_op jit(solution)/shard_map/ppermute | solution.py:26
  118.9 47.6 %collective-permute-start.8 = (bf16[1024,512]{1,0:T(8,128)(2,1)}, bf16[1024,512]{1,0:T(8,128)(2,1)}, u32[]{:S(2)}, u32[]{:S(2)}) collective-permute-start(bf16[1024,512]{1,0:T(8,128)(2,1)} %pad_maximum_fusion.1), channel_id=1, source_target_pairs={{0,96},{1,33},{32,64},{33,1},{64,32},{65,97},{96,0},{97,65},{2,98}... | collective-permute-start | bytes 3145736 | tf_op jit(solution)/shard_map/ppermute | solution.py:26
  142.6 1.6 copy-start
  144.2 22.4 %copy-start.2 = (bf16[256,1792]{1,0:T(8,128)(2,1)S(1)}, bf16[256,1792]{1,0:T(8,128)(2,1)}, u32[]{:S(2)}) copy-start(bf16[256,1792]{1,0:T(8,128)(2,1)} %copy-done.1) | copy-start | bytes 2752516
Sparse Core Ops, SparseCore 0:
  59.1 40.7 all-gather.1

commit v2 on v0

v2 whole, which is shorter than its diff:
```python
import jax
import jax.numpy as jnp
import numpy as np
from jax import lax
from jax.experimental import pallas as pl
from jax.experimental.pallas import tpu as pltpu
from jax.sharding import Mesh, PartitionSpec as P

ROWS_DEV = 512
EPS = 1e-06
TOKENS = 2048
HALF = ROWS_DEV // 2
FIRST = 1280
PIECE = 128
TILE = 256
ALL = ("x", "yh", "yl", "z", "c")

SLOTS = [(0, 0), (1, 0), (2, 0), (3, 0), (0, 1), (1, 1), (0, 2), (1, 2), (0, 3), (1, 3)]
SLOTS += [(2, 1), (3, 1), (2, 2), (3, 2), (2, 3), (3, 3)]


def exchange(values, axis, step):
    perm = []
    for i in range(4):
        for core in range(2):
            flip = 1 if core == step else 3
            perm.append((i * 2 + core, (i ^ flip) * 2 + core))
    return lax.ppermute(values, (axis, "c"), perm)


def swap_places(values, flip):
    perm = [(a * 16 + b, b * 16 + (a ^ flip)) for a in range(16) for b in range(16)]
    return lax.ppermute(values, ("x", "yh", "yl", "z"), perm)


EVEN = [1, 0, 3, 2, 5, 4, 7, 6]
ODD = [7, 2, 1, 4, 3, 6, 5, 0]
Z_STEPS = [([3, 6, 5, 0, 7, 2, 1, 4], [5, 4, 7, 6, 1, 0, 3, 2]), (ODD, EVEN), (EVEN, ODD)]


def z_exchange(values, step):
    perm = [(z * 2 + core, Z_STEPS[step][core][z] * 2 + core) for z in range(8) for core in range(2)]
    return jnp.concatenate([values, lax.ppermute(values, ("z", "c"), perm)], axis=0)


def z_places():
    held = {(z, core): [z] for z in range(8) for core in range(2)}
    for step in range(3):
        held = {(z, core): held[z, core] + held[Z_STEPS[step][core][z], core] for z, core in held}
    return np.array([[np.argsort(held[z, core]) for core in range(2)] for z in range(8)], np.int32)


def fold(values):
    return jnp.sum(values.reshape(values.shape[0] // 8, 8, values.shape[1]), axis=0)


def slab_kernel(place_ref, mine_ref, other_ref, out_ref, sums_ref):
    n = TOKENS // PIECE
    for i, ref in enumerate((mine_ref, other_ref)):

        def rows(j, ref=ref):
            return ref[pl.ds(pl.multiple_of(j * PIECE, PIECE), PIECE), :].astype(jnp.float32)

        def add(j, total):
            return total + fold(rows(j))

        zero = jnp.zeros((8, HALF), jnp.float32)
        mean = jnp.sum(lax.fori_loop(0, n, add, zero), axis=0, keepdims=True) / TOKENS

        def square(j, total):
            centered = rows(j) - mean
            return total + fold(centered * centered)

        variance = jnp.sum(lax.fori_loop(0, n, square, zero), axis=0, keepdims=True) / TOKENS
        scale = 1.0 / jnp.sqrt(variance + EPS)
        units = pl.ds(pl.multiple_of(place_ref[2, i] * HALF, HALF), HALF)
        sums = jnp.zeros((HALF, 1), jnp.float32)
        for slot in range(n):
            standard = ((rows(place_ref[i, slot]) - mean) * scale).T.astype(jnp.bfloat16)
            out_ref[units, slot * PIECE : (slot + 1) * PIECE] = standard
            sums += jnp.sum(standard.astype(jnp.float32), axis=1, keepdims=True)
        sums_ref[units, :] = jnp.broadcast_to(sums, (HALF, 128))


def call(kernel, outs, in_specs, scratch, flops, moved, args):
    return pl.pallas_call(
        kernel,
        out_shape=outs,
        in_specs=in_specs,
        out_specs=[pl.BlockSpec(memory_space=pltpu.VMEM)] * len(outs),
        scratch_shapes=scratch,
        compiler_params=pltpu.CompilerParams(vmem_limit_bytes=32 * 2**20),
        cost_estimate=pl.CostEstimate(flops=flops, bytes_accessed=moved, transcendentals=0),
    )(*args)


VMEM = pl.BlockSpec(memory_space=pltpu.VMEM)


def slab_standard(mine, other, place):
    return call(
        slab_kernel,
        [jax.ShapeDtypeStruct((ROWS_DEV, TOKENS), jnp.bfloat16), jax.ShapeDtypeStruct((ROWS_DEV, 128), jnp.float32)],
        [pl.BlockSpec(memory_space=pltpu.SMEM), VMEM, VMEM],
        [],
        8 * TOKENS * ROWS_DEV,
        4 * TOKENS * ROWS_DEV,
        (place, mine, other),
    )


def tile_at(ref, part, j, shift):
    lanes = pl.ds(pl.multiple_of(j * TILE + shift, TILE), TILE)
    return ref[part * PIECE : (part + 1) * PIECE, lanes].astype(jnp.float32)


def early_kernel(slab_ref, own, x1, x2, y1, y2, x3, y3, acc_ref, pivot_ref, square_ref, shifted):
    width = own.shape[1]

    def tiles(pieces, n_tiles, offset, spans):
        @pl.loop(0, n_tiles)
        def _(j):
            lanes = pl.ds(pl.multiple_of(j * TILE + offset, TILE), TILE)
            total = jnp.zeros((8, TILE), jnp.float32)
            for ref, part, shift in pieces:
                total += fold(tile_at(ref, part, j, shift))
            pivot = jnp.sum(total, axis=0, keepdims=True) / (len(pieces) * PIECE)
            square = jnp.zeros((8, TILE), jnp.float32)
            for i, (ref, part, shift) in enumerate(pieces):
                values = tile_at(ref, part, j, shift) - pivot
                square += fold(values * values)
                shifted[i * PIECE : (i + 1) * PIECE, :] = values.astype(jnp.bfloat16)
            pivot_ref[:, lanes] = jnp.broadcast_to(pivot, (8, TILE))
            square_ref[:, lanes] = square
            acc = None
            row = 0
            for first, size in spans:
                part = jnp.dot(
                    slab_ref[:, first : first + size], shifted[row : row + size, :], preferred_element_type=jnp.float32
                )
                acc = part if acc is None else acc + part
                row += size
            acc_ref[:, lanes] = acc

    tiles(
        [(own, 0, 0), (x1, 0, 0), (x2, 0, 0), (x2, 1, 0), (y1, 0, 0)]
        + [(x3, 0, 0), (y2, 0, 0), (x3, 1, 0), (y2, 1, 0), (x3, 2, 0)],
        FIRST // TILE,
        0,
        [(0, 1280)],
    )
    tiles(
        [(own, 0, FIRST), (x1, 0, FIRST), (x2, 0, FIRST), (x2, 1, FIRST)] + [(y3, i, 0) for i in range(4)],
        (width - FIRST) // TILE,
        FIRST,
        [(0, 768), (1280, 256)],
    )


def late_kernel(slab_ref, sums_ref, acc_ref, pivot_ref, square_ref, x4, y4, out_ref, shifted):
    width = acc_ref.shape[1]

    def tiles(pieces, n_tiles, offset, spans):
        @pl.loop(0, n_tiles)
        def _(j):
            lanes = pl.ds(pl.multiple_of(j * TILE + offset, TILE), TILE)
            pivot = pivot_ref[0:1, lanes]
            total = jnp.zeros((8, TILE), jnp.float32)
            square = square_ref[:, lanes]
            for i, (ref, part) in enumerate(pieces):
                values = tile_at(ref, part, j, 0) - pivot
                total += fold(values)
                square += fold(values * values)
                shifted[i * PIECE : (i + 1) * PIECE, :] = values.astype(jnp.bfloat16)
            delta = jnp.sum(total, axis=0, keepdims=True) / TOKENS
            variance = jnp.sum(square, axis=0, keepdims=True) / TOKENS - delta * delta
            scale = 1.0 / (jnp.sqrt(jnp.maximum(variance, 0.0) + EPS) * TOKENS)
            acc = acc_ref[:, lanes]
            row = 0
            for first, size in spans:
                acc += jnp.dot(
                    slab_ref[:, first : first + size], shifted[row : row + size, :], preferred_element_type=jnp.float32
                )
                row += size
            out_ref[:, lanes] = ((acc - sums_ref[:, 0:1] * delta) * scale).astype(jnp.bfloat16)

    tiles([(x4, 0), (x4, 3), (x4, 1), (x4, 4), (x4, 2), (x4, 5)], FIRST // TILE, 0, [(1280, 768)])
    tiles(
        [(y4, 0), (y4, 1), (y4, 4), (y4, 5), (y4, 2), (y4, 3), (y4, 6), (y4, 7)],
        (width - FIRST) // TILE,
        FIRST,
        [(768, 512), (1536, 512)],
    )


def per_device(activations):
    together = lax.optimization_barrier
    tok, units = activations.shape
    n_col = 32
    width = units // n_col
    with_slab = jnp.concatenate(
        [activations.reshape(tok, n_col, width), activations[:, : n_col * HALF].reshape(tok, n_col, HALF)], axis=2
    )
    block = lax.all_to_all(
        with_slab.reshape(tok, n_col * (width + HALF)), ("yl", "z", "c"), split_axis=1, concat_axis=0, tiled=True
    )
    own, own_first, slab0 = block[:, :width], block[:, :FIRST], block[:, width:]
    y1 = exchange(own_first, "yh", 0)
    x1 = exchange(own, "x", 0)
    slab1 = jnp.concatenate([swap_places(slab0, 0), swap_places(slab0, 8)], axis=0)
    x1, y1, slab1 = together((x1, y1, slab1))
    y2 = exchange(jnp.concatenate([own_first, y1], axis=0), "yh", 1)
    x2 = exchange(jnp.concatenate([own, x1], axis=0), "x", 1)
    slab2 = z_exchange(z_exchange(slab1, 0), 1)
    x2, y2, slab2 = together((x2, y2, slab2))
    rest = jnp.concatenate([own[:, FIRST:], x1[:, FIRST:], x2[:, FIRST:]], axis=0)
    three = jnp.concatenate([y1, y2], axis=0)
    y3 = exchange(rest, "yh", 0)
    x3 = exchange(three, "x", 0)
    mine = z_exchange(slab2, 2)
    x3, y3, mine = together((x3, y3, mine))
    other = lax.ppermute(mine, "c", [(0, 1), (1, 0)])
    rest = jnp.concatenate([rest, y3], axis=0)
    y4 = exchange(rest, "yh", 1)
    three, x3, rest = together((three, x3, rest))
    x4 = exchange(jnp.concatenate([three, x3], axis=0), "x", 1)

    near = jnp.where(lax.axis_index("c") == 0, 1, 3)
    flips = [0, near, 4 - near, 2]
    token_of = jnp.stack(
        [(lax.axis_index("x") ^ flips[i]) * 4 + (lax.axis_index("yh") ^ flips[j]) for i, j in SLOTS]
    )
    z, core = lax.axis_index("z"), lax.axis_index("c")
    swapped = (token_of // 8) ^ lax.axis_index("yl")
    tables = jnp.asarray(z_places())[z]
    place = jnp.stack(
        [tables[core][token_of % 8] * 2 + swapped, tables[1 - core][token_of % 8] * 2 + swapped]
        + [jnp.where(jnp.arange(16) == 0, core, 1 - core)]
    )
    slab, sums = slab_standard(mine, other, place.astype(jnp.int32))

    wide = jax.ShapeDtypeStruct((8, width), jnp.float32)
    acc, pivot, square = call(
        early_kernel,
        [jax.ShapeDtypeStruct((ROWS_DEV, width), jnp.float32), wide, wide],
        [VMEM] * 8,
        [pltpu.VMEM((1280, TILE), jnp.bfloat16)],
        TOKENS * ROWS_DEV * width,
        4 * ROWS_DEV * width,
        (slab, own, x1, x2, y1, y2, x3, y3),
    )
    (out,) = call(
        late_kernel,
        [jax.ShapeDtypeStruct((ROWS_DEV, width), jnp.bfloat16)],
        [VMEM] * 7,
        [pltpu.VMEM((1024, TILE), jnp.bfloat16)],
        TOKENS * ROWS_DEV * width,
        4 * ROWS_DEV * width,
        (slab, sums, acc, pivot, square, x4, y4),
    )
    return out


def solution(mesh):
    fine = Mesh(mesh.devices.reshape(4, 4, 2, 8, 2), ALL)
    out_specs = P(("x", "yh"), ("yl", "z", "c"))
    return jax.shard_map(per_device, mesh=fine, in_specs=(P(ALL, None),), out_specs=out_specs, check_vma=False)
```

time: 229 us -> 154 us (0.67)
  waiting for transfers between devices: 135 us -> 38.3 us
  starting transfers between devices: 0.04 us -> 59.1 us
  blocking collectives: 44.4 us -> 27.4 us
  Pallas kernels: 0 us -> 15 us
  between operations: 13.4 us -> 0.49 us
  local copies, waits for them, and re-layouts: 18.7 us -> 7.15 us
  other arithmetic: 10.1 us -> 4.16 us
  matrix products: 5.44 us -> 0 us
    all_gather x2 -> x0, waiting for transfers between devices: 135 us -> none  [the longest x1 91.6 us: per_device(): column_all = lax.all_gather(column_local, 'row', axis=0, tiled=True)]
    ppermute x0 -> x14, starting transfers between devices: none -> 59.1 us  [the longest x8 36.3 us: exchange(): return lax.ppermute(values, (axis, 'c'), perm)]
    ppermute x0 -> x14, waiting for transfers between devices: none -> 38.3 us  [the longest x3 17.7 us: z_exchange(): lax.ppermute(values, ('z', 'c'), perm)]
    all_to_all x2 -> x1, blocking collectives: 44.4 us -> 27.4 us  [per_device(): lax.all_to_all(with_slab.reshape(tok, n_col * (width + HALF)), ('yl', 'z'...]
    convert_element_type x3 -> x0, local copies, waits for them, and re-layouts: 15.4 us -> none  [standard_local(): widened = values.astype(jnp.float32)]
    pallas_call x0 -> x3, Pallas kernels: none -> 15 us  [call(): pl.pallas_call(kernel, out_shape=outs, in_specs=in_specs, out_specs=[pl.B...]
    reduce_sum x4 -> x0, other arithmetic: 10.1 us -> none  [the longest x2 5.42 us: standard_local(): spread = jnp.sqrt(jnp.mean(centered * centered, axis=0) + EPS)]
    dot_general x1 -> x0, matrix products: 5.44 us -> none  [per_device(): lax.dot_general(slab_standard, column_standard, dims, preferred_element_t...]
  transfers between devices with their start and end apart: 2 -> 14, of which waited for: 2 -> 7; matrix products, arithmetic and copies ran while one was open for 8% -> 2% of each run, Pallas kernels for 0% -> 6%
where the time goes in v2:
time: 154 us; the launch traced here: 152 us
  starting transfers between devices  59.1 us (38%)
  waiting for transfers between devices  38.3 us (25%)
  blocking collectives  27.4 us (18%)
  Pallas kernels  15 us (10%)
  local copies, waits for them, and re-layouts  7.15 us (5%)
  other arithmetic  4.16 us (3%)
    ppermute x8, starting transfers between devices, exchange(): return lax.ppermute(values, (axis, 'c'), perm)  36.3 us
    all_to_all x1, blocking collectives, per_device(): lax.all_to_all(with_slab.reshape(tok, n_col * (width + HALF)), ('yl', 'z'...  27.4 us
    ppermute x3, waiting for transfers between devices, z_exchange(): lax.ppermute(values, ('z', 'c'), perm)  17.7 us
    pallas_call x3, Pallas kernels, call(): pl.pallas_call(kernel, out_shape=outs, in_specs=in_specs, out_specs=[pl.B...  15 us
    ppermute x8, waiting for transfers between devices, exchange(): return lax.ppermute(values, (axis, 'c'), perm)  14.9 us
    ppermute x2, starting transfers between devices, swap_places(): return lax.ppermute(values, ('x', 'yh', 'yl', 'z'), perm)  13.2 us
    ppermute x3, starting transfers between devices, z_exchange(): lax.ppermute(values, ('z', 'c'), perm)  7.7 us
    ppermute x2, waiting for transfers between devices, swap_places(): return lax.ppermute(values, ('x', 'yh', 'yl', 'z'), perm)  5.62 us
  transfers between devices with their start and end apart: 14, of which 7 were waited for; matrix products, arithmetic and copies ran while one was open for 2% of the time, Pallas kernels for 6%

profile of v2, /device:TPU:6, one launch (start us, length us, event | category | flops | bytes accessed | tf_op | source)
XLA Modules:
  0.0 151.5 jit_solution(3087880375389790125)
XLA Ops:
  2.2 27.4 %all_to_all.16 = bf16[4,32,2048]{2,0,1:T(4,128)(2,1)S(1)} all-to-all(bf16[4,32,2048]{2,0,1:T(4,128)(2,1)S(1)} %pad_maximum_fusion.5), channel_id=1, replica_groups=mesh['x'=4,'yh'=4,'yl'=2,'z'=8,'c'=2] {'yl','z','c'}, dimensions={1} | all-to-all | bytes 1048576 | tf_op jit(solution)/shard_map/all_to_all | solution.py:204
  29.8 2.7 %collective-permute-start = (bf16[128,1792]{1,0:T(8,128)(2,1)S(1)}, bf16[128,1792]{1,0:T(8,128)(2,1)S(1)}, u32[]{:S(2)}, u32[]{:S(2)}) collective-permute-start(bf16[128,1792]{1,0:T(8,128)(2,1)S(1)} %slice.33.own), channel_id=1, source_target_pairs={{0,128},{1,385},{128,0},{129,257},{256,384},{257,129},{384,256},{3... | collective-permute-start | bytes 1376264 | tf_op jit(solution)/shard_map/ppermute | solution.py:28
  32.5 4.5 %collective-permute-start.1 = (bf16[128,1280]{1,0:T(8,128)(2,1)S(1)}, bf16[128,1280]{1,0:T(8,128)(2,1)S(1)}, u32[]{:S(2)}, u32[]{:S(2)}) collective-permute-start(bf16[128,1280]{1,0:T(8,128)(2,1)S(1)} %slice.34), channel_id=1, source_target_pairs={{0,32},{1,97},{32,0},{33,65},{64,96},{65,33},{96,64},{97,1},{2,34}... | collective-permute-start | bytes 983048 | tf_op jit(solution)/shard_map/ppermute | solution.py:28
  37.1 4.9 %collective-permute-start.3 = (bf16[128,256]{1,0:T(8,128)(2,1)S(1)}, bf16[128,256]{1,0:T(8,128)(2,1)S(1)}, u32[]{:S(2)}, u32[]{:S(2)}) collective-permute-start(bf16[128,256]{1,0:T(8,128)(2,1)S(1)} %slice.35), channel_id=1, source_target_pairs={{0,16},{2,48},{4,80},{6,112},{8,144},{10,176},{12,208},{14,240},{1... | collective-permute-start | bytes 196616 | tf_op jit(solution)/shard_map/ppermute | solution.py:33
  42.0 8.3 %collective-permute-start.2 = (bf16[128,256]{1,0:T(8,128)(2,1)S(1)}, bf16[128,256]{1,0:T(8,128)(2,1)S(1)}, u32[]{:S(2)}, u32[]{:S(2)}) collective-permute-start(bf16[128,256]{1,0:T(8,128)(2,1)S(1)} %slice.35), channel_id=1, source_target_pairs={{0,0},{2,32},{4,64},{6,96},{8,128},{10,160},{12,192},{14,224},{16,... | collective-permute-start | bytes 196616 | tf_op jit(solution)/shard_map/ppermute | solution.py:33
  51.2 4.6 %collective-permute-done.2 = bf16[128,256]{1,0:T(8,128)(2,1)S(1)} collective-permute-done((bf16[128,256]{1,0:T(8,128)(2,1)S(1)}, bf16[128,256]{1,0:T(8,128)(2,1)S(1)}, u32[]{:S(2)}, u32[]{:S(2)}) %collective-permute-start.2) | collective-permute-done | bytes 65568 | tf_op jit(solution)/shard_map/ppermute | solution.py:33
  56.0 1.9 %collective-permute-start.4 = (bf16[256,1792]{1,0:T(8,128)(2,1)S(1)}, bf16[256,1792]{1,0:T(8,128)(2,1)S(1)}, u32[]{:S(2)}, u32[]{:S(2)}) collective-permute-start(bf16[256,1792]{1,0:T(8,128)(2,1)S(1)} %pad_maximum_fusion.3), channel_id=1, source_target_pairs={{0,384},{1,129},{128,256},{129,1},{256,128},{257,385},{384,0},{385... | collective-permute-start | bytes 2752520 | tf_op jit(solution)/shard_map/ppermute | solution.py:28
  58.0 6.7 %collective-permute-start.5 = (bf16[256,1280]{1,0:T(8,128)(2,1)S(1)}, bf16[256,1280]{1,0:T(8,128)(2,1)S(1)}, u32[]{:S(2)}, u32[]{:S(2)}) collective-permute-start(bf16[256,1280]{1,0:T(8,128)(2,1)S(1)} %pad_maximum_fusion.4), channel_id=1, source_target_pairs={{0,96},{1,33},{32,64},{33,1},{64,32},{65,97},{96,0},{97,65},{2,98}... | collective-permute-start | bytes 1966088 | tf_op jit(solution)/shard_map/ppermute | solution.py:28
  64.6 1.9 %collective-permute-start.6 = (bf16[256,256]{1,0:T(8,128)(2,1)S(1)}, bf16[256,256]{1,0:T(8,128)(2,1)S(1)}, u32[]{:S(2)}, u32[]{:S(2)}) collective-permute-start(bf16[256,256]{1,0:T(8,128)(2,1)S(1)} %pad_maximum_fusion.9), channel_id=1, source_target_pairs={{0,6},{1,11},{2,12},{3,9},{4,10},{5,15},{6,0},{7,13},{8,14},{9,3},... | collective-permute-start | bytes 393224 | tf_op jit(solution)/shard_map/ppermute | solution.py:43
  66.6 7.7 %collective-permute-done.6 = bf16[256,256]{1,0:T(8,128)(2,1)S(1)} collective-permute-done((bf16[256,256]{1,0:T(8,128)(2,1)S(1)}, bf16[256,256]{1,0:T(8,128)(2,1)S(1)}, u32[]{:S(2)}, u32[]{:S(2)}) %collective-permute-start.6) | collective-permute-done | bytes 131104 | tf_op jit(solution)/shard_map/ppermute | solution.py:43
  74.3 3.9 %collective-permute-start.7 = (bf16[512,256]{1,0:T(8,128)(2,1)S(1)}, bf16[512,256]{1,0:T(8,128)(2,1)S(1)}, u32[]{:S(2)}, u32[]{:S(2)}) collective-permute-start(bf16[512,256]{1,0:T(8,128)(2,1)S(1)} %pad_maximum_fusion.8), channel_id=1, source_target_pairs={{0,14},{1,3},{2,4},{3,1},{4,2},{5,7},{6,8},{7,5},{8,6},{9,11},{10,... | collective-permute-start | bytes 786440 | tf_op jit(solution)/shard_map/ppermute | solution.py:43
  78.2 5.6 %collective-permute-done.7 = bf16[512,256]{1,0:T(8,128)(2,1)S(1)} collective-permute-done((bf16[512,256]{1,0:T(8,128)(2,1)S(1)}, bf16[512,256]{1,0:T(8,128)(2,1)S(1)}, u32[]{:S(2)}, u32[]{:S(2)}) %collective-permute-start.7) | collective-permute-done | bytes 262176 | tf_op jit(solution)/shard_map/ppermute | solution.py:43
  83.9 5.4 %collective-permute-start.8 = (bf16[384,1280]{1,0:T(8,128)(2,1)S(1)}, bf16[384,1280]{1,0:T(8,128)(2,1)S(1)}, u32[]{:S(2)}, u32[]{:S(2)}) collective-permute-start(bf16[384,1280]{1,0:T(8,128)(2,1)S(1)} %constant_dynamic-update-slice_fusion), channel_id=1, source_target_pairs={{0,128},{1,385},{128,0},{129,257},{256,384},{257,129},{384,256},{3... | collective-permute-start | bytes 2949128 | tf_op jit(solution)/shard_map/ppermute | solution.py:28
  89.3 1.9 %collective-permute-start.10 = (bf16[1024,256]{1,0:T(8,128)(2,1)S(1)}, bf16[1024,256]{1,0:T(8,128)(2,1)S(1)}, u32[]{:S(2)}, u32[]{:S(2)}) collective-permute-start(bf16[1024,256]{1,0:T(8,128)(2,1)S(1)} %pad_maximum_fusion.6), channel_id=1, source_target_pairs={{0,2},{1,15},{2,0},{3,5},{4,6},{5,3},{6,4},{7,9},{8,10},{9,7},{10,... | collective-permute-start | bytes 1572872 | tf_op jit(solution)/shard_map/ppermute | solution.py:43
  91.3 4.5 %collective-permute-start.9 = (bf16[512,512]{1,0:T(8,128)(2,1)S(1)}, bf16[512,512]{1,0:T(8,128)(2,1)S(1)}, u32[]{:S(2)}, u32[]{:S(2)}) collective-permute-start(bf16[512,512]{1,0:T(8,128)(2,1)S(1)} %pad_maximum_fusion.7), channel_id=1, source_target_pairs={{0,32},{1,97},{32,0},{33,65},{64,96},{65,33},{96,64},{97,1},{2,34}... | collective-permute-start | bytes 1572872 | tf_op jit(solution)/shard_map/ppermute | solution.py:28
  95.9 4.5 %collective-permute-done.10 = bf16[1024,256]{1,0:T(8,128)(2,1)S(1)} collective-permute-done((bf16[1024,256]{1,0:T(8,128)(2,1)S(1)}, bf16[1024,256]{1,0:T(8,128)(2,1)S(1)}, u32[]{:S(2)}, u32[]{:S(2)}) %collective-permute-start.10) | collective-permute-done | bytes 524320 | tf_op jit(solution)/shard_map/ppermute | solution.py:43
  100.4 5.2 %collective-permute-done.9.y3 = bf16[512,512]{1,0:T(8,128)(2,1)S(1)} collective-permute-done((bf16[512,512]{1,0:T(8,128)(2,1)S(1)}, bf16[512,512]{1,0:T(8,128)(2,1)S(1)}, u32[]{:S(2)}, u32[]{:S(2)}) %collective-permute-start.9) | collective-permute-done | bytes 524320 | tf_op jit(solution)/shard_map/ppermute | solution.py:28
  108.5 4.5 %collective-permute-start.12 = (bf16[768,1280]{1,0:T(8,128)(2,1)}, bf16[768,1280]{1,0:T(8,128)(2,1)S(1)}, u32[]{:S(2)}, u32[]{:S(2)}) collective-permute-start(bf16[768,1280]{1,0:T(8,128)(2,1)} %pad_maximum_fusion), channel_id=1, source_target_pairs={{0,384},{1,129},{128,256},{129,1},{256,128},{257,385},{384,0},{385... | collective-permute-start | bytes 5898248 | tf_op jit(solution)/shard_map/ppermute | solution.py:28
  113.0 1.9 %collective-permute-start.11 = (bf16[2048,256]{1,0:T(8,128)(2,1)S(1)}, bf16[2048,256]{1,0:T(8,128)(2,1)}, u32[]{:S(2)}, u32[]{:S(2)}) collective-permute-start(bf16[2048,256]{1,0:T(8,128)(2,1)S(1)} %pad_maximum_fusion.1.mine_ref), channel_id=1, source_target_pairs={{0,1},{1,0},{2,3},{3,2},{4,5},{5,4},{6,7},{7,6},{8,9},{9,8},{10,11... | collective-permute-start | bytes 3145736 | tf_op jit(solution)/shard_map/ppermute | solution.py:222
  115.9 6.1 %collective-permute-start.13 = (bf16[1024,512]{1,0:T(8,128)(2,1)}, bf16[1024,512]{1,0:T(8,128)(2,1)}, u32[]{:S(2)}, u32[]{:S(2)}) collective-permute-start(bf16[1024,512]{1,0:T(8,128)(2,1)} %pad_maximum_fusion.2), channel_id=1, source_target_pairs={{0,96},{1,33},{32,64},{33,1},{64,32},{65,97},{96,0},{97,65},{2,98}... | collective-permute-start | bytes 3145736 | tf_op jit(solution)/shard_map/ppermute | solution.py:28
  123.6 4.8 %shard_map.28 = (bf16[512,2048]{1,0:T(8,128)(2,1)S(1)}, f32[512,128]{1,0:T(8,128)S(1)}) custom-call(s32[3,16]{1,0:T(4,128)S(1)} %pad_add_fusion.place_ref, bf16[2048,256]{1,0:T(8,128)(2,1)S(1)} %pad_maximum_fusion.1.mine_ref, bf16[2048,256]{1,0:T(8,128)(2,1)} %collective-permute-done.11.other_ref), custom_call_target="tpu_custom_call" | custom-call | flops 8388608 | bytes 4194304 | tf_op jit(solution)/shard_map/pallas_call | solution.py:86
  131.7 4.5 %shard_map.29 = (f32[512,1792]{1,0:T(8,128)S(1)}, f32[8,1792]{1,0:T(8,128)S(1)}, f32[8,1792]{1,0:T(8,128)S(1)}) custom-call(bf16[512,2048]{1,0:T(8,128)(2,1)S(1)} %get-tuple-element.28.slab_ref, bf16[128,1792]{1,0:T(8,128)(2,1)S(1)} %slice.33.own, bf16[128,1792]{1,0:T(8,128)(2,1)S(1)} %copy-done.5, bf16[256,1792]{1,0:T(8,128)(2,1)S(1)} %copy-done.11, ...), custom_call_target="tpu_custom_call" | custom-call | flops 1879048192 | bytes 3670016 | tf_op jit(solution)/shard_map/pallas_call | solution.py:86
  136.2 9.7 %collective-permute-done.13.y4 = bf16[1024,512]{1,0:T(8,128)(2,1)} collective-permute-done((bf16[1024,512]{1,0:T(8,128)(2,1)}, bf16[1024,512]{1,0:T(8,128)(2,1)}, u32[]{:S(2)}, u32[]{:S(2)}) %collective-permute-start.13) | collective-permute-done | bytes 1048608 | tf_op jit(solution)/shard_map/ppermute | solution.py:28
  145.8 5.7 %shard_map.30 = bf16[512,1792]{1,0:T(8,128)(2,1)} custom-call(bf16[512,2048]{1,0:T(8,128)(2,1)S(1)} %get-tuple-element.28.slab_ref, f32[512,128]{1,0:T(8,128)S(1)} %get-tuple-element.29.sums_ref, f32[512,1792]{1,0:T(8,128)S(1)} %get-tuple-element.33.acc_ref, f32[8,1792]{1,0:T(8,128)S(1)} %get-tuple-element.34.pivot_ref, ...), custom_call_target="tpu_custom_call" | custom-call | flops 1879048192 | bytes 3670016 | tf_op jit(solution)/shard_map/pallas_call | solution.py:86
  (62 shorter events, 12.3 us)
Async XLA Ops:
  29.8 26.1 %collective-permute-start = (bf16[128,1792]{1,0:T(8,128)(2,1)S(1)}, bf16[128,1792]{1,0:T(8,128)(2,1)S(1)}, u32[]{:S(2)}, u32[]{:S(2)}) collective-permute-start(bf16[128,1792]{1,0:T(8,128)(2,1)S(1)} %slice.33.own), channel_id=1, source_target_pairs={{0,128},{1,385},{128,0},{129,257},{256,384},{257,129},{384,256},{3... | collective-permute-start | bytes 1376264 | tf_op jit(solution)/shard_map/ppermute | solution.py:28
  32.5 23.3 %collective-permute-start.1 = (bf16[128,1280]{1,0:T(8,128)(2,1)S(1)}, bf16[128,1280]{1,0:T(8,128)(2,1)S(1)}, u32[]{:S(2)}, u32[]{:S(2)}) collective-permute-start(bf16[128,1280]{1,0:T(8,128)(2,1)S(1)} %slice.34), channel_id=1, source_target_pairs={{0,32},{1,97},{32,0},{33,65},{64,96},{65,33},{96,64},{97,1},{2,34}... | collective-permute-start | bytes 983048 | tf_op jit(solution)/shard_map/ppermute | solution.py:28
  37.1 14.2 %collective-permute-start.3 = (bf16[128,256]{1,0:T(8,128)(2,1)S(1)}, bf16[128,256]{1,0:T(8,128)(2,1)S(1)}, u32[]{:S(2)}, u32[]{:S(2)}) collective-permute-start(bf16[128,256]{1,0:T(8,128)(2,1)S(1)} %slice.35), channel_id=1, source_target_pairs={{0,16},{2,48},{4,80},{6,112},{8,144},{10,176},{12,208},{14,240},{1... | collective-permute-start | bytes 196616 | tf_op jit(solution)/shard_map/ppermute | solution.py:33
  42.0 13.9 %collective-permute-start.2 = (bf16[128,256]{1,0:T(8,128)(2,1)S(1)}, bf16[128,256]{1,0:T(8,128)(2,1)S(1)}, u32[]{:S(2)}, u32[]{:S(2)}) collective-permute-start(bf16[128,256]{1,0:T(8,128)(2,1)S(1)} %slice.35), channel_id=1, source_target_pairs={{0,0},{2,32},{4,64},{6,96},{8,128},{10,160},{12,192},{14,224},{16,... | collective-permute-start | bytes 196616 | tf_op jit(solution)/shard_map/ppermute | solution.py:33
  55.9 22.3 %copy-start = (bf16[128,1280]{1,0:T(8,128)(2,1)}, bf16[128,1280]{1,0:T(8,128)(2,1)S(1)}, u32[]{:S(2)}) copy-start(bf16[128,1280]{1,0:T(8,128)(2,1)S(1)} %collective-permute-done.1.y1) | copy-start | bytes 983044
  55.9 35.3 %copy-start.4 = (bf16[128,1792]{1,0:T(8,128)(2,1)}, bf16[128,1792]{1,0:T(8,128)(2,1)S(1)}, u32[]{:S(2)}) copy-start(bf16[128,1792]{1,0:T(8,128)(2,1)S(1)} %collective-permute-done.x1) | copy-start | bytes 1376260
  56.0 27.9 %collective-permute-start.4 = (bf16[256,1792]{1,0:T(8,128)(2,1)S(1)}, bf16[256,1792]{1,0:T(8,128)(2,1)S(1)}, u32[]{:S(2)}, u32[]{:S(2)}) collective-permute-start(bf16[256,1792]{1,0:T(8,128)(2,1)S(1)} %pad_maximum_fusion.3), channel_id=1, source_target_pairs={{0,384},{1,129},{128,256},{129,1},{256,128},{257,385},{384,0},{385... | collective-permute-start | bytes 2752520 | tf_op jit(solution)/shard_map/ppermute | solution.py:28
  58.0 25.9 %collective-permute-start.5 = (bf16[256,1280]{1,0:T(8,128)(2,1)S(1)}, bf16[256,1280]{1,0:T(8,128)(2,1)S(1)}, u32[]{:S(2)}, u32[]{:S(2)}) collective-permute-start(bf16[256,1280]{1,0:T(8,128)(2,1)S(1)} %pad_maximum_fusion.4), channel_id=1, source_target_pairs={{0,96},{1,33},{32,64},{33,1},{64,32},{65,97},{96,0},{97,65},{2,98}... | collective-permute-start | bytes 1966088 | tf_op jit(solution)/shard_map/ppermute | solution.py:28
  64.6 9.6 %collective-permute-start.6 = (bf16[256,256]{1,0:T(8,128)(2,1)S(1)}, bf16[256,256]{1,0:T(8,128)(2,1)S(1)}, u32[]{:S(2)}, u32[]{:S(2)}) collective-permute-start(bf16[256,256]{1,0:T(8,128)(2,1)S(1)} %pad_maximum_fusion.9), channel_id=1, source_target_pairs={{0,6},{1,11},{2,12},{3,9},{4,10},{5,15},{6,0},{7,13},{8,14},{9,3},... | collective-permute-start | bytes 393224 | tf_op jit(solution)/shard_map/ppermute | solution.py:43
  74.3 9.5 %collective-permute-start.7 = (bf16[512,256]{1,0:T(8,128)(2,1)S(1)}, bf16[512,256]{1,0:T(8,128)(2,1)S(1)}, u32[]{:S(2)}, u32[]{:S(2)}) collective-permute-start(bf16[512,256]{1,0:T(8,128)(2,1)S(1)} %pad_maximum_fusion.8), channel_id=1, source_target_pairs={{0,14},{1,3},{2,4},{3,1},{4,2},{5,7},{6,8},{7,5},{8,6},{9,11},{10,... | collective-permute-start | bytes 786440 | tf_op jit(solution)/shard_map/ppermute | solution.py:43
  83.8 12.1 %copy-start.6 = (bf16[256,1280]{1,0:T(8,128)(2,1)}, bf16[256,1280]{1,0:T(8,128)(2,1)S(1)}, u32[]{:S(2)}) copy-start(bf16[256,1280]{1,0:T(8,128)(2,1)S(1)} %collective-permute-done.5.y2) | copy-start | bytes 1966084
  83.8 12.0 %copy-start.10 = (bf16[256,1792]{1,0:T(8,128)(2,1)}, bf16[256,1792]{1,0:T(8,128)(2,1)S(1)}, u32[]{:S(2)}) copy-start(bf16[256,1792]{1,0:T(8,128)(2,1)S(1)} %collective-permute-done.4.x2) | copy-start | bytes 2752516
  83.9 21.8 %collective-permute-start.8 = (bf16[384,1280]{1,0:T(8,128)(2,1)S(1)}, bf16[384,1280]{1,0:T(8,128)(2,1)S(1)}, u32[]{:S(2)}, u32[]{:S(2)}) collective-permute-start(bf16[384,1280]{1,0:T(8,128)(2,1)S(1)} %constant_dynamic-update-slice_fusion), channel_id=1, source_target_pairs={{0,128},{1,385},{128,0},{129,257},{256,384},{257,129},{384,256},{3... | collective-permute-start | bytes 2949128 | tf_op jit(solution)/shard_map/ppermute | solution.py:28
  89.3 11.1 %collective-permute-start.10 = (bf16[1024,256]{1,0:T(8,128)(2,1)S(1)}, bf16[1024,256]{1,0:T(8,128)(2,1)S(1)}, u32[]{:S(2)}, u32[]{:S(2)}) collective-permute-start(bf16[1024,256]{1,0:T(8,128)(2,1)S(1)} %pad_maximum_fusion.6), channel_id=1, source_target_pairs={{0,2},{1,15},{2,0},{3,5},{4,6},{5,3},{6,4},{7,9},{8,10},{9,7},{10,... | collective-permute-start | bytes 1572872 | tf_op jit(solution)/shard_map/ppermute | solution.py:43
  91.3 14.3 %collective-permute-start.9 = (bf16[512,512]{1,0:T(8,128)(2,1)S(1)}, bf16[512,512]{1,0:T(8,128)(2,1)S(1)}, u32[]{:S(2)}, u32[]{:S(2)}) collective-permute-start(bf16[512,512]{1,0:T(8,128)(2,1)S(1)} %pad_maximum_fusion.7), channel_id=1, source_target_pairs={{0,32},{1,97},{32,0},{33,65},{64,96},{65,33},{96,64},{97,1},{2,34}... | collective-permute-start | bytes 1572872 | tf_op jit(solution)/shard_map/ppermute | solution.py:28
  105.7 1.1 copy-start.8
  105.7 1.4 copy-start.2
  108.5 37.3 %collective-permute-start.12 = (bf16[768,1280]{1,0:T(8,128)(2,1)}, bf16[768,1280]{1,0:T(8,128)(2,1)S(1)}, u32[]{:S(2)}, u32[]{:S(2)}) collective-permute-start(bf16[768,1280]{1,0:T(8,128)(2,1)} %pad_maximum_fusion), channel_id=1, source_target_pairs={{0,384},{1,129},{128,256},{129,1},{256,128},{257,385},{384,0},{385... | collective-permute-start | bytes 5898248 | tf_op jit(solution)/shard_map/ppermute | solution.py:28
  113.0 10.5 %collective-permute-start.11 = (bf16[2048,256]{1,0:T(8,128)(2,1)S(1)}, bf16[2048,256]{1,0:T(8,128)(2,1)}, u32[]{:S(2)}, u32[]{:S(2)}) collective-permute-start(bf16[2048,256]{1,0:T(8,128)(2,1)S(1)} %pad_maximum_fusion.1.mine_ref), channel_id=1, source_target_pairs={{0,1},{1,0},{2,3},{3,2},{4,5},{5,4},{6,7},{7,6},{8,9},{9,8},{10,11... | collective-permute-start | bytes 3145736 | tf_op jit(solution)/shard_map/ppermute | solution.py:222
  115.9 29.9 %collective-permute-start.13 = (bf16[1024,512]{1,0:T(8,128)(2,1)}, bf16[1024,512]{1,0:T(8,128)(2,1)}, u32[]{:S(2)}, u32[]{:S(2)}) collective-permute-start(bf16[1024,512]{1,0:T(8,128)(2,1)} %pad_maximum_fusion.2), channel_id=1, source_target_pairs={{0,96},{1,33},{32,64},{33,1},{64,32},{65,97},{96,0},{97,65},{2,98}... | collective-permute-start | bytes 3145736 | tf_op jit(solution)/shard_map/ppermute | solution.py:28
  123.5 4.9 %copy-start.1 = (bf16[128,1280]{1,0:T(8,128)(2,1)S(1)}, bf16[128,1280]{1,0:T(8,128)(2,1)}, u32[]{:S(2)}) copy-start(bf16[128,1280]{1,0:T(8,128)(2,1)} %copy-done) | copy-start | bytes 983044
  123.5 4.9 %copy-start.3 = (bf16[384,1280]{1,0:T(8,128)(2,1)S(1)}, bf16[384,1280]{1,0:T(8,128)(2,1)}, u32[]{:S(2)}) copy-start(bf16[384,1280]{1,0:T(8,128)(2,1)} %copy-done.2) | copy-start | bytes 2949124
  123.5 4.9 %copy-start.5 = (bf16[128,1792]{1,0:T(8,128)(2,1)S(1)}, bf16[128,1792]{1,0:T(8,128)(2,1)}, u32[]{:S(2)}) copy-start(bf16[128,1792]{1,0:T(8,128)(2,1)} %copy-done.4) | copy-start | bytes 1376260
  130.5 1.2 copy-start.11
  (2 other events, 2.1 us)

commit v3 on v2

v3 whole, which is shorter than its diff:
```python
import jax
import jax.numpy as jnp
import numpy as np
from jax import lax
from jax.experimental import pallas as pl
from jax.experimental.pallas import tpu as pltpu
from jax.sharding import Mesh, PartitionSpec as P

ROWS_DEV = 512
EPS = 1e-06
TOKENS = 2048
FIRST = 1408
PIECE = 128
TILE = 256
ALL = ("x", "yh", "yl", "z", "c")

SLOTS = [(0, 0), (1, 0), (2, 0), (3, 0), (0, 1), (1, 1), (0, 2), (1, 2), (0, 3), (1, 3)]
SLOTS += [(2, 1), (3, 1), (2, 2), (3, 2), (2, 3), (3, 3)]


def exchange(values, axis, step):
    perm = []
    for i in range(4):
        for core in range(2):
            flip = 1 if core == step else 3
            perm.append((i * 2 + core, (i ^ flip) * 2 + core))
    return lax.ppermute(values, (axis, "c"), perm)


def swap_places(values):
    perm = [(a * 32 + y * 16 + b, b * 32 + y * 16 + a) for a in range(16) for y in range(2) for b in range(16)]
    return lax.ppermute(values, ALL, perm)


EVEN = [1, 0, 3, 2, 5, 4, 7, 6]
ODD = [7, 2, 1, 4, 3, 6, 5, 0]
Z_STEPS = [([3, 6, 5, 0, 7, 2, 1, 4], [5, 4, 7, 6, 1, 0, 3, 2]), (ODD, EVEN), (EVEN, ODD)]


def z_permute(values, step):
    perm = [(z * 2 + core, Z_STEPS[step][core][z] * 2 + core) for z in range(8) for core in range(2)]
    return lax.ppermute(values, ("z", "c"), perm)


def z_places():
    held = {(z, core): [z] for z in range(8) for core in range(2)}
    for step in range(3):
        held = {(z, core): held[z, core] + held[Z_STEPS[step][core][z], core] for z, core in held}
    return np.array([[np.argsort(held[z, core]) for core in range(2)] for z in range(8)], np.int32)


def fold(values):
    return jnp.sum(values.reshape(values.shape[0] // 8, 8, values.shape[1]), axis=0)


def slab_kernel(place_ref, mine2_ref, mine3_ref, other2_ref, other3_ref, out_ref, sums_ref, whole):
    n = TOKENS // PIECE
    for first in range(0, ROWS_DEV, TILE):
        lanes = slice(first, first + TILE)
        total = jnp.zeros((8, TILE), jnp.float32)
        for part, ref in enumerate((mine2_ref, mine3_ref, other2_ref, other3_ref)):

            def add(i, total, part=part, ref=ref):
                start = pl.multiple_of(i * PIECE, PIECE)
                values = ref[pl.ds(start, PIECE), lanes]
                whole[pl.ds(start + part * (TOKENS // 4), PIECE), lanes] = values
                return total + fold(values.astype(jnp.float32))

            total = lax.fori_loop(0, n // 4, add, total)
        mean = jnp.sum(total, axis=0, keepdims=True) / TOKENS

        def rows(i):
            return whole[pl.ds(pl.multiple_of(i * PIECE, PIECE), PIECE), lanes].astype(jnp.float32)

        def square(i, total):
            centered = rows(i) - mean
            return total + fold(centered * centered)

        variance = jnp.sum(lax.fori_loop(0, n, square, jnp.zeros((8, TILE), jnp.float32)), axis=0, keepdims=True) / TOKENS
        scale = 1.0 / jnp.sqrt(variance + EPS)
        sums = jnp.zeros((TILE, 1), jnp.float32)
        for slot in range(n):
            standard = ((rows(place_ref[slot]) - mean) * scale).T.astype(jnp.bfloat16)
            out_ref[first : first + TILE, slot * PIECE : (slot + 1) * PIECE] = standard
            sums += jnp.sum(standard.astype(jnp.float32), axis=1, keepdims=True)
        sums_ref[first : first + TILE, :] = jnp.broadcast_to(sums, (TILE, 128))


def call(kernel, outs, in_specs, scratch, flops, moved, args):
    return pl.pallas_call(
        kernel,
        out_shape=outs,
        in_specs=in_specs,
        out_specs=[pl.BlockSpec(memory_space=pltpu.VMEM)] * len(outs),
        scratch_shapes=scratch,
        compiler_params=pltpu.CompilerParams(vmem_limit_bytes=32 * 2**20),
        cost_estimate=pl.CostEstimate(flops=flops // 64, bytes_accessed=moved // 64, transcendentals=0),
    )(*args)


VMEM = pl.BlockSpec(memory_space=pltpu.VMEM)


def slab_standard(quarters, place):
    return call(
        slab_kernel,
        [jax.ShapeDtypeStruct((ROWS_DEV, TOKENS), jnp.bfloat16), jax.ShapeDtypeStruct((ROWS_DEV, 128), jnp.float32)],
        [pl.BlockSpec(memory_space=pltpu.SMEM)] + [VMEM] * 4,
        [pltpu.VMEM((TOKENS, ROWS_DEV), jnp.bfloat16)],
        8 * TOKENS * ROWS_DEV,
        4 * TOKENS * ROWS_DEV,
        (place, *quarters),
    )


def tile_at(ref, part, lanes):
    return ref[pl.ds(pl.multiple_of(part * PIECE, PIECE), PIECE), lanes].astype(jnp.float32)


def over_tiles(width, body):
    whole = width // TILE

    @pl.loop(0, whole)
    def _(j):
        body(j * TILE, TILE)

    if width % TILE:
        body(whole * TILE, width % TILE)


def at(start, size):
    return pl.ds(pl.multiple_of(start, 128), size)


def product(slab_ref, shifted, spans, size):
    acc, row = None, 0
    for first, depth in spans:
        part = jnp.dot(
            slab_ref[:, first : first + depth], shifted[row : row + depth, :size], preferred_element_type=jnp.float32
        )
        acc = part if acc is None else acc + part
        row += depth
    return acc


def early_kernel(slab_ref, own, x1, x2, y1, y2, x3, y3, acc_ref, pivot_ref, square_ref, shifted):
    width = own.shape[1]

    def tiles(pieces, offset, columns, spans):
        def body(start, size):
            lanes = at(start + offset, size)

            def load(piece):
                ref, part, whole = piece
                return tile_at(ref, part, lanes if whole else at(start, size))

            total = jnp.zeros((8, size), jnp.float32)
            for piece in pieces:
                total += fold(load(piece))
            pivot = jnp.sum(total, axis=0, keepdims=True) / (len(pieces) * PIECE)
            square = jnp.zeros((8, size), jnp.float32)
            for i, piece in enumerate(pieces):
                values = load(piece) - pivot
                square += fold(values * values)
                shifted[i * PIECE : (i + 1) * PIECE, :size] = values.astype(jnp.bfloat16)
            pivot_ref[:, lanes] = jnp.broadcast_to(pivot, (8, size))
            square_ref[:, lanes] = square
            acc_ref[:, lanes] = product(slab_ref, shifted, spans, size)

        over_tiles(columns, body)

    near = [(own, 0, True), (x1, 0, True), (x2, 0, True), (x2, 1, True)]
    tiles(
        near
        + [(y1, 0, False), (x3, 0, False), (y2, 0, False), (x3, 1, False), (y2, 1, False), (x3, 2, False)],
        0,
        FIRST,
        [(0, 1280)],
    )
    tiles(near + [(y3, i, False) for i in range(4)], FIRST, width - FIRST, [(0, 768), (1280, 256)])


def late_kernel(slab_ref, sums_ref, acc_ref, pivot_ref, square_ref, x4, y4, out_ref, shifted):
    width = acc_ref.shape[1]

    def tiles(pieces, offset, columns, spans):
        def body(start, size):
            lanes = at(start + offset, size)
            pivot = pivot_ref[0:1, lanes]
            total = jnp.zeros((8, size), jnp.float32)
            square = square_ref[:, lanes]
            for i, (ref, part) in enumerate(pieces):
                values = tile_at(ref, part, at(start, size)) - pivot
                total += fold(values)
                square += fold(values * values)
                shifted[i * PIECE : (i + 1) * PIECE, :size] = values.astype(jnp.bfloat16)
            delta = jnp.sum(total, axis=0, keepdims=True) / TOKENS
            variance = jnp.sum(square, axis=0, keepdims=True) / TOKENS - delta * delta
            scale = 1.0 / (jnp.sqrt(jnp.maximum(variance, 0.0) + EPS) * TOKENS)
            acc = acc_ref[:, lanes] + product(slab_ref, shifted, spans, size)
            out_ref[:, lanes] = ((acc - sums_ref[:, 0:1] * delta) * scale).astype(jnp.bfloat16)

        over_tiles(columns, body)

    tiles([(x4, i) for i in (0, 3, 1, 4, 2, 5)], 0, FIRST, [(1280, 768)])
    tiles([(y4, i) for i in (0, 1, 4, 5, 2, 3, 6, 7)], FIRST, width - FIRST, [(768, 512), (1536, 512)])


def per_device(activations):
    together = lax.optimization_barrier
    tok, units = activations.shape
    n_col = 32
    width = units // n_col
    slab = activations[:, : 16 * ROWS_DEV].reshape(tok, 1, 16, ROWS_DEV)
    with_slab = jnp.concatenate(
        [activations.reshape(tok, 2, 16, width), jnp.broadcast_to(slab, (tok, 2, 16, ROWS_DEV))], axis=3
    )
    block = lax.all_to_all(
        with_slab.reshape(tok, n_col * (width + ROWS_DEV)), ("yl", "z", "c"), split_axis=1, concat_axis=0, tiled=True
    )
    own, own_first, slab0 = block[:, :width], block[:, :FIRST], block[:, width:]
    y1 = exchange(own_first, "yh", 0)
    x1 = exchange(own, "x", 0)
    slab0 = swap_places(slab0)
    x1, y1, slab0 = together((x1, y1, slab0))
    y2 = exchange(jnp.concatenate([own_first, y1], axis=0), "yh", 1)
    x2 = exchange(jnp.concatenate([own, x1], axis=0), "x", 1)
    slab1 = jnp.concatenate([slab0, z_permute(slab0, 0)], axis=0)
    slab2 = z_permute(slab1, 1)
    x2, y2, slab1, slab2 = together((x2, y2, slab1, slab2))
    rest = jnp.concatenate([own[:, FIRST:], x1[:, FIRST:], x2[:, FIRST:]], axis=0)
    three = jnp.concatenate([y1, y2], axis=0)
    y3 = exchange(rest, "yh", 0)
    x3 = exchange(three, "x", 0)
    slab2 = jnp.concatenate([slab1, slab2], axis=0)
    slab3 = z_permute(slab2, 2)
    x3, y3, slab2, slab3 = together((x3, y3, slab2, slab3))
    rest = jnp.concatenate([rest, y3], axis=0)
    y4 = exchange(rest, "yh", 1)
    three, x3, rest = together((three, x3, rest))
    x4 = exchange(jnp.concatenate([three, x3], axis=0), "x", 1)

    quarters = [slab2, slab3] + [lax.ppermute(part, "c", [(0, 1), (1, 0)]) for part in (slab2, slab3)]

    near = jnp.where(lax.axis_index("c") == 0, 1, 3)
    flips = [0, near, 4 - near, 2]
    token_of = jnp.stack(
        [(lax.axis_index("x") ^ flips[i]) * 4 + (lax.axis_index("yh") ^ flips[j]) for i, j in SLOTS]
    )
    core = lax.axis_index("c")
    table = jnp.asarray(z_places())[lax.axis_index("z")]
    table = jnp.where(core == 0, table, table[::-1])
    place = jnp.where(token_of % 2 == core, table[0][token_of // 2], table[1][token_of // 2] + 8)
    slab, sums = slab_standard(quarters, place.astype(jnp.int32))

    wide = jax.ShapeDtypeStruct((8, width), jnp.float32)
    acc, pivot, square = call(
        early_kernel,
        [jax.ShapeDtypeStruct((ROWS_DEV, width), jnp.float32), wide, wide],
        [VMEM] * 8,
        [pltpu.VMEM((1280, TILE), jnp.bfloat16)],
        TOKENS * ROWS_DEV * width,
        4 * ROWS_DEV * width,
        (slab, own, x1, x2, y1, y2, x3, y3),
    )
    (out,) = call(
        late_kernel,
        [jax.ShapeDtypeStruct((ROWS_DEV, width), jnp.bfloat16)],
        [VMEM] * 7,
        [pltpu.VMEM((1024, TILE), jnp.bfloat16)],
        TOKENS * ROWS_DEV * width,
        4 * ROWS_DEV * width,
        (slab, sums, acc, pivot, square, x4, y4),
    )
    return out


def solution(mesh):
    fine = Mesh(mesh.devices.reshape(4, 4, 2, 8, 2), ALL)
    out_specs = P(("x", "yh"), ("yl", "z", "c"))
    return jax.shard_map(per_device, mesh=fine, in_specs=(P(ALL, None),), out_specs=out_specs, check_vma=False)
```

time: 154 us -> 149 us (0.968)
  starting transfers between devices: 59.1 us -> 54.5 us
  waiting for transfers between devices: 38.3 us -> 35.2 us
    ppermute x6, starting transfers between devices: 22.8 us -> 15 us  [the longest x3 5.76 us: z_permute(): return lax.ppermute(values, ('z', 'c'), perm)]
    ppermute x8, starting transfers between devices: 36.3 us -> 39.5 us  [exchange(): return lax.ppermute(values, (axis, 'c'), perm)]
    ppermute x8, waiting for transfers between devices: 14.9 us -> 12.9 us  [exchange(): return lax.ppermute(values, (axis, 'c'), perm)]
    unnamed x25 -> x17, local copies, waits for them, and re-layouts: 3.68 us -> 2.98 us
  transfers between devices with their start and end apart: 14 -> 14, of which waited for: 7 -> 6; matrix products, arithmetic and copies ran while one was open for 2% -> 3% of each run, Pallas kernels for 6% -> 7%
where the time goes in v3:
time: 149 us; the launch traced here: 147 us
  starting transfers between devices  54.5 us (37%)
  waiting for transfers between devices  35.2 us (24%)
  blocking collectives  28.7 us (19%)
  Pallas kernels  16 us (11%)
  local copies, waits for them, and re-layouts  7.39 us (5%)
  other arithmetic  4.65 us (3%)
    ppermute x8, starting transfers between devices, exchange(): return lax.ppermute(values, (axis, 'c'), perm)  39.5 us
    all_to_all x1, blocking collectives, per_device(): lax.all_to_all(with_slab.reshape(tok, n_col * (width + ROWS_DEV)), ('yl',...  28.7 us
    pallas_call x3, Pallas kernels, call(): pl.pallas_call(kernel, out_shape=outs, in_specs=in_specs, out_specs=[pl.B...  16 us
    ppermute x3, waiting for transfers between devices, z_permute(): return lax.ppermute(values, ('z', 'c'), perm)  15.7 us
    ppermute x8, waiting for transfers between devices, exchange(): return lax.ppermute(values, (axis, 'c'), perm)  12.9 us
    ppermute x1, waiting for transfers between devices, swap_places(): return lax.ppermute(values, ALL, perm)  6.18 us
    ppermute x3, starting transfers between devices, z_permute(): return lax.ppermute(values, ('z', 'c'), perm)  5.76 us
    ppermute x1, starting transfers between devices, swap_places(): return lax.ppermute(values, ALL, perm)  4.89 us
  transfers between devices with their start and end apart: 14, of which 6 were waited for; matrix products, arithmetic and copies ran while one was open for 3% of the time, Pallas kernels for 7%

profile of v3, /device:TPU:6, one launch (start us, length us, event | category | flops | bytes accessed | tf_op | source)
XLA Modules:
  0.0 146.9 jit_solution(9075165307885848318)
XLA Ops:
  2.2 28.7 %all_to_all.16 = bf16[4,32,2304]{2,0,1:T(4,128)(2,1)S(1)} all-to-all(bf16[4,32,2304]{2,0,1:T(4,128)(2,1)S(1)} %pad_maximum_fusion.4), channel_id=1, replica_groups=mesh['x'=4,'yh'=4,'yl'=2,'z'=8,'c'=2] {'yl','z','c'}, dimensions={1} | all-to-all | bytes 1179648 | tf_op jit(solution)/shard_map/all_to_all | solution.py:218
  31.1 2.7 %collective-permute-start = (bf16[128,1792]{1,0:T(8,128)(2,1)S(1)}, bf16[128,1792]{1,0:T(8,128)(2,1)S(1)}, u32[]{:S(2)}, u32[]{:S(2)}) collective-permute-start(bf16[128,1792]{1,0:T(8,128)(2,1)S(1)} %slice.41.own), channel_id=1, source_target_pairs={{0,128},{1,385},{128,0},{129,257},{256,384},{257,129},{384,256},{3... | collective-permute-start | bytes 1376264 | tf_op jit(solution)/shard_map/ppermute | solution.py:27
  33.9 4.5 %collective-permute-start.1 = (bf16[128,1408]{1,0:T(8,128)(2,1)S(1)}, bf16[128,1408]{1,0:T(8,128)(2,1)S(1)}, u32[]{:S(2)}, u32[]{:S(2)}) collective-permute-start(bf16[128,1408]{1,0:T(8,128)(2,1)S(1)} %slice.42), channel_id=1, source_target_pairs={{0,32},{1,97},{32,0},{33,65},{64,96},{65,33},{96,64},{97,1},{2,34}... | collective-permute-start | bytes 1081352 | tf_op jit(solution)/shard_map/ppermute | solution.py:27
  38.4 4.9 %collective-permute-start.2 = (bf16[128,512]{1,0:T(8,128)(2,1)S(1)}, bf16[128,512]{1,0:T(8,128)(2,1)S(1)}, u32[]{:S(2)}, u32[]{:S(2)}) collective-permute-start(bf16[128,512]{1,0:T(8,128)(2,1)S(1)} %slice.43), channel_id=1, source_target_pairs={{0,0},{1,32},{2,64},{3,96},{4,128},{5,160},{6,192},{7,224},{8,256}... | collective-permute-start | bytes 393224 | tf_op jit(solution)/shard_map/ppermute | solution.py:32
  43.3 6.2 %collective-permute-done.2 = bf16[128,512]{1,0:T(8,128)(2,1)S(1)} collective-permute-done((bf16[128,512]{1,0:T(8,128)(2,1)S(1)}, bf16[128,512]{1,0:T(8,128)(2,1)S(1)}, u32[]{:S(2)}, u32[]{:S(2)}) %collective-permute-start.2) | collective-permute-done | bytes 131104 | tf_op jit(solution)/shard_map/ppermute | solution.py:32
  49.6 1.9 %collective-permute-start.3 = (bf16[256,1792]{1,0:T(8,128)(2,1)S(1)}, bf16[256,1792]{1,0:T(8,128)(2,1)S(1)}, u32[]{:S(2)}, u32[]{:S(2)}) collective-permute-start(bf16[256,1792]{1,0:T(8,128)(2,1)S(1)} %pad_maximum_fusion.1), channel_id=1, source_target_pairs={{0,384},{1,129},{128,256},{129,1},{256,128},{257,385},{384,0},{385... | collective-permute-start | bytes 2752520 | tf_op jit(solution)/shard_map/ppermute | solution.py:27
  51.6 15.0 %collective-permute-start.4 = (bf16[256,1408]{1,0:T(8,128)(2,1)S(1)}, bf16[256,1408]{1,0:T(8,128)(2,1)S(1)}, u32[]{:S(2)}, u32[]{:S(2)}) collective-permute-start(bf16[256,1408]{1,0:T(8,128)(2,1)S(1)} %pad_maximum_fusion.3), channel_id=1, source_target_pairs={{0,96},{1,33},{32,64},{33,1},{64,32},{65,97},{96,0},{97,65},{2,98}... | collective-permute-start | bytes 2162696 | tf_op jit(solution)/shard_map/ppermute | solution.py:27
  66.5 1.9 %collective-permute-start.5 = (bf16[128,512]{1,0:T(8,128)(2,1)S(1)}, bf16[128,512]{1,0:T(8,128)(2,1)S(1)}, u32[]{:S(2)}, u32[]{:S(2)}) collective-permute-start(bf16[128,512]{1,0:T(8,128)(2,1)S(1)} %collective-permute-done.2), channel_id=1, source_target_pairs={{0,6},{1,11},{2,12},{3,9},{4,10},{5,15},{6,0},{7,13},{8,14},{9,3},... | collective-permute-start | bytes 393224 | tf_op jit(solution)/shard_map/ppermute | solution.py:42
  68.5 8.2 %collective-permute-done.5 = bf16[128,512]{1,0:T(8,128)(2,1)S(1)} collective-permute-done((bf16[128,512]{1,0:T(8,128)(2,1)S(1)}, bf16[128,512]{1,0:T(8,128)(2,1)S(1)}, u32[]{:S(2)}, u32[]{:S(2)}) %collective-permute-start.5) | collective-permute-done | bytes 131104 | tf_op jit(solution)/shard_map/ppermute | solution.py:42
  76.7 1.9 %collective-permute-start.6 = (bf16[256,512]{1,0:T(8,128)(2,1)S(1)}, bf16[256,512]{1,0:T(8,128)(2,1)S(1)}, u32[]{:S(2)}, u32[]{:S(2)}) collective-permute-start(bf16[256,512]{1,0:T(8,128)(2,1)S(1)} %constant_dynamic-update-slice_fusion), channel_id=1, source_target_pairs={{0,14},{1,3},{2,4},{3,1},{4,2},{5,7},{6,8},{7,5},{8,6},{9,11},{10,... | collective-permute-start | bytes 786440 | tf_op jit(solution)/shard_map/ppermute | solution.py:42
  78.7 7.5 %collective-permute-done.6 = bf16[256,512]{1,0:T(8,128)(2,1)S(1)} collective-permute-done((bf16[256,512]{1,0:T(8,128)(2,1)S(1)}, bf16[256,512]{1,0:T(8,128)(2,1)S(1)}, u32[]{:S(2)}, u32[]{:S(2)}) %collective-permute-start.6) | collective-permute-done | bytes 262176 | tf_op jit(solution)/shard_map/ppermute | solution.py:42
  86.3 4.4 %collective-permute-start.7 = (bf16[384,1408]{1,0:T(8,128)(2,1)S(1)}, bf16[384,1408]{1,0:T(8,128)(2,1)S(1)}, u32[]{:S(2)}, u32[]{:S(2)}) collective-permute-start(bf16[384,1408]{1,0:T(8,128)(2,1)S(1)} %constant_dynamic-update-slice_fusion.2), channel_id=1, source_target_pairs={{0,128},{1,385},{128,0},{129,257},{256,384},{257,129},{384,256},{3... | collective-permute-start | bytes 3244040 | tf_op jit(solution)/shard_map/ppermute | solution.py:27
  90.8 1.9 %collective-permute-start.9 = (bf16[512,512]{1,0:T(8,128)(2,1)S(1)}, bf16[512,512]{1,0:T(8,128)(2,1)S(1)}, u32[]{:S(2)}, u32[]{:S(2)}) collective-permute-start(bf16[512,512]{1,0:T(8,128)(2,1)S(1)} %constant_dynamic-update-slice_fusion.4.mine2_ref), channel_id=1, source_target_pairs={{0,2},{1,15},{2,0},{3,5},{4,6},{5,3},{6,4},{7,9},{8,10},{9,7},{10,... | collective-permute-start | bytes 1572872 | tf_op jit(solution)/shard_map/ppermute | solution.py:42
  93.7 1.9 %collective-permute-start.8 = (bf16[512,384]{1,0:T(8,128)(2,1)S(1)}, bf16[512,384]{1,0:T(8,128)(2,1)S(1)}, u32[]{:S(2)}, u32[]{:S(2)}) collective-permute-start(bf16[512,384]{1,0:T(8,128)(2,1)S(1)} %pad_maximum_fusion.5), channel_id=1, source_target_pairs={{0,32},{1,97},{32,0},{33,65},{64,96},{65,33},{96,64},{97,1},{2,34}... | collective-permute-start | bytes 1179656 | tf_op jit(solution)/shard_map/ppermute | solution.py:27
  95.7 9.0 %collective-permute-done.8.y3 = bf16[512,384]{1,0:T(8,128)(2,1)S(1)} collective-permute-done((bf16[512,384]{1,0:T(8,128)(2,1)S(1)}, bf16[512,384]{1,0:T(8,128)(2,1)S(1)}, u32[]{:S(2)}, u32[]{:S(2)}) %collective-permute-start.8) | collective-permute-done | bytes 393248 | tf_op jit(solution)/shard_map/ppermute | solution.py:27
  106.5 1.5 %pad_maximum_fusion = bf16[768,1408]{1,0:T(8,128)(2,1)} fusion(bf16[384,1408]{1,0:T(8,128)(2,1)S(1)} %collective-permute-done.7.x3, bf16[384,1408]{1,0:T(8,128)(2,1)S(1)} %constant_dynamic-update-slice_fusion.2), kind=kLoop, calls=%fused_computation.2 | loop fusion | flops 4325376 | bytes 4325376 | tf_op jit(solution)/shard_map/concatenate | solution.py:241
  108.0 7.2 %collective-permute-start.12 = (bf16[768,1408]{1,0:T(8,128)(2,1)}, bf16[768,1408]{1,0:T(8,128)(2,1)}, u32[]{:S(2)}, u32[]{:S(2)}) collective-permute-start(bf16[768,1408]{1,0:T(8,128)(2,1)} %pad_maximum_fusion), channel_id=1, source_target_pairs={{0,384},{1,129},{128,256},{129,1},{256,128},{257,385},{384,0},{385... | collective-permute-start | bytes 6488072 | tf_op jit(solution)/shard_map/ppermute | solution.py:27
  116.7 1.9 %collective-permute-start.13 = (bf16[1024,384]{1,0:T(8,128)(2,1)}, bf16[1024,384]{1,0:T(8,128)(2,1)}, u32[]{:S(2)}, u32[]{:S(2)}) collective-permute-start(bf16[1024,384]{1,0:T(8,128)(2,1)} %pad_maximum_fusion.2), channel_id=1, source_target_pairs={{0,96},{1,33},{32,64},{33,1},{64,32},{65,97},{96,0},{97,65},{2,98}... | collective-permute-start | bytes 2359304 | tf_op jit(solution)/shard_map/ppermute | solution.py:27
  118.6 1.9 %collective-permute-start.10 = (bf16[512,512]{1,0:T(8,128)(2,1)}, bf16[512,512]{1,0:T(8,128)(2,1)}, u32[]{:S(2)}, u32[]{:S(2)}) collective-permute-start(bf16[512,512]{1,0:T(8,128)(2,1)} %copy-done.2), channel_id=1, source_target_pairs={{0,1},{1,0},{2,3},{3,2},{4,5},{5,4},{6,7},{7,6},{8,9},{9,8},{10,11... | collective-permute-start | bytes 1572872 | tf_op jit(solution)/shard_map/ppermute | solution.py:243
  120.6 2.4 %collective-permute-start.11 = (bf16[512,512]{1,0:T(8,128)(2,1)}, bf16[512,512]{1,0:T(8,128)(2,1)}, u32[]{:S(2)}, u32[]{:S(2)}) collective-permute-start(bf16[512,512]{1,0:T(8,128)(2,1)} %copy-done.4), channel_id=1, source_target_pairs={{0,1},{1,0},{2,3},{3,2},{4,5},{5,4},{6,7},{7,6},{8,9},{9,8},{10,11... | collective-permute-start | bytes 1572872 | tf_op jit(solution)/shard_map/ppermute | solution.py:243
  126.9 4.7 %shard_map.28 = (bf16[512,2048]{1,0:T(8,128)(2,1)S(1)}, f32[512,128]{1,0:T(8,128)S(1)}) custom-call(s32[16]{0:T(128)S(1)} %compare_select_fusion.3.place_ref, bf16[512,512]{1,0:T(8,128)(2,1)S(1)} %copy-done.3, bf16[512,512]{1,0:T(8,128)(2,1)S(1)} %copy-done.5, bf16[512,512]{1,0:T(8,128)(2,1)} %collective-permute-done.10.other2_ref, ...), custom_call_target="tpu_custom_call" | custom-call | flops 131072 | bytes 65536 | tf_op jit(solution)/shard_map/pallas_call | solution.py:90
  131.6 4.9 %shard_map.29 = (f32[512,1792]{1,0:T(8,128)S(1)}, f32[8,1792]{1,0:T(8,128)S(1)}, f32[8,1792]{1,0:T(8,128)S(1)}) custom-call(bf16[512,2048]{1,0:T(8,128)(2,1)S(1)} %get-tuple-element.32.slab_ref, bf16[128,1792]{1,0:T(8,128)(2,1)S(1)} %slice.41.own, bf16[128,1792]{1,0:T(8,128)(2,1)S(1)} %collective-permute-done.x1, bf16[256,1792]{1,0:T(8,128)(2,1)S(1)} %copy-done.1, ...), custom_call_target="tpu_custom_call" | custom-call | flops 29360128 | bytes 57344 | tf_op jit(solution)/shard_map/pallas_call | solution.py:90
  136.6 3.9 %collective-permute-done.13.y4 = bf16[1024,384]{1,0:T(8,128)(2,1)} collective-permute-done((bf16[1024,384]{1,0:T(8,128)(2,1)}, bf16[1024,384]{1,0:T(8,128)(2,1)}, u32[]{:S(2)}, u32[]{:S(2)}) %collective-permute-start.13) | collective-permute-done | bytes 786464 | tf_op jit(solution)/shard_map/ppermute | solution.py:27
  140.5 6.4 %shard_map.30 = bf16[512,1792]{1,0:T(8,128)(2,1)} custom-call(bf16[512,2048]{1,0:T(8,128)(2,1)S(1)} %get-tuple-element.32.slab_ref, f32[512,128]{1,0:T(8,128)S(1)} %get-tuple-element.33.sums_ref, f32[512,1792]{1,0:T(8,128)S(1)} %get-tuple-element.37.acc_ref, f32[8,1792]{1,0:T(8,128)S(1)} %get-tuple-element.38.pivot_ref, ...), custom_call_target="tpu_custom_call" | custom-call | flops 29360128 | bytes 57344 | tf_op jit(solution)/shard_map/pallas_call | solution.py:90
  (54 shorter events, 10.9 us)
Async XLA Ops:
  31.1 18.5 %copy-start.6 = (bf16[128,2304]{1,0:T(8,128)(2,1)}, bf16[128,2304]{1,0:T(8,128)(2,1)S(1)}, u32[]{:S(2)}) copy-start(bf16[128,2304]{1,0:T(8,128)(2,1)S(1)} %all_to_all.14) | copy-start | bytes 1769476
  31.1 18.4 %collective-permute-start = (bf16[128,1792]{1,0:T(8,128)(2,1)S(1)}, bf16[128,1792]{1,0:T(8,128)(2,1)S(1)}, u32[]{:S(2)}, u32[]{:S(2)}) collective-permute-start(bf16[128,1792]{1,0:T(8,128)(2,1)S(1)} %slice.41.own), channel_id=1, source_target_pairs={{0,128},{1,385},{128,0},{129,257},{256,384},{257,129},{384,256},{3... | collective-permute-start | bytes 1376264 | tf_op jit(solution)/shard_map/ppermute | solution.py:27
  33.9 15.6 %collective-permute-start.1 = (bf16[128,1408]{1,0:T(8,128)(2,1)S(1)}, bf16[128,1408]{1,0:T(8,128)(2,1)S(1)}, u32[]{:S(2)}, u32[]{:S(2)}) collective-permute-start(bf16[128,1408]{1,0:T(8,128)(2,1)S(1)} %slice.42), channel_id=1, source_target_pairs={{0,32},{1,97},{32,0},{33,65},{64,96},{65,33},{96,64},{97,1},{2,34}... | collective-permute-start | bytes 1081352 | tf_op jit(solution)/shard_map/ppermute | solution.py:27
  38.4 11.1 %collective-permute-start.2 = (bf16[128,512]{1,0:T(8,128)(2,1)S(1)}, bf16[128,512]{1,0:T(8,128)(2,1)S(1)}, u32[]{:S(2)}, u32[]{:S(2)}) collective-permute-start(bf16[128,512]{1,0:T(8,128)(2,1)S(1)} %slice.43), channel_id=1, source_target_pairs={{0,0},{1,32},{2,64},{3,96},{4,128},{5,160},{6,192},{7,224},{8,256}... | collective-permute-start | bytes 393224 | tf_op jit(solution)/shard_map/ppermute | solution.py:32
  49.6 36.6 %collective-permute-start.3 = (bf16[256,1792]{1,0:T(8,128)(2,1)S(1)}, bf16[256,1792]{1,0:T(8,128)(2,1)S(1)}, u32[]{:S(2)}, u32[]{:S(2)}) collective-permute-start(bf16[256,1792]{1,0:T(8,128)(2,1)S(1)} %pad_maximum_fusion.1), channel_id=1, source_target_pairs={{0,384},{1,129},{128,256},{129,1},{256,128},{257,385},{384,0},{385... | collective-permute-start | bytes 2752520 | tf_op jit(solution)/shard_map/ppermute | solution.py:27
  51.6 34.6 %collective-permute-start.4 = (bf16[256,1408]{1,0:T(8,128)(2,1)S(1)}, bf16[256,1408]{1,0:T(8,128)(2,1)S(1)}, u32[]{:S(2)}, u32[]{:S(2)}) collective-permute-start(bf16[256,1408]{1,0:T(8,128)(2,1)S(1)} %pad_maximum_fusion.3), channel_id=1, source_target_pairs={{0,96},{1,33},{32,64},{33,1},{64,32},{65,97},{96,0},{97,65},{2,98}... | collective-permute-start | bytes 2162696 | tf_op jit(solution)/shard_map/ppermute | solution.py:27
  66.5 10.2 %collective-permute-start.5 = (bf16[128,512]{1,0:T(8,128)(2,1)S(1)}, bf16[128,512]{1,0:T(8,128)(2,1)S(1)}, u32[]{:S(2)}, u32[]{:S(2)}) collective-permute-start(bf16[128,512]{1,0:T(8,128)(2,1)S(1)} %collective-permute-done.2), channel_id=1, source_target_pairs={{0,6},{1,11},{2,12},{3,9},{4,10},{5,15},{6,0},{7,13},{8,14},{9,3},... | collective-permute-start | bytes 393224 | tf_op jit(solution)/shard_map/ppermute | solution.py:42
  76.7 9.5 %collective-permute-start.6 = (bf16[256,512]{1,0:T(8,128)(2,1)S(1)}, bf16[256,512]{1,0:T(8,128)(2,1)S(1)}, u32[]{:S(2)}, u32[]{:S(2)}) collective-permute-start(bf16[256,512]{1,0:T(8,128)(2,1)S(1)} %constant_dynamic-update-slice_fusion), channel_id=1, source_target_pairs={{0,14},{1,3},{2,4},{3,1},{4,2},{5,7},{6,8},{7,5},{8,6},{9,11},{10,... | collective-permute-start | bytes 786440 | tf_op jit(solution)/shard_map/ppermute | solution.py:42
  86.2 7.5 %copy-start = (bf16[256,1792]{1,0:T(8,128)(2,1)}, bf16[256,1792]{1,0:T(8,128)(2,1)S(1)}, u32[]{:S(2)}) copy-start(bf16[256,1792]{1,0:T(8,128)(2,1)S(1)} %collective-permute-done.3.x2) | copy-start | bytes 2752516
  86.3 19.2 %collective-permute-start.7 = (bf16[384,1408]{1,0:T(8,128)(2,1)S(1)}, bf16[384,1408]{1,0:T(8,128)(2,1)S(1)}, u32[]{:S(2)}, u32[]{:S(2)}) collective-permute-start(bf16[384,1408]{1,0:T(8,128)(2,1)S(1)} %constant_dynamic-update-slice_fusion.2), channel_id=1, source_target_pairs={{0,128},{1,385},{128,0},{129,257},{256,384},{257,129},{384,256},{3... | collective-permute-start | bytes 3244040 | tf_op jit(solution)/shard_map/ppermute | solution.py:27
  90.8 13.9 %copy-start.2 = (bf16[512,512]{1,0:T(8,128)(2,1)}, bf16[512,512]{1,0:T(8,128)(2,1)S(1)}, u32[]{:S(2)}) copy-start(bf16[512,512]{1,0:T(8,128)(2,1)S(1)} %constant_dynamic-update-slice_fusion.4.mine2_ref) | copy-start | bytes 1572868
  90.8 13.9 %collective-permute-start.9 = (bf16[512,512]{1,0:T(8,128)(2,1)S(1)}, bf16[512,512]{1,0:T(8,128)(2,1)S(1)}, u32[]{:S(2)}, u32[]{:S(2)}) collective-permute-start(bf16[512,512]{1,0:T(8,128)(2,1)S(1)} %constant_dynamic-update-slice_fusion.4.mine2_ref), channel_id=1, source_target_pairs={{0,2},{1,15},{2,0},{3,5},{4,6},{5,3},{6,4},{7,9},{8,10},{9,7},{10,... | collective-permute-start | bytes 1572872 | tf_op jit(solution)/shard_map/ppermute | solution.py:42
  93.7 10.9 %collective-permute-start.8 = (bf16[512,384]{1,0:T(8,128)(2,1)S(1)}, bf16[512,384]{1,0:T(8,128)(2,1)S(1)}, u32[]{:S(2)}, u32[]{:S(2)}) collective-permute-start(bf16[512,384]{1,0:T(8,128)(2,1)S(1)} %pad_maximum_fusion.5), channel_id=1, source_target_pairs={{0,32},{1,97},{32,0},{33,65},{64,96},{65,33},{96,64},{97,1},{2,34}... | collective-permute-start | bytes 1179656 | tf_op jit(solution)/shard_map/ppermute | solution.py:27
  104.7 0.8 copy-start.4
  108.0 32.5 %collective-permute-start.12 = (bf16[768,1408]{1,0:T(8,128)(2,1)}, bf16[768,1408]{1,0:T(8,128)(2,1)}, u32[]{:S(2)}, u32[]{:S(2)}) collective-permute-start(bf16[768,1408]{1,0:T(8,128)(2,1)} %pad_maximum_fusion), channel_id=1, source_target_pairs={{0,384},{1,129},{128,256},{129,1},{256,128},{257,385},{384,0},{385... | collective-permute-start | bytes 6488072 | tf_op jit(solution)/shard_map/ppermute | solution.py:27
  116.7 23.8 %collective-permute-start.13 = (bf16[1024,384]{1,0:T(8,128)(2,1)}, bf16[1024,384]{1,0:T(8,128)(2,1)}, u32[]{:S(2)}, u32[]{:S(2)}) collective-permute-start(bf16[1024,384]{1,0:T(8,128)(2,1)} %pad_maximum_fusion.2), channel_id=1, source_target_pairs={{0,96},{1,33},{32,64},{33,1},{64,32},{65,97},{96,0},{97,65},{2,98}... | collective-permute-start | bytes 2359304 | tf_op jit(solution)/shard_map/ppermute | solution.py:27
  118.6 5.8 %collective-permute-start.10 = (bf16[512,512]{1,0:T(8,128)(2,1)}, bf16[512,512]{1,0:T(8,128)(2,1)}, u32[]{:S(2)}, u32[]{:S(2)}) collective-permute-start(bf16[512,512]{1,0:T(8,128)(2,1)} %copy-done.2), channel_id=1, source_target_pairs={{0,1},{1,0},{2,3},{3,2},{4,5},{5,4},{6,7},{7,6},{8,9},{9,8},{10,11... | collective-permute-start | bytes 1572872 | tf_op jit(solution)/shard_map/ppermute | solution.py:243
  120.6 4.3 %collective-permute-start.11 = (bf16[512,512]{1,0:T(8,128)(2,1)}, bf16[512,512]{1,0:T(8,128)(2,1)}, u32[]{:S(2)}, u32[]{:S(2)}) collective-permute-start(bf16[512,512]{1,0:T(8,128)(2,1)} %copy-done.4), channel_id=1, source_target_pairs={{0,1},{1,0},{2,3},{3,2},{4,5},{5,4},{6,7},{7,6},{8,9},{9,8},{10,11... | collective-permute-start | bytes 1572872 | tf_op jit(solution)/shard_map/ppermute | solution.py:243
  124.4 7.2 %copy-start.1 = (bf16[256,1792]{1,0:T(8,128)(2,1)S(1)}, bf16[256,1792]{1,0:T(8,128)(2,1)}, u32[]{:S(2)}) copy-start(bf16[256,1792]{1,0:T(8,128)(2,1)} %copy-done) | copy-start | bytes 2752516
  124.8 1.0 copy-start.3
  125.9 1.0 copy-start.5

commit v4 on v3

--- a/solution.py
+++ b/solution.py
@@ -117,15 +117,16 @@
     return ref[pl.ds(pl.multiple_of(part * PIECE, PIECE), PIECE), lanes].astype(jnp.float32)
 
 
-def over_tiles(width, body):
-    whole = width // TILE
-
-    @pl.loop(0, whole)
+def over_tiles(width, scratch, body):
+    pairs = width // (2 * TILE)
+
+    @pl.loop(0, pairs)
     def _(j):
-        body(j * TILE, TILE)
-
-    if width % TILE:
-        body(whole * TILE, width % TILE)
+        for i in range(2):
+            body((2 * j + i) * TILE, TILE, scratch[i])
+
+    for i, start in enumerate(range(pairs * 2 * TILE, width, TILE)):
+        body(start, min(TILE, width - start), scratch[i])
 
 
 def at(start, size):
@@ -143,11 +144,11 @@
     return acc
 
 
-def early_kernel(slab_ref, own, x1, x2, y1, y2, x3, y3, acc_ref, pivot_ref, square_ref, shifted):
+def early_kernel(slab_ref, own, x1, x2, y1, y2, x3, y3, acc_ref, pivot_ref, square_ref, *scratch):
     width = own.shape[1]
 
     def tiles(pieces, offset, columns, spans):
-        def body(start, size):
+        def body(start, size, shifted):
             lanes = at(start + offset, size)
 
             def load(piece):
@@ -167,7 +168,7 @@
             square_ref[:, lanes] = square
             acc_ref[:, lanes] = product(slab_ref, shifted, spans, size)
 
-        over_tiles(columns, body)
+        over_tiles(columns, scratch, body)
 
     near = [(own, 0, True), (x1, 0, True), (x2, 0, True), (x2, 1, True)]
     tiles(
@@ -180,11 +181,11 @@
     tiles(near + [(y3, i, False) for i in range(4)], FIRST, width - FIRST, [(0, 768), (1280, 256)])
 
 
-def late_kernel(slab_ref, sums_ref, acc_ref, pivot_ref, square_ref, x4, y4, out_ref, shifted):
+def late_kernel(slab_ref, sums_ref, acc_ref, pivot_ref, square_ref, x4, y4, out_ref, *scratch):
     width = acc_ref.shape[1]
 
     def tiles(pieces, offset, columns, spans):
-        def body(start, size):
+        def body(start, size, shifted):
             lanes = at(start + offset, size)
             pivot = pivot_ref[0:1, lanes]
             total = jnp.zeros((8, size), jnp.float32)
@@ -200,7 +201,7 @@
             acc = acc_ref[:, lanes] + product(slab_ref, shifted, spans, size)
             out_ref[:, lanes] = ((acc - sums_ref[:, 0:1] * delta) * scale).astype(jnp.bfloat16)
 
-        over_tiles(columns, body)
+        over_tiles(columns, scratch, body)
 
     tiles([(x4, i) for i in (0, 3, 1, 4, 2, 5)], 0, FIRST, [(1280, 768)])
     tiles([(y4, i) for i in (0, 1, 4, 5, 2, 3, 6, 7)], FIRST, width - FIRST, [(768, 512), (1536, 512)])
@@ -227,8 +228,8 @@
     x2 = exchange(jnp.concatenate([own, x1], axis=0), "x", 1)
     slab1 = jnp.concatenate([slab0, z_permute(slab0, 0)], axis=0)
     slab2 = z_permute(slab1, 1)
-    x2, y2, slab1, slab2 = together((x2, y2, slab1, slab2))
     rest = jnp.concatenate([own[:, FIRST:], x1[:, FIRST:], x2[:, FIRST:]], axis=0)
+    x2, y2, rest, slab1, slab2 = together((x2, y2, rest, slab1, slab2))
     three = jnp.concatenate([y1, y2], axis=0)
     y3 = exchange(rest, "yh", 0)
     x3 = exchange(three, "x", 0)
@@ -237,7 +238,6 @@
     x3, y3, slab2, slab3 = together((x3, y3, slab2, slab3))
     rest = jnp.concatenate([rest, y3], axis=0)
     y4 = exchange(rest, "yh", 1)
-    three, x3, rest = together((three, x3, rest))
     x4 = exchange(jnp.concatenate([three, x3], axis=0), "x", 1)
 
     quarters = [slab2, slab3] + [lax.ppermute(part, "c", [(0, 1), (1, 0)]) for part in (slab2, slab3)]
@@ -258,7 +258,7 @@
         early_kernel,
         [jax.ShapeDtypeStruct((ROWS_DEV, width), jnp.float32), wide, wide],
         [VMEM] * 8,
-        [pltpu.VMEM((1280, TILE), jnp.bfloat16)],
+        [pltpu.VMEM((1280, TILE), jnp.bfloat16)] * 2,
         TOKENS * ROWS_DEV * width,
         4 * ROWS_DEV * width,
         (slab, own, x1, x2, y1, y2, x3, y3),
@@ -267,7 +267,7 @@
         late_kernel,
         [jax.ShapeDtypeStruct((ROWS_DEV, width), jnp.bfloat16)],
         [VMEM] * 7,
-        [pltpu.VMEM((1024, TILE), jnp.bfloat16)],
+        [pltpu.VMEM((1024, TILE), jnp.bfloat16)] * 2,
         TOKENS * ROWS_DEV * width,
         4 * ROWS_DEV * width,
         (slab, sums, acc, pivot, square, x4, y4),

time: 149 us -> 147 us (0.987); the launches traced: 147 us -> 146 us
  transfers between devices with their start and end apart: 14 -> 14, of which waited for: 6 -> 6; matrix products, arithmetic and copies ran while one was open for 3% -> 4% of each run, Pallas kernels for 7% -> 6%
where the time goes in v4:
time: 147 us; the launch traced here: 146 us
  starting transfers between devices  54.5 us (37%)
  waiting for transfers between devices  35.8 us (24%)
  blocking collectives  28.7 us (20%)
  Pallas kernels  14.8 us (10%)
  local copies, waits for them, and re-layouts  6.36 us (4%)
  other arithmetic  5.78 us (4%)
    ppermute x8, starting transfers between devices, exchange(): return lax.ppermute(values, (axis, 'c'), perm)  39.5 us
    all_to_all x1, blocking collectives, per_device(): lax.all_to_all(with_slab.reshape(tok, n_col * (width + ROWS_DEV)), ('yl',...  28.7 us
    ppermute x3, waiting for transfers between devices, z_permute(): return lax.ppermute(values, ('z', 'c'), perm)  15.6 us
    pallas_call x3, Pallas kernels, call(): pl.pallas_call(kernel, out_shape=outs, in_specs=in_specs, out_specs=[pl.B...  14.8 us
    ppermute x8, waiting for transfers between devices, exchange(): return lax.ppermute(values, (axis, 'c'), perm)  13.7 us
    ppermute x1, waiting for transfers between devices, swap_places(): return lax.ppermute(values, ALL, perm)  6.18 us
    ppermute x3, starting transfers between devices, z_permute(): return lax.ppermute(values, ('z', 'c'), perm)  5.76 us
    ppermute x1, starting transfers between devices, swap_places(): return lax.ppermute(values, ALL, perm)  4.89 us
  transfers between devices with their start and end apart: 14, of which 6 were waited for; matrix products, arithmetic and copies ran while one was open for 4% of the time, Pallas kernels for 6%

profile of v4, /device:TPU:6, one launch (start us, length us, event | category | flops | bytes accessed | tf_op | source)
XLA Modules:
  0.0 146.4 jit_solution(10727217116465418589)
XLA Ops:
  2.2 28.7 %all_to_all.16 = bf16[4,32,2304]{2,0,1:T(4,128)(2,1)S(1)} all-to-all(bf16[4,32,2304]{2,0,1:T(4,128)(2,1)S(1)} %pad_maximum_fusion.5), channel_id=1, replica_groups=mesh['x'=4,'yh'=4,'yl'=2,'z'=8,'c'=2] {'yl','z','c'}, dimensions={1} | all-to-all | bytes 1179648 | tf_op jit(solution)/shard_map/all_to_all | solution.py:219
  31.1 2.7 %collective-permute-start = (bf16[128,1792]{1,0:T(8,128)(2,1)S(1)}, bf16[128,1792]{1,0:T(8,128)(2,1)S(1)}, u32[]{:S(2)}, u32[]{:S(2)}) collective-permute-start(bf16[128,1792]{1,0:T(8,128)(2,1)S(1)} %slice.41.own), channel_id=1, source_target_pairs={{0,128},{1,385},{128,0},{129,257},{256,384},{257,129},{384,256},{3... | collective-permute-start | bytes 1376264 | tf_op jit(solution)/shard_map/ppermute | solution.py:27
  33.9 4.5 %collective-permute-start.1 = (bf16[128,1408]{1,0:T(8,128)(2,1)S(1)}, bf16[128,1408]{1,0:T(8,128)(2,1)S(1)}, u32[]{:S(2)}, u32[]{:S(2)}) collective-permute-start(bf16[128,1408]{1,0:T(8,128)(2,1)S(1)} %slice.42), channel_id=1, source_target_pairs={{0,32},{1,97},{32,0},{33,65},{64,96},{65,33},{96,64},{97,1},{2,34}... | collective-permute-start | bytes 1081352 | tf_op jit(solution)/shard_map/ppermute | solution.py:27
  38.4 4.9 %collective-permute-start.2 = (bf16[128,512]{1,0:T(8,128)(2,1)S(1)}, bf16[128,512]{1,0:T(8,128)(2,1)S(1)}, u32[]{:S(2)}, u32[]{:S(2)}) collective-permute-start(bf16[128,512]{1,0:T(8,128)(2,1)S(1)} %slice.43), channel_id=1, source_target_pairs={{0,0},{1,32},{2,64},{3,96},{4,128},{5,160},{6,192},{7,224},{8,256}... | collective-permute-start | bytes 393224 | tf_op jit(solution)/shard_map/ppermute | solution.py:32
  43.3 6.2 %collective-permute-done.2 = bf16[128,512]{1,0:T(8,128)(2,1)S(1)} collective-permute-done((bf16[128,512]{1,0:T(8,128)(2,1)S(1)}, bf16[128,512]{1,0:T(8,128)(2,1)S(1)}, u32[]{:S(2)}, u32[]{:S(2)}) %collective-permute-start.2) | collective-permute-done | bytes 131104 | tf_op jit(solution)/shard_map/ppermute | solution.py:32
  49.6 1.9 %collective-permute-start.3 = (bf16[256,1792]{1,0:T(8,128)(2,1)S(1)}, bf16[256,1792]{1,0:T(8,128)(2,1)S(1)}, u32[]{:S(2)}, u32[]{:S(2)}) collective-permute-start(bf16[256,1792]{1,0:T(8,128)(2,1)S(1)} %pad_maximum_fusion.2), channel_id=1, source_target_pairs={{0,384},{1,129},{128,256},{129,1},{256,128},{257,385},{384,0},{385... | collective-permute-start | bytes 2752520 | tf_op jit(solution)/shard_map/ppermute | solution.py:27
  51.6 15.0 %collective-permute-start.4 = (bf16[256,1408]{1,0:T(8,128)(2,1)S(1)}, bf16[256,1408]{1,0:T(8,128)(2,1)S(1)}, u32[]{:S(2)}, u32[]{:S(2)}) collective-permute-start(bf16[256,1408]{1,0:T(8,128)(2,1)S(1)} %pad_maximum_fusion.4), channel_id=1, source_target_pairs={{0,96},{1,33},{32,64},{33,1},{64,32},{65,97},{96,0},{97,65},{2,98}... | collective-permute-start | bytes 2162696 | tf_op jit(solution)/shard_map/ppermute | solution.py:27
  66.5 1.9 %collective-permute-start.5 = (bf16[128,512]{1,0:T(8,128)(2,1)S(1)}, bf16[128,512]{1,0:T(8,128)(2,1)S(1)}, u32[]{:S(2)}, u32[]{:S(2)}) collective-permute-start(bf16[128,512]{1,0:T(8,128)(2,1)S(1)} %collective-permute-done.2), channel_id=1, source_target_pairs={{0,6},{1,11},{2,12},{3,9},{4,10},{5,15},{6,0},{7,13},{8,14},{9,3},... | collective-permute-start | bytes 393224 | tf_op jit(solution)/shard_map/ppermute | solution.py:42
  68.5 8.2 %collective-permute-done.5 = bf16[128,512]{1,0:T(8,128)(2,1)S(1)} collective-permute-done((bf16[128,512]{1,0:T(8,128)(2,1)S(1)}, bf16[128,512]{1,0:T(8,128)(2,1)S(1)}, u32[]{:S(2)}, u32[]{:S(2)}) %collective-permute-start.5) | collective-permute-done | bytes 131104 | tf_op jit(solution)/shard_map/ppermute | solution.py:42
  76.7 1.9 %collective-permute-start.6 = (bf16[256,512]{1,0:T(8,128)(2,1)S(1)}, bf16[256,512]{1,0:T(8,128)(2,1)S(1)}, u32[]{:S(2)}, u32[]{:S(2)}) collective-permute-start(bf16[256,512]{1,0:T(8,128)(2,1)S(1)} %constant_dynamic-update-slice_fusion), channel_id=1, source_target_pairs={{0,14},{1,3},{2,4},{3,1},{4,2},{5,7},{6,8},{7,5},{8,6},{9,11},{10,... | collective-permute-start | bytes 786440 | tf_op jit(solution)/shard_map/ppermute | solution.py:42
  78.8 7.4 %collective-permute-done.6 = bf16[256,512]{1,0:T(8,128)(2,1)S(1)} collective-permute-done((bf16[256,512]{1,0:T(8,128)(2,1)S(1)}, bf16[256,512]{1,0:T(8,128)(2,1)S(1)}, u32[]{:S(2)}, u32[]{:S(2)}) %collective-permute-start.6) | collective-permute-done | bytes 262176 | tf_op jit(solution)/shard_map/ppermute | solution.py:42
  86.3 4.4 %collective-permute-start.7 = (bf16[384,1408]{1,0:T(8,128)(2,1)S(1)}, bf16[384,1408]{1,0:T(8,128)(2,1)S(1)}, u32[]{:S(2)}, u32[]{:S(2)}) collective-permute-start(bf16[384,1408]{1,0:T(8,128)(2,1)S(1)} %pad_maximum_fusion.1), channel_id=1, source_target_pairs={{0,128},{1,385},{128,0},{129,257},{256,384},{257,129},{384,256},{3... | collective-permute-start | bytes 3244040 | tf_op jit(solution)/shard_map/ppermute | solution.py:27
  90.8 1.9 %collective-permute-start.9 = (bf16[512,512]{1,0:T(8,128)(2,1)S(1)}, bf16[512,512]{1,0:T(8,128)(2,1)S(1)}, u32[]{:S(2)}, u32[]{:S(2)}) collective-permute-start(bf16[512,512]{1,0:T(8,128)(2,1)S(1)} %constant_dynamic-update-slice_fusion.2.mine2_ref), channel_id=1, source_target_pairs={{0,2},{1,15},{2,0},{3,5},{4,6},{5,3},{6,4},{7,9},{8,10},{9,7},{10,... | collective-permute-start | bytes 1572872 | tf_op jit(solution)/shard_map/ppermute | solution.py:42
  92.7 1.9 %collective-permute-start.8 = (bf16[512,384]{1,0:T(8,128)(2,1)S(1)}, bf16[512,384]{1,0:T(8,128)(2,1)S(1)}, u32[]{:S(2)}, u32[]{:S(2)}) collective-permute-start(bf16[512,384]{1,0:T(8,128)(2,1)S(1)} %pad_maximum_fusion.6), channel_id=1, source_target_pairs={{0,32},{1,97},{32,0},{33,65},{64,96},{65,33},{96,64},{97,1},{2,34}... | collective-permute-start | bytes 1179656 | tf_op jit(solution)/shard_map/ppermute | solution.py:27
  94.6 9.0 %collective-permute-done.8.y3 = bf16[512,384]{1,0:T(8,128)(2,1)S(1)} collective-permute-done((bf16[512,384]{1,0:T(8,128)(2,1)S(1)}, bf16[512,384]{1,0:T(8,128)(2,1)S(1)}, u32[]{:S(2)}, u32[]{:S(2)}) %collective-permute-start.8) | collective-permute-done | bytes 393248 | tf_op jit(solution)/shard_map/ppermute | solution.py:27
  106.0 7.2 %collective-permute-start.12 = (bf16[768,1408]{1,0:T(8,128)(2,1)}, bf16[768,1408]{1,0:T(8,128)(2,1)}, u32[]{:S(2)}, u32[]{:S(2)}) collective-permute-start(bf16[768,1408]{1,0:T(8,128)(2,1)} %pad_maximum_fusion), channel_id=1, source_target_pairs={{0,384},{1,129},{128,256},{129,1},{256,128},{257,385},{384,0},{385... | collective-permute-start | bytes 6488072 | tf_op jit(solution)/shard_map/ppermute | solution.py:27
  114.7 2.0 %pad_maximum_fusion.3 = bf16[1024,384]{1,0:T(8,128)(2,1)} fusion(bf16[512,384]{1,0:T(8,128)(2,1)S(1)} %collective-permute-done.8.y3, bf16[512,384]{1,0:T(8,128)(2,1)} %copy-done.7), kind=kLoop, calls=%fused_computation.5 | loop fusion | flops 1572864 | bytes 1572864 | tf_op jit(solution)/shard_map/concatenate | solution.py:239
  116.7 1.9 %collective-permute-start.13 = (bf16[1024,384]{1,0:T(8,128)(2,1)}, bf16[1024,384]{1,0:T(8,128)(2,1)}, u32[]{:S(2)}, u32[]{:S(2)}) collective-permute-start(bf16[1024,384]{1,0:T(8,128)(2,1)} %pad_maximum_fusion.3), channel_id=1, source_target_pairs={{0,96},{1,33},{32,64},{33,1},{64,32},{65,97},{96,0},{97,65},{2,98}... | collective-permute-start | bytes 2359304 | tf_op jit(solution)/shard_map/ppermute | solution.py:27
  118.7 1.9 %collective-permute-start.10 = (bf16[512,512]{1,0:T(8,128)(2,1)}, bf16[512,512]{1,0:T(8,128)(2,1)}, u32[]{:S(2)}, u32[]{:S(2)}) collective-permute-start(bf16[512,512]{1,0:T(8,128)(2,1)} %copy-done.2), channel_id=1, source_target_pairs={{0,1},{1,0},{2,3},{3,2},{4,5},{5,4},{6,7},{7,6},{8,9},{9,8},{10,11... | collective-permute-start | bytes 1572872 | tf_op jit(solution)/shard_map/ppermute | solution.py:243
  120.6 2.4 %collective-permute-start.11 = (bf16[512,512]{1,0:T(8,128)(2,1)}, bf16[512,512]{1,0:T(8,128)(2,1)}, u32[]{:S(2)}, u32[]{:S(2)}) collective-permute-start(bf16[512,512]{1,0:T(8,128)(2,1)} %copy-done.4), channel_id=1, source_target_pairs={{0,1},{1,0},{2,3},{3,2},{4,5},{5,4},{6,7},{7,6},{8,9},{9,8},{10,11... | collective-permute-start | bytes 1572872 | tf_op jit(solution)/shard_map/ppermute | solution.py:243
  126.9 4.7 %shard_map.28 = (bf16[512,2048]{1,0:T(8,128)(2,1)S(1)}, f32[512,128]{1,0:T(8,128)S(1)}) custom-call(s32[16]{0:T(128)S(1)} %compare_select_fusion.3.place_ref, bf16[512,512]{1,0:T(8,128)(2,1)S(1)} %copy-done.3, bf16[512,512]{1,0:T(8,128)(2,1)S(1)} %copy-done.5, bf16[512,512]{1,0:T(8,128)(2,1)} %collective-permute-done.10.other2_ref, ...), custom_call_target="tpu_custom_call" | custom-call | flops 131072 | bytes 65536 | tf_op jit(solution)/shard_map/pallas_call | solution.py:90
  131.6 4.2 %shard_map.29 = (f32[512,1792]{1,0:T(8,128)S(1)}, f32[8,1792]{1,0:T(8,128)S(1)}, f32[8,1792]{1,0:T(8,128)S(1)}) custom-call(bf16[512,2048]{1,0:T(8,128)(2,1)S(1)} %get-tuple-element.31.slab_ref, bf16[128,1792]{1,0:T(8,128)(2,1)S(1)} %slice.41.own, bf16[128,1792]{1,0:T(8,128)(2,1)S(1)} %collective-permute-done.x1, bf16[256,1792]{1,0:T(8,128)(2,1)S(1)} %copy-done.1, ...), custom_call_target="tpu_custom_call" | custom-call | flops 29360128 | bytes 57344 | tf_op jit(solution)/shard_map/pallas_call | solution.py:90
  135.8 4.6 %collective-permute-done.13.y4 = bf16[1024,384]{1,0:T(8,128)(2,1)} collective-permute-done((bf16[1024,384]{1,0:T(8,128)(2,1)}, bf16[1024,384]{1,0:T(8,128)(2,1)}, u32[]{:S(2)}, u32[]{:S(2)}) %collective-permute-start.13) | collective-permute-done | bytes 786464 | tf_op jit(solution)/shard_map/ppermute | solution.py:27
  140.5 6.0 %shard_map.30 = bf16[512,1792]{1,0:T(8,128)(2,1)} custom-call(bf16[512,2048]{1,0:T(8,128)(2,1)S(1)} %get-tuple-element.31.slab_ref, f32[512,128]{1,0:T(8,128)S(1)} %get-tuple-element.32.sums_ref, f32[512,1792]{1,0:T(8,128)S(1)} %get-tuple-element.36.acc_ref, f32[8,1792]{1,0:T(8,128)S(1)} %get-tuple-element.37.pivot_ref, ...), custom_call_target="tpu_custom_call" | custom-call | flops 29360128 | bytes 57344 | tf_op jit(solution)/shard_map/pallas_call | solution.py:90
  (56 shorter events, 10.5 us)
Async XLA Ops:
  31.1 18.5 %copy-start.6 = (bf16[128,2304]{1,0:T(8,128)(2,1)}, bf16[128,2304]{1,0:T(8,128)(2,1)S(1)}, u32[]{:S(2)}) copy-start(bf16[128,2304]{1,0:T(8,128)(2,1)S(1)} %all_to_all.14) | copy-start | bytes 1769476
  31.1 18.4 %collective-permute-start = (bf16[128,1792]{1,0:T(8,128)(2,1)S(1)}, bf16[128,1792]{1,0:T(8,128)(2,1)S(1)}, u32[]{:S(2)}, u32[]{:S(2)}) collective-permute-start(bf16[128,1792]{1,0:T(8,128)(2,1)S(1)} %slice.41.own), channel_id=1, source_target_pairs={{0,128},{1,385},{128,0},{129,257},{256,384},{257,129},{384,256},{3... | collective-permute-start | bytes 1376264 | tf_op jit(solution)/shard_map/ppermute | solution.py:27
  33.9 15.6 %collective-permute-start.1 = (bf16[128,1408]{1,0:T(8,128)(2,1)S(1)}, bf16[128,1408]{1,0:T(8,128)(2,1)S(1)}, u32[]{:S(2)}, u32[]{:S(2)}) collective-permute-start(bf16[128,1408]{1,0:T(8,128)(2,1)S(1)} %slice.42), channel_id=1, source_target_pairs={{0,32},{1,97},{32,0},{33,65},{64,96},{65,33},{96,64},{97,1},{2,34}... | collective-permute-start | bytes 1081352 | tf_op jit(solution)/shard_map/ppermute | solution.py:27
  38.4 11.1 %collective-permute-start.2 = (bf16[128,512]{1,0:T(8,128)(2,1)S(1)}, bf16[128,512]{1,0:T(8,128)(2,1)S(1)}, u32[]{:S(2)}, u32[]{:S(2)}) collective-permute-start(bf16[128,512]{1,0:T(8,128)(2,1)S(1)} %slice.43), channel_id=1, source_target_pairs={{0,0},{1,32},{2,64},{3,96},{4,128},{5,160},{6,192},{7,224},{8,256}... | collective-permute-start | bytes 393224 | tf_op jit(solution)/shard_map/ppermute | solution.py:32
  49.6 29.1 %collective-permute-start.3 = (bf16[256,1792]{1,0:T(8,128)(2,1)S(1)}, bf16[256,1792]{1,0:T(8,128)(2,1)S(1)}, u32[]{:S(2)}, u32[]{:S(2)}) collective-permute-start(bf16[256,1792]{1,0:T(8,128)(2,1)S(1)} %pad_maximum_fusion.2), channel_id=1, source_target_pairs={{0,384},{1,129},{128,256},{129,1},{256,128},{257,385},{384,0},{385... | collective-permute-start | bytes 2752520 | tf_op jit(solution)/shard_map/ppermute | solution.py:27
  51.5 27.2 %slice-start = ((bf16[128,2304]{1,0:T(8,128)(2,1)}), bf16[128,384]{1,0:T(8,128)(2,1)S(1)}, s32[]{:S(2)}) async-start(bf16[128,2304]{1,0:T(8,128)(2,1)} %copy-done.6), calls=%async_computation.1 | async-start | bytes 196608 | tf_op jit(solution)/shard_map/slice | solution.py:231
  51.6 34.6 %collective-permute-start.4 = (bf16[256,1408]{1,0:T(8,128)(2,1)S(1)}, bf16[256,1408]{1,0:T(8,128)(2,1)S(1)}, u32[]{:S(2)}, u32[]{:S(2)}) collective-permute-start(bf16[256,1408]{1,0:T(8,128)(2,1)S(1)} %pad_maximum_fusion.4), channel_id=1, source_target_pairs={{0,96},{1,33},{32,64},{33,1},{64,32},{65,97},{96,0},{97,65},{2,98}... | collective-permute-start | bytes 2162696 | tf_op jit(solution)/shard_map/ppermute | solution.py:27
  66.5 10.2 %collective-permute-start.5 = (bf16[128,512]{1,0:T(8,128)(2,1)S(1)}, bf16[128,512]{1,0:T(8,128)(2,1)S(1)}, u32[]{:S(2)}, u32[]{:S(2)}) collective-permute-start(bf16[128,512]{1,0:T(8,128)(2,1)S(1)} %collective-permute-done.2), channel_id=1, source_target_pairs={{0,6},{1,11},{2,12},{3,9},{4,10},{5,15},{6,0},{7,13},{8,14},{9,3},... | collective-permute-start | bytes 393224 | tf_op jit(solution)/shard_map/ppermute | solution.py:42
  76.7 9.5 %collective-permute-start.6 = (bf16[256,512]{1,0:T(8,128)(2,1)S(1)}, bf16[256,512]{1,0:T(8,128)(2,1)S(1)}, u32[]{:S(2)}, u32[]{:S(2)}) collective-permute-start(bf16[256,512]{1,0:T(8,128)(2,1)S(1)} %constant_dynamic-update-slice_fusion), channel_id=1, source_target_pairs={{0,14},{1,3},{2,4},{3,1},{4,2},{5,7},{6,8},{7,5},{8,6},{9,11},{10,... | collective-permute-start | bytes 786440 | tf_op jit(solution)/shard_map/ppermute | solution.py:42
  78.7 7.5 %copy-start = (bf16[256,1792]{1,0:T(8,128)(2,1)}, bf16[256,1792]{1,0:T(8,128)(2,1)S(1)}, u32[]{:S(2)}) copy-start(bf16[256,1792]{1,0:T(8,128)(2,1)S(1)} %collective-permute-done.3.x2) | copy-start | bytes 2752516
  78.8 24.9 %copy-start.7 = (bf16[512,384]{1,0:T(8,128)(2,1)}, bf16[512,384]{1,0:T(8,128)(2,1)S(1)}, u32[]{:S(2)}) copy-start(bf16[512,384]{1,0:T(8,128)(2,1)S(1)} %pad_maximum_fusion.6) | copy-start | bytes 1179652
  86.3 18.2 %collective-permute-start.7 = (bf16[384,1408]{1,0:T(8,128)(2,1)S(1)}, bf16[384,1408]{1,0:T(8,128)(2,1)S(1)}, u32[]{:S(2)}, u32[]{:S(2)}) collective-permute-start(bf16[384,1408]{1,0:T(8,128)(2,1)S(1)} %pad_maximum_fusion.1), channel_id=1, source_target_pairs={{0,128},{1,385},{128,0},{129,257},{256,384},{257,129},{384,256},{3... | collective-permute-start | bytes 3244040 | tf_op jit(solution)/shard_map/ppermute | solution.py:27
  90.8 12.9 %copy-start.2 = (bf16[512,512]{1,0:T(8,128)(2,1)}, bf16[512,512]{1,0:T(8,128)(2,1)S(1)}, u32[]{:S(2)}) copy-start(bf16[512,512]{1,0:T(8,128)(2,1)S(1)} %constant_dynamic-update-slice_fusion.2.mine2_ref) | copy-start | bytes 1572868
  90.8 12.9 %collective-permute-start.9 = (bf16[512,512]{1,0:T(8,128)(2,1)S(1)}, bf16[512,512]{1,0:T(8,128)(2,1)S(1)}, u32[]{:S(2)}, u32[]{:S(2)}) collective-permute-start(bf16[512,512]{1,0:T(8,128)(2,1)S(1)} %constant_dynamic-update-slice_fusion.2.mine2_ref), channel_id=1, source_target_pairs={{0,2},{1,15},{2,0},{3,5},{4,6},{5,3},{6,4},{7,9},{8,10},{9,7},{10,... | collective-permute-start | bytes 1572872 | tf_op jit(solution)/shard_map/ppermute | solution.py:42
  92.7 10.9 %collective-permute-start.8 = (bf16[512,384]{1,0:T(8,128)(2,1)S(1)}, bf16[512,384]{1,0:T(8,128)(2,1)S(1)}, u32[]{:S(2)}, u32[]{:S(2)}) collective-permute-start(bf16[512,384]{1,0:T(8,128)(2,1)S(1)} %pad_maximum_fusion.6), channel_id=1, source_target_pairs={{0,32},{1,97},{32,0},{33,65},{64,96},{65,33},{96,64},{97,1},{2,34}... | collective-permute-start | bytes 1179656 | tf_op jit(solution)/shard_map/ppermute | solution.py:27
  103.7 0.8 copy-start.4
  106.0 34.5 %collective-permute-start.12 = (bf16[768,1408]{1,0:T(8,128)(2,1)}, bf16[768,1408]{1,0:T(8,128)(2,1)}, u32[]{:S(2)}, u32[]{:S(2)}) collective-permute-start(bf16[768,1408]{1,0:T(8,128)(2,1)} %pad_maximum_fusion), channel_id=1, source_target_pairs={{0,384},{1,129},{128,256},{129,1},{256,128},{257,385},{384,0},{385... | collective-permute-start | bytes 6488072 | tf_op jit(solution)/shard_map/ppermute | solution.py:27
  116.7 23.7 %collective-permute-start.13 = (bf16[1024,384]{1,0:T(8,128)(2,1)}, bf16[1024,384]{1,0:T(8,128)(2,1)}, u32[]{:S(2)}, u32[]{:S(2)}) collective-permute-start(bf16[1024,384]{1,0:T(8,128)(2,1)} %pad_maximum_fusion.3), channel_id=1, source_target_pairs={{0,96},{1,33},{32,64},{33,1},{64,32},{65,97},{96,0},{97,65},{2,98}... | collective-permute-start | bytes 2359304 | tf_op jit(solution)/shard_map/ppermute | solution.py:27
  118.7 5.8 %collective-permute-start.10 = (bf16[512,512]{1,0:T(8,128)(2,1)}, bf16[512,512]{1,0:T(8,128)(2,1)}, u32[]{:S(2)}, u32[]{:S(2)}) collective-permute-start(bf16[512,512]{1,0:T(8,128)(2,1)} %copy-done.2), channel_id=1, source_target_pairs={{0,1},{1,0},{2,3},{3,2},{4,5},{5,4},{6,7},{7,6},{8,9},{9,8},{10,11... | collective-permute-start | bytes 1572872 | tf_op jit(solution)/shard_map/ppermute | solution.py:243
  120.6 4.3 %collective-permute-start.11 = (bf16[512,512]{1,0:T(8,128)(2,1)}, bf16[512,512]{1,0:T(8,128)(2,1)}, u32[]{:S(2)}, u32[]{:S(2)}) collective-permute-start(bf16[512,512]{1,0:T(8,128)(2,1)} %copy-done.4), channel_id=1, source_target_pairs={{0,1},{1,0},{2,3},{3,2},{4,5},{5,4},{6,7},{7,6},{8,9},{9,8},{10,11... | collective-permute-start | bytes 1572872 | tf_op jit(solution)/shard_map/ppermute | solution.py:243
  124.5 7.2 %copy-start.1 = (bf16[256,1792]{1,0:T(8,128)(2,1)S(1)}, bf16[256,1792]{1,0:T(8,128)(2,1)}, u32[]{:S(2)}) copy-start(bf16[256,1792]{1,0:T(8,128)(2,1)} %copy-done) | copy-start | bytes 2752516
  124.9 1.0 copy-start.3
  125.9 1.0 copy-start.5

commit v5 on v4

--- a/solution.py
+++ b/solution.py
@@ -14,8 +14,9 @@
 TILE = 256
 ALL = ("x", "yh", "yl", "z", "c")
 
-SLOTS = [(0, 0), (1, 0), (2, 0), (3, 0), (0, 1), (1, 1), (0, 2), (1, 2), (0, 3), (1, 3)]
-SLOTS += [(2, 1), (3, 1), (2, 2), (3, 2), (2, 3), (3, 3)]
+SLOTS = [(0, 0), (1, 0), (2, 0), (3, 0), (0, 1), (1, 1), (2, 1), (0, 2), (1, 2), (2, 2)]
+SLOTS += [(0, 3), (1, 3), (2, 3), (3, 3), (3, 1), (3, 2)]
+N_EARLY = 13
 
 
 def exchange(values, axis, step):
@@ -144,16 +145,16 @@
     return acc
 
 
-def early_kernel(slab_ref, own, x1, x2, y1, y2, x3, y3, acc_ref, pivot_ref, square_ref, *scratch):
-    width = own.shape[1]
+def early_kernel(slab_ref, x0, x1, x2, x3, y0, y1, y2, r0, r1, r2, acc_ref, pivot_ref, square_ref, *scratch):
+    width = x0.shape[1]
 
     def tiles(pieces, offset, columns, spans):
         def body(start, size, shifted):
             lanes = at(start + offset, size)
 
             def load(piece):
-                ref, part, whole = piece
-                return tile_at(ref, part, lanes if whole else at(start, size))
+                ref, part = piece
+                return tile_at(ref, part, at(start, size))
 
             total = jnp.zeros((8, size), jnp.float32)
             for piece in pieces:
@@ -170,15 +171,10 @@
 
         over_tiles(columns, scratch, body)
 
-    near = [(own, 0, True), (x1, 0, True), (x2, 0, True), (x2, 1, True)]
-    tiles(
-        near
-        + [(y1, 0, False), (x3, 0, False), (y2, 0, False), (x3, 1, False), (y2, 1, False), (x3, 2, False)],
-        0,
-        FIRST,
-        [(0, 1280)],
-    )
-    tiles(near + [(y3, i, False) for i in range(4)], FIRST, width - FIRST, [(0, 768), (1280, 256)])
+    first = [(x0, 0), (x1, 0), (x2, 0), (x3, 0)] + [((y0, y1, y2)[i], j - 1) for i, j in SLOTS[4:N_EARLY]]
+    tiles(first, 0, FIRST, [(0, N_EARLY * PIECE)])
+    others = [((r0, r1, r2)[j], i) for i, j in SLOTS[:10] + SLOTS[14:]]
+    tiles(others, FIRST, width - FIRST, [(0, 10 * PIECE), (14 * PIECE, 2 * PIECE)])
 
 
 def late_kernel(slab_ref, sums_ref, acc_ref, pivot_ref, square_ref, x4, y4, out_ref, *scratch):
@@ -203,8 +199,8 @@
 
         over_tiles(columns, scratch, body)
 
-    tiles([(x4, i) for i in (0, 3, 1, 4, 2, 5)], 0, FIRST, [(1280, 768)])
-    tiles([(y4, i) for i in (0, 1, 4, 5, 2, 3, 6, 7)], FIRST, width - FIRST, [(768, 512), (1536, 512)])
+    tiles([(x4, j - 1) for _, j in SLOTS[N_EARLY:]], 0, FIRST, [(N_EARLY * PIECE, 3 * PIECE)])
+    tiles([(y4, i) for i, _ in SLOTS[10:14]], FIRST, width - FIRST, [(10 * PIECE, 4 * PIECE)])
 
 
 def per_device(activations):
@@ -220,25 +216,23 @@
         with_slab.reshape(tok, n_col * (width + ROWS_DEV)), ("yl", "z", "c"), split_axis=1, concat_axis=0, tiled=True
     )
     own, own_first, slab0 = block[:, :width], block[:, :FIRST], block[:, width:]
-    y1 = exchange(own_first, "yh", 0)
-    x1 = exchange(own, "x", 0)
+    x1, x2 = exchange(own, "x", 0), exchange(own, "x", 1)
+    y1, y2 = exchange(own_first, "yh", 0), exchange(own_first, "yh", 1)
     slab0 = swap_places(slab0)
-    x1, y1, slab0 = together((x1, y1, slab0))
-    y2 = exchange(jnp.concatenate([own_first, y1], axis=0), "yh", 1)
-    x2 = exchange(jnp.concatenate([own, x1], axis=0), "x", 1)
+    x1, x2, y1, y2, slab0 = together((x1, x2, y1, y2, slab0))
+    x3 = exchange(x1, "x", 1)
+    y3 = exchange(y1, "yh", 1)
     slab1 = jnp.concatenate([slab0, z_permute(slab0, 0)], axis=0)
-    slab2 = z_permute(slab1, 1)
-    rest = jnp.concatenate([own[:, FIRST:], x1[:, FIRST:], x2[:, FIRST:]], axis=0)
-    x2, y2, rest, slab1, slab2 = together((x2, y2, rest, slab1, slab2))
-    three = jnp.concatenate([y1, y2], axis=0)
-    y3 = exchange(rest, "yh", 0)
-    x3 = exchange(three, "x", 0)
-    slab2 = jnp.concatenate([slab1, slab2], axis=0)
+    x3, y3, slab1 = together((x3, y3, slab1))
+    three = jnp.concatenate([y1, y2, y3], axis=0)
+    rest = jnp.concatenate([x[:, FIRST:] for x in (own, x1, x2, x3)], axis=0)
+    three1, three2 = exchange(three, "x", 0), exchange(three, "x", 1)
+    rest1, rest2 = exchange(rest, "yh", 0), exchange(rest, "yh", 1)
+    slab2 = jnp.concatenate([slab1, z_permute(slab1, 1)], axis=0)
     slab3 = z_permute(slab2, 2)
-    x3, y3, slab2, slab3 = together((x3, y3, slab2, slab3))
-    rest = jnp.concatenate([rest, y3], axis=0)
-    y4 = exchange(rest, "yh", 1)
-    x4 = exchange(jnp.concatenate([three, x3], axis=0), "x", 1)
+    three1, three2, rest1, rest2, slab2, slab3 = together((three1, three2, rest1, rest2, slab2, slab3))
+    three3 = exchange(three1, "x", 1)
+    rest3 = exchange(rest1, "yh", 1)
 
     quarters = [slab2, slab3] + [lax.ppermute(part, "c", [(0, 1), (1, 0)]) for part in (slab2, slab3)]
 
@@ -257,20 +251,20 @@
     acc, pivot, square = call(
         early_kernel,
         [jax.ShapeDtypeStruct((ROWS_DEV, width), jnp.float32), wide, wide],
-        [VMEM] * 8,
-        [pltpu.VMEM((1280, TILE), jnp.bfloat16)] * 2,
+        [VMEM] * 11,
+        [pltpu.VMEM((N_EARLY * PIECE, TILE), jnp.bfloat16)] * 2,
         TOKENS * ROWS_DEV * width,
         4 * ROWS_DEV * width,
-        (slab, own, x1, x2, y1, y2, x3, y3),
+        (slab, own, x1, x2, x3, three, three1, three2, rest, rest1, rest2),
     )
     (out,) = call(
         late_kernel,
         [jax.ShapeDtypeStruct((ROWS_DEV, width), jnp.bfloat16)],
         [VMEM] * 7,
-        [pltpu.VMEM((1024, TILE), jnp.bfloat16)] * 2,
+        [pltpu.VMEM((4 * PIECE, TILE), jnp.bfloat16)] * 2,
         TOKENS * ROWS_DEV * width,
         4 * ROWS_DEV * width,
-        (slab, sums, acc, pivot, square, x4, y4),
+        (slab, sums, acc, pivot, square, three3, rest3),
     )
     return out
 

time: 147 us -> 161 us (1.095)
  starting transfers between devices: 54.5 us -> 72.1 us
  other arithmetic: 5.78 us -> 2.07 us
    ppermute x3, starting transfers between devices: 5.76 us -> 14.8 us  [z_permute(): return lax.ppermute(values, ('z', 'c'), perm)]
    ppermute x8 -> x12, starting transfers between devices: 39.5 us -> 47.1 us  [exchange(): return lax.ppermute(values, (axis, 'c'), perm)]
    ppermute x3, waiting for transfers between devices: 15.6 us -> 8.7 us  [z_permute(): return lax.ppermute(values, ('z', 'c'), perm)]
    concatenate x6 -> x2, other arithmetic: 3.77 us -> 0.06 us  [the longest x1 0.04 us: per_device(): rest = jnp.concatenate([x[:, FIRST:] for x in (own, x1, x2, x3)], axis=0)]
    ppermute x8 -> x12, waiting for transfers between devices: 13.7 us -> 17.4 us  [exchange(): return lax.ppermute(values, (axis, 'c'), perm)]
    ppermute x1, waiting for transfers between devices: 6.18 us -> 8.63 us  [swap_places(): return lax.ppermute(values, ALL, perm)]
  transfers between devices with their start and end apart: 14 -> 18, of which waited for: 6 -> 6; matrix products, arithmetic and copies ran while one was open for 4% -> 2% of each run, Pallas kernels for 6% -> 7%
where the time goes in v5:
time: 161 us; the launch traced here: 160 us
  starting transfers between devices  72.1 us (45%)
  waiting for transfers between devices  34.7 us (22%)
  blocking collectives  28.7 us (18%)
  Pallas kernels  16.1 us (10%)
  local copies, waits for them, and re-layouts  5.56 us (3%)
  other arithmetic  2.07 us (1%)
    ppermute x12, starting transfers between devices, exchange(): return lax.ppermute(values, (axis, 'c'), perm)  47.1 us
    all_to_all x1, blocking collectives, per_device(): lax.all_to_all(with_slab.reshape(tok, n_col * (width + ROWS_DEV)), ('yl',...  28.7 us
    ppermute x12, waiting for transfers between devices, exchange(): return lax.ppermute(values, (axis, 'c'), perm)  17.4 us
    pallas_call x3, Pallas kernels, call(): pl.pallas_call(kernel, out_shape=outs, in_specs=in_specs, out_specs=[pl.B...  16.1 us
    ppermute x3, starting transfers between devices, z_permute(): return lax.ppermute(values, ('z', 'c'), perm)  14.8 us
    ppermute x3, waiting for transfers between devices, z_permute(): return lax.ppermute(values, ('z', 'c'), perm)  8.7 us
    ppermute x1, waiting for transfers between devices, swap_places(): return lax.ppermute(values, ALL, perm)  8.63 us
    ppermute x1, starting transfers between devices, swap_places(): return lax.ppermute(values, ALL, perm)  5.85 us
  transfers between devices with their start and end apart: 18, of which 6 were waited for; matrix products, arithmetic and copies ran while one was open for 2% of the time, Pallas kernels for 7%

profile of v5, /device:TPU:6, one launch (start us, length us, event | category | flops | bytes accessed | tf_op | source)
XLA Modules:
  0.0 159.8 jit_solution(1056345447599963248)
XLA Ops:
  2.2 28.7 %all_to_all.16 = bf16[4,32,2304]{2,0,1:T(4,128)(2,1)S(1)} all-to-all(bf16[4,32,2304]{2,0,1:T(4,128)(2,1)S(1)} %pad_maximum_fusion), channel_id=1, replica_groups=mesh['x'=4,'yh'=4,'yl'=2,'z'=8,'c'=2] {'yl','z','c'}, dimensions={1} | all-to-all | bytes 1179648 | tf_op jit(solution)/shard_map/all_to_all | solution.py:215
  31.1 2.7 %collective-permute-start = (bf16[128,1792]{1,0:T(8,128)(2,1)S(1)}, bf16[128,1792]{1,0:T(8,128)(2,1)S(1)}, u32[]{:S(2)}, u32[]{:S(2)}) collective-permute-start(bf16[128,1792]{1,0:T(8,128)(2,1)S(1)} %slice.45.x0), channel_id=1, source_target_pairs={{0,128},{1,385},{128,0},{129,257},{256,384},{257,129},{384,256},{3... | collective-permute-start | bytes 1376264 | tf_op jit(solution)/shard_map/ppermute | solution.py:28
  33.9 3.0 %collective-permute-start.1 = (bf16[128,1792]{1,0:T(8,128)(2,1)S(1)}, bf16[128,1792]{1,0:T(8,128)(2,1)S(1)}, u32[]{:S(2)}, u32[]{:S(2)}) collective-permute-start(bf16[128,1792]{1,0:T(8,128)(2,1)S(1)} %slice.45.x0), channel_id=1, source_target_pairs={{0,384},{1,129},{128,256},{129,1},{256,128},{257,385},{384,0},{385... | collective-permute-start | bytes 1376264 | tf_op jit(solution)/shard_map/ppermute | solution.py:28
  37.0 4.5 %collective-permute-start.2 = (bf16[128,1408]{1,0:T(8,128)(2,1)S(1)}, bf16[128,1408]{1,0:T(8,128)(2,1)S(1)}, u32[]{:S(2)}, u32[]{:S(2)}) collective-permute-start(bf16[128,1408]{1,0:T(8,128)(2,1)S(1)} %slice.46), channel_id=1, source_target_pairs={{0,32},{1,97},{32,0},{33,65},{64,96},{65,33},{96,64},{97,1},{2,34}... | collective-permute-start | bytes 1081352 | tf_op jit(solution)/shard_map/ppermute | solution.py:28
  41.5 4.8 %collective-permute-start.3 = (bf16[128,1408]{1,0:T(8,128)(2,1)S(1)}, bf16[128,1408]{1,0:T(8,128)(2,1)S(1)}, u32[]{:S(2)}, u32[]{:S(2)}) collective-permute-start(bf16[128,1408]{1,0:T(8,128)(2,1)S(1)} %slice.46), channel_id=1, source_target_pairs={{0,96},{1,33},{32,64},{33,1},{64,32},{65,97},{96,0},{97,65},{2,98}... | collective-permute-start | bytes 1081352 | tf_op jit(solution)/shard_map/ppermute | solution.py:28
  46.3 5.8 %collective-permute-start.4 = (bf16[128,512]{1,0:T(8,128)(2,1)S(1)}, bf16[128,512]{1,0:T(8,128)(2,1)S(1)}, u32[]{:S(2)}, u32[]{:S(2)}) collective-permute-start(bf16[128,512]{1,0:T(8,128)(2,1)S(1)} %slice.47), channel_id=1, source_target_pairs={{0,0},{1,32},{2,64},{3,96},{4,128},{5,160},{6,192},{7,224},{8,256}... | collective-permute-start | bytes 393224 | tf_op jit(solution)/shard_map/ppermute | solution.py:33
  52.2 8.6 %collective-permute-done.4 = bf16[128,512]{1,0:T(8,128)(2,1)S(1)} collective-permute-done((bf16[128,512]{1,0:T(8,128)(2,1)S(1)}, bf16[128,512]{1,0:T(8,128)(2,1)S(1)}, u32[]{:S(2)}, u32[]{:S(2)}) %collective-permute-start.4) | collective-permute-done | bytes 131104 | tf_op jit(solution)/shard_map/ppermute | solution.py:33
  63.3 4.0 %collective-permute-start.5 = (bf16[128,1792]{1,0:T(8,128)(2,1)S(1)}, bf16[128,1792]{1,0:T(8,128)(2,1)S(1)}, u32[]{:S(2)}, u32[]{:S(2)}) collective-permute-start(bf16[128,1792]{1,0:T(8,128)(2,1)S(1)} %collective-permute-done.x1), channel_id=1, source_target_pairs={{0,384},{1,129},{128,256},{129,1},{256,128},{257,385},{384,0},{385... | collective-permute-start | bytes 1376264 | tf_op jit(solution)/shard_map/ppermute | solution.py:28
  67.3 2.9 %collective-permute-start.6 = (bf16[128,1408]{1,0:T(8,128)(2,1)S(1)}, bf16[128,1408]{1,0:T(8,128)(2,1)S(1)}, u32[]{:S(2)}, u32[]{:S(2)}) collective-permute-start(bf16[128,1408]{1,0:T(8,128)(2,1)S(1)} %collective-permute-done.2), channel_id=1, source_target_pairs={{0,96},{1,33},{32,64},{33,1},{64,32},{65,97},{96,0},{97,65},{2,98}... | collective-permute-start | bytes 1081352 | tf_op jit(solution)/shard_map/ppermute | solution.py:28
  70.2 7.9 %collective-permute-start.7 = (bf16[128,512]{1,0:T(8,128)(2,1)S(1)}, bf16[128,512]{1,0:T(8,128)(2,1)S(1)}, u32[]{:S(2)}, u32[]{:S(2)}) collective-permute-start(bf16[128,512]{1,0:T(8,128)(2,1)S(1)} %collective-permute-done.4), channel_id=1, source_target_pairs={{0,6},{1,11},{2,12},{3,9},{4,10},{5,15},{6,0},{7,13},{8,14},{9,3},... | collective-permute-start | bytes 393224 | tf_op jit(solution)/shard_map/ppermute | solution.py:43
  78.1 3.0 %collective-permute-done.7 = bf16[128,512]{1,0:T(8,128)(2,1)S(1)} collective-permute-done((bf16[128,512]{1,0:T(8,128)(2,1)S(1)}, bf16[128,512]{1,0:T(8,128)(2,1)S(1)}, u32[]{:S(2)}, u32[]{:S(2)}) %collective-permute-start.7) | collective-permute-done | bytes 131104 | tf_op jit(solution)/shard_map/ppermute | solution.py:43
  81.2 4.7 %collective-permute-start.8 = (bf16[384,1408]{1,0:T(8,128)(2,1)S(1)}, bf16[384,1408]{1,0:T(8,128)(2,1)S(1)}, u32[]{:S(2)}, u32[]{:S(2)}) collective-permute-start(bf16[384,1408]{1,0:T(8,128)(2,1)S(1)} %constant_dynamic-update-slice_fusion.y0), channel_id=1, source_target_pairs={{0,128},{1,385},{128,0},{129,257},{256,384},{257,129},{384,256},{3... | collective-permute-start | bytes 3244040 | tf_op jit(solution)/shard_map/ppermute | solution.py:28
  85.9 5.0 %collective-permute-start.9 = (bf16[384,1408]{1,0:T(8,128)(2,1)S(1)}, bf16[384,1408]{1,0:T(8,128)(2,1)}, u32[]{:S(2)}, u32[]{:S(2)}) collective-permute-start(bf16[384,1408]{1,0:T(8,128)(2,1)S(1)} %constant_dynamic-update-slice_fusion.y0), channel_id=1, source_target_pairs={{0,384},{1,129},{128,256},{129,1},{256,128},{257,385},{384,0},{385... | collective-permute-start | bytes 3244040 | tf_op jit(solution)/shard_map/ppermute | solution.py:28
  90.9 3.7 %collective-permute-start.12 = (bf16[256,512]{1,0:T(8,128)(2,1)S(1)}, bf16[256,512]{1,0:T(8,128)(2,1)S(1)}, u32[]{:S(2)}, u32[]{:S(2)}) collective-permute-start(bf16[256,512]{1,0:T(8,128)(2,1)S(1)} %pad_maximum_fusion.2), channel_id=1, source_target_pairs={{0,14},{1,3},{2,4},{3,1},{4,2},{5,7},{6,8},{7,5},{8,6},{9,11},{10,... | collective-permute-start | bytes 786440 | tf_op jit(solution)/shard_map/ppermute | solution.py:43
  94.7 5.7 %collective-permute-done.12 = bf16[256,512]{1,0:T(8,128)(2,1)S(1)} collective-permute-done((bf16[256,512]{1,0:T(8,128)(2,1)S(1)}, bf16[256,512]{1,0:T(8,128)(2,1)S(1)}, u32[]{:S(2)}, u32[]{:S(2)}) %collective-permute-start.12) | collective-permute-done | bytes 262176 | tf_op jit(solution)/shard_map/ppermute | solution.py:43
  100.4 3.2 %collective-permute-start.13 = (bf16[512,512]{1,0:T(8,128)(2,1)S(1)}, bf16[512,512]{1,0:T(8,128)(2,1)}, u32[]{:S(2)}, u32[]{:S(2)}) collective-permute-start(bf16[512,512]{1,0:T(8,128)(2,1)S(1)} %constant_dynamic-update-slice_fusion.3.mine2_ref), channel_id=1, source_target_pairs={{0,2},{1,15},{2,0},{3,5},{4,6},{5,3},{6,4},{7,9},{8,10},{9,7},{10,... | collective-permute-start | bytes 1572872 | tf_op jit(solution)/shard_map/ppermute | solution.py:43
  103.8 4.3 %collective-permute-start.10 = (bf16[512,384]{1,0:T(8,128)(2,1)S(1)}, bf16[512,384]{1,0:T(8,128)(2,1)}, u32[]{:S(2)}, u32[]{:S(2)}) collective-permute-start(bf16[512,384]{1,0:T(8,128)(2,1)S(1)} %pad_maximum_fusion.1.r0), channel_id=1, source_target_pairs={{0,32},{1,97},{32,0},{33,65},{64,96},{65,33},{96,64},{97,1},{2,34}... | collective-permute-start | bytes 1179656 | tf_op jit(solution)/shard_map/ppermute | solution.py:28
  108.1 3.2 %collective-permute-start.11 = (bf16[512,384]{1,0:T(8,128)(2,1)S(1)}, bf16[512,384]{1,0:T(8,128)(2,1)}, u32[]{:S(2)}, u32[]{:S(2)}) collective-permute-start(bf16[512,384]{1,0:T(8,128)(2,1)S(1)} %pad_maximum_fusion.1.r0), channel_id=1, source_target_pairs={{0,96},{1,33},{32,64},{33,1},{64,32},{65,97},{96,0},{97,65},{2,98}... | collective-permute-start | bytes 1179656 | tf_op jit(solution)/shard_map/ppermute | solution.py:28
  111.3 12.5 %collective-permute-done.10.r1 = bf16[512,384]{1,0:T(8,128)(2,1)} collective-permute-done((bf16[512,384]{1,0:T(8,128)(2,1)S(1)}, bf16[512,384]{1,0:T(8,128)(2,1)}, u32[]{:S(2)}, u32[]{:S(2)}) %collective-permute-start.10) | collective-permute-done | bytes 393248 | tf_op jit(solution)/shard_map/ppermute | solution.py:28
  127.2 3.2 %collective-permute-start.16 = (bf16[384,1408]{1,0:T(8,128)(2,1)}, bf16[384,1408]{1,0:T(8,128)(2,1)S(1)}, u32[]{:S(2)}, u32[]{:S(2)}) collective-permute-start(bf16[384,1408]{1,0:T(8,128)(2,1)} %copy-done), channel_id=1, source_target_pairs={{0,384},{1,129},{128,256},{129,1},{256,128},{257,385},{384,0},{385... | collective-permute-start | bytes 3244040 | tf_op jit(solution)/shard_map/ppermute | solution.py:28
  136.3 4.8 %collective-permute-start.17 = (bf16[512,384]{1,0:T(8,128)(2,1)}, bf16[512,384]{1,0:T(8,128)(2,1)}, u32[]{:S(2)}, u32[]{:S(2)}) collective-permute-start(bf16[512,384]{1,0:T(8,128)(2,1)} %collective-permute-done.10.r1), channel_id=1, source_target_pairs={{0,96},{1,33},{32,64},{33,1},{64,32},{65,97},{96,0},{97,65},{2,98}... | collective-permute-start | bytes 1179656 | tf_op jit(solution)/shard_map/ppermute | solution.py:28
  142.6 5.0 %shard_map.28 = (bf16[512,2048]{1,0:T(8,128)(2,1)S(1)}, f32[512,128]{1,0:T(8,128)S(1)}) custom-call(s32[16]{0:T(128)S(1)} %compare_select_fusion.3.place_ref, bf16[512,512]{1,0:T(8,128)(2,1)S(1)} %constant_dynamic-update-slice_fusion.3.mine2_ref, bf16[512,512]{1,0:T(8,128)(2,1)} %collective-permute-done.13.mine3_ref, ...), custom_call_target="tpu_custom_call" | custom-call | flops 131072 | bytes 65536 | tf_op jit(solution)/shard_map/pallas_call | solution.py:91
  148.6 6.8 %shard_map.29 = (f32[512,1792]{1,0:T(8,128)S(1)}, f32[8,1792]{1,0:T(8,128)S(1)}, f32[8,1792]{1,0:T(8,128)S(1)}) custom-call(bf16[512,2048]{1,0:T(8,128)(2,1)S(1)} %get-tuple-element.34.slab_ref, bf16[128,1792]{1,0:T(8,128)(2,1)S(1)} %slice.45.x0, bf16[128,1792]{1,0:T(8,128)(2,1)S(1)} %copy-done.3, bf16[128,1792]{1,0:T(8,128)(2,1)S(1)} %copy-done.5, ...), custom_call_target="tpu_custom_call" | custom-call | flops 29360128 | bytes 57344 | tf_op jit(solution)/shard_map/pallas_call | solution.py:91
  155.5 4.3 %shard_map.30 = bf16[512,1792]{1,0:T(8,128)(2,1)} custom-call(bf16[512,2048]{1,0:T(8,128)(2,1)S(1)} %get-tuple-element.34.slab_ref, f32[512,128]{1,0:T(8,128)S(1)} %get-tuple-element.35.sums_ref, f32[512,1792]{1,0:T(8,128)S(1)} %get-tuple-element.40.acc_ref, f32[8,1792]{1,0:T(8,128)S(1)} %get-tuple-element.41.pivot_ref, ...), custom_call_target="tpu_custom_call" | custom-call | flops 29360128 | bytes 57344 | tf_op jit(solution)/shard_map/pallas_call | solution.py:91
  (64 shorter events, 16.8 us)
Async XLA Ops:
  31.1 36.2 %copy-start.8 = (bf16[128,2304]{1,0:T(8,128)(2,1)}, bf16[128,2304]{1,0:T(8,128)(2,1)S(1)}, u32[]{:S(2)}) copy-start(bf16[128,2304]{1,0:T(8,128)(2,1)S(1)} %all_to_all.14) | copy-start | bytes 1769476
  31.1 32.1 %collective-permute-start = (bf16[128,1792]{1,0:T(8,128)(2,1)S(1)}, bf16[128,1792]{1,0:T(8,128)(2,1)S(1)}, u32[]{:S(2)}, u32[]{:S(2)}) collective-permute-start(bf16[128,1792]{1,0:T(8,128)(2,1)S(1)} %slice.45.x0), channel_id=1, source_target_pairs={{0,128},{1,385},{128,0},{129,257},{256,384},{257,129},{384,256},{3... | collective-permute-start | bytes 1376264 | tf_op jit(solution)/shard_map/ppermute | solution.py:28
  33.9 29.4 %collective-permute-start.1 = (bf16[128,1792]{1,0:T(8,128)(2,1)S(1)}, bf16[128,1792]{1,0:T(8,128)(2,1)S(1)}, u32[]{:S(2)}, u32[]{:S(2)}) collective-permute-start(bf16[128,1792]{1,0:T(8,128)(2,1)S(1)} %slice.45.x0), channel_id=1, source_target_pairs={{0,384},{1,129},{128,256},{129,1},{256,128},{257,385},{384,0},{385... | collective-permute-start | bytes 1376264 | tf_op jit(solution)/shard_map/ppermute | solution.py:28
  37.0 23.8 %collective-permute-start.2 = (bf16[128,1408]{1,0:T(8,128)(2,1)S(1)}, bf16[128,1408]{1,0:T(8,128)(2,1)S(1)}, u32[]{:S(2)}, u32[]{:S(2)}) collective-permute-start(bf16[128,1408]{1,0:T(8,128)(2,1)S(1)} %slice.46), channel_id=1, source_target_pairs={{0,32},{1,97},{32,0},{33,65},{64,96},{65,33},{96,64},{97,1},{2,34}... | collective-permute-start | bytes 1081352 | tf_op jit(solution)/shard_map/ppermute | solution.py:28
  41.5 21.8 %collective-permute-start.3 = (bf16[128,1408]{1,0:T(8,128)(2,1)S(1)}, bf16[128,1408]{1,0:T(8,128)(2,1)S(1)}, u32[]{:S(2)}, u32[]{:S(2)}) collective-permute-start(bf16[128,1408]{1,0:T(8,128)(2,1)S(1)} %slice.46), channel_id=1, source_target_pairs={{0,96},{1,33},{32,64},{33,1},{64,32},{65,97},{96,0},{97,65},{2,98}... | collective-permute-start | bytes 1081352 | tf_op jit(solution)/shard_map/ppermute | solution.py:28
  46.3 14.5 %collective-permute-start.4 = (bf16[128,512]{1,0:T(8,128)(2,1)S(1)}, bf16[128,512]{1,0:T(8,128)(2,1)S(1)}, u32[]{:S(2)}, u32[]{:S(2)}) collective-permute-start(bf16[128,512]{1,0:T(8,128)(2,1)S(1)} %slice.47), channel_id=1, source_target_pairs={{0,0},{1,32},{2,64},{3,96},{4,128},{5,160},{6,192},{7,224},{8,256}... | collective-permute-start | bytes 393224 | tf_op jit(solution)/shard_map/ppermute | solution.py:33
  63.2 40.4 %copy-start.2 = (bf16[128,1792]{1,0:T(8,128)(2,1)}, bf16[128,1792]{1,0:T(8,128)(2,1)S(1)}, u32[]{:S(2)}) copy-start(bf16[128,1792]{1,0:T(8,128)(2,1)S(1)} %collective-permute-done.x1) | copy-start | bytes 1376260
  63.2 40.5 %copy-start.4 = (bf16[128,1792]{1,0:T(8,128)(2,1)}, bf16[128,1792]{1,0:T(8,128)(2,1)S(1)}, u32[]{:S(2)}) copy-start(bf16[128,1792]{1,0:T(8,128)(2,1)S(1)} %collective-permute-done.1.x2) | copy-start | bytes 1376260
  63.3 17.9 %collective-permute-start.5 = (bf16[128,1792]{1,0:T(8,128)(2,1)S(1)}, bf16[128,1792]{1,0:T(8,128)(2,1)S(1)}, u32[]{:S(2)}, u32[]{:S(2)}) collective-permute-start(bf16[128,1792]{1,0:T(8,128)(2,1)S(1)} %collective-permute-done.x1), channel_id=1, source_target_pairs={{0,384},{1,129},{128,256},{129,1},{256,128},{257,385},{384,0},{385... | collective-permute-start | bytes 1376264 | tf_op jit(solution)/shard_map/ppermute | solution.py:28
  67.3 13.9 %collective-permute-start.6 = (bf16[128,1408]{1,0:T(8,128)(2,1)S(1)}, bf16[128,1408]{1,0:T(8,128)(2,1)S(1)}, u32[]{:S(2)}, u32[]{:S(2)}) collective-permute-start(bf16[128,1408]{1,0:T(8,128)(2,1)S(1)} %collective-permute-done.2), channel_id=1, source_target_pairs={{0,96},{1,33},{32,64},{33,1},{64,32},{65,97},{96,0},{97,65},{2,98}... | collective-permute-start | bytes 1081352 | tf_op jit(solution)/shard_map/ppermute | solution.py:28
  70.2 10.9 %collective-permute-start.7 = (bf16[128,512]{1,0:T(8,128)(2,1)S(1)}, bf16[128,512]{1,0:T(8,128)(2,1)S(1)}, u32[]{:S(2)}, u32[]{:S(2)}) collective-permute-start(bf16[128,512]{1,0:T(8,128)(2,1)S(1)} %collective-permute-done.4), channel_id=1, source_target_pairs={{0,6},{1,11},{2,12},{3,9},{4,10},{5,15},{6,0},{7,13},{8,14},{9,3},... | collective-permute-start | bytes 393224 | tf_op jit(solution)/shard_map/ppermute | solution.py:43
  81.2 22.6 %copy-start.6 = (bf16[128,1792]{1,0:T(8,128)(2,1)}, bf16[128,1792]{1,0:T(8,128)(2,1)S(1)}, u32[]{:S(2)}) copy-start(bf16[128,1792]{1,0:T(8,128)(2,1)S(1)} %collective-permute-done.5.x3) | copy-start | bytes 1376260
  81.2 22.5 %slice-start = ((bf16[128,2304]{1,0:T(8,128)(2,1)}), bf16[128,384]{1,0:T(8,128)(2,1)S(1)}, s32[]{:S(2)}) async-start(bf16[128,2304]{1,0:T(8,128)(2,1)} %copy-done.8), calls=%async_computation.1 | async-start | bytes 196608 | tf_op jit(solution)/shard_map/slice | solution.py:228
  81.2 45.0 %collective-permute-start.8 = (bf16[384,1408]{1,0:T(8,128)(2,1)S(1)}, bf16[384,1408]{1,0:T(8,128)(2,1)S(1)}, u32[]{:S(2)}, u32[]{:S(2)}) collective-permute-start(bf16[384,1408]{1,0:T(8,128)(2,1)S(1)} %constant_dynamic-update-slice_fusion.y0), channel_id=1, source_target_pairs={{0,128},{1,385},{128,0},{129,257},{256,384},{257,129},{384,256},{3... | collective-permute-start | bytes 3244040 | tf_op jit(solution)/shard_map/ppermute | solution.py:28
  85.9 41.3 %collective-permute-start.9 = (bf16[384,1408]{1,0:T(8,128)(2,1)S(1)}, bf16[384,1408]{1,0:T(8,128)(2,1)}, u32[]{:S(2)}, u32[]{:S(2)}) collective-permute-start(bf16[384,1408]{1,0:T(8,128)(2,1)S(1)} %constant_dynamic-update-slice_fusion.y0), channel_id=1, source_target_pairs={{0,384},{1,129},{128,256},{129,1},{256,128},{257,385},{384,0},{385... | collective-permute-start | bytes 3244040 | tf_op jit(solution)/shard_map/ppermute | solution.py:28
  90.9 9.5 %collective-permute-start.12 = (bf16[256,512]{1,0:T(8,128)(2,1)S(1)}, bf16[256,512]{1,0:T(8,128)(2,1)S(1)}, u32[]{:S(2)}, u32[]{:S(2)}) collective-permute-start(bf16[256,512]{1,0:T(8,128)(2,1)S(1)} %pad_maximum_fusion.2), channel_id=1, source_target_pairs={{0,14},{1,3},{2,4},{3,1},{4,2},{5,7},{6,8},{7,5},{8,6},{9,11},{10,... | collective-permute-start | bytes 786440 | tf_op jit(solution)/shard_map/ppermute | solution.py:43
  100.4 25.8 %collective-permute-start.13 = (bf16[512,512]{1,0:T(8,128)(2,1)S(1)}, bf16[512,512]{1,0:T(8,128)(2,1)}, u32[]{:S(2)}, u32[]{:S(2)}) collective-permute-start(bf16[512,512]{1,0:T(8,128)(2,1)S(1)} %constant_dynamic-update-slice_fusion.3.mine2_ref), channel_id=1, source_target_pairs={{0,2},{1,15},{2,0},{3,5},{4,6},{5,3},{6,4},{7,9},{8,10},{9,7},{10,... | collective-permute-start | bytes 1572872 | tf_op jit(solution)/shard_map/ppermute | solution.py:43
  103.8 20.0 %collective-permute-start.10 = (bf16[512,384]{1,0:T(8,128)(2,1)S(1)}, bf16[512,384]{1,0:T(8,128)(2,1)}, u32[]{:S(2)}, u32[]{:S(2)}) collective-permute-start(bf16[512,384]{1,0:T(8,128)(2,1)S(1)} %pad_maximum_fusion.1.r0), channel_id=1, source_target_pairs={{0,32},{1,97},{32,0},{33,65},{64,96},{65,33},{96,64},{97,1},{2,34}... | collective-permute-start | bytes 1179656 | tf_op jit(solution)/shard_map/ppermute | solution.py:28
  108.1 18.1 %collective-permute-start.11 = (bf16[512,384]{1,0:T(8,128)(2,1)S(1)}, bf16[512,384]{1,0:T(8,128)(2,1)}, u32[]{:S(2)}, u32[]{:S(2)}) collective-permute-start(bf16[512,384]{1,0:T(8,128)(2,1)S(1)} %pad_maximum_fusion.1.r0), channel_id=1, source_target_pairs={{0,96},{1,33},{32,64},{33,1},{64,32},{65,97},{96,0},{97,65},{2,98}... | collective-permute-start | bytes 1179656 | tf_op jit(solution)/shard_map/ppermute | solution.py:28
  127.2 28.3 %collective-permute-start.16 = (bf16[384,1408]{1,0:T(8,128)(2,1)}, bf16[384,1408]{1,0:T(8,128)(2,1)S(1)}, u32[]{:S(2)}, u32[]{:S(2)}) collective-permute-start(bf16[384,1408]{1,0:T(8,128)(2,1)} %copy-done), channel_id=1, source_target_pairs={{0,384},{1,129},{128,256},{129,1},{256,128},{257,385},{384,0},{385... | collective-permute-start | bytes 3244040 | tf_op jit(solution)/shard_map/ppermute | solution.py:28
  131.9 10.7 %collective-permute-start.14 = (bf16[512,512]{1,0:T(8,128)(2,1)S(1)}, bf16[512,512]{1,0:T(8,128)(2,1)}, u32[]{:S(2)}, u32[]{:S(2)}) collective-permute-start(bf16[512,512]{1,0:T(8,128)(2,1)S(1)} %constant_dynamic-update-slice_fusion.3.mine2_ref), channel_id=1, source_target_pairs={{0,1},{1,0},{2,3},{3,2},{4,5},{5,4},{6,7},{7,6},{8,9},{9,8},{10,11... | collective-permute-start | bytes 1572872 | tf_op jit(solution)/shard_map/ppermute | solution.py:237
  133.8 8.8 %collective-permute-start.15 = (bf16[512,512]{1,0:T(8,128)(2,1)}, bf16[512,512]{1,0:T(8,128)(2,1)}, u32[]{:S(2)}, u32[]{:S(2)}) collective-permute-start(bf16[512,512]{1,0:T(8,128)(2,1)} %collective-permute-done.13.mine3_ref), channel_id=1, source_target_pairs={{0,1},{1,0},{2,3},{3,2},{4,5},{5,4},{6,7},{7,6},{8,9},{9,8},{10,11... | collective-permute-start | bytes 1572872 | tf_op jit(solution)/shard_map/ppermute | solution.py:237
  136.3 19.2 %collective-permute-start.17 = (bf16[512,384]{1,0:T(8,128)(2,1)}, bf16[512,384]{1,0:T(8,128)(2,1)}, u32[]{:S(2)}, u32[]{:S(2)}) collective-permute-start(bf16[512,384]{1,0:T(8,128)(2,1)} %collective-permute-done.10.r1), channel_id=1, source_target_pairs={{0,96},{1,33},{32,64},{33,1},{64,32},{65,97},{96,0},{97,65},{2,98}... | collective-permute-start | bytes 1179656 | tf_op jit(solution)/shard_map/ppermute | solution.py:28
  142.5 5.1 %copy-start.1 = (bf16[384,1408]{1,0:T(8,128)(2,1)S(1)}, bf16[384,1408]{1,0:T(8,128)(2,1)}, u32[]{:S(2)}) copy-start(bf16[384,1408]{1,0:T(8,128)(2,1)} %copy-done) | copy-start | bytes 3244036
  (4 other events, 12.1 us)

commit v6 on v4

--- a/solution.py
+++ b/solution.py
@@ -181,7 +181,7 @@
     tiles(near + [(y3, i, False) for i in range(4)], FIRST, width - FIRST, [(0, 768), (1280, 256)])
 
 
-def late_kernel(slab_ref, sums_ref, acc_ref, pivot_ref, square_ref, x4, y4, out_ref, *scratch):
+def late_kernel(slab_ref, sums_ref, acc_ref, pivot_ref, square_ref, far, opposite, y4, out_ref, *scratch):
     width = acc_ref.shape[1]
 
     def tiles(pieces, offset, columns, spans):
@@ -203,7 +203,7 @@
 
         over_tiles(columns, scratch, body)
 
-    tiles([(x4, i) for i in (0, 3, 1, 4, 2, 5)], 0, FIRST, [(1280, 768)])
+    tiles([(ref, i) for i in range(3) for ref in (far, opposite)], 0, FIRST, [(1280, 768)])
     tiles([(y4, i) for i in (0, 1, 4, 5, 2, 3, 6, 7)], FIRST, width - FIRST, [(768, 512), (1536, 512)])
 
 
@@ -238,7 +238,7 @@
     x3, y3, slab2, slab3 = together((x3, y3, slab2, slab3))
     rest = jnp.concatenate([rest, y3], axis=0)
     y4 = exchange(rest, "yh", 1)
-    x4 = exchange(jnp.concatenate([three, x3], axis=0), "x", 1)
+    x4 = [exchange(part, "x", 1) for part in (three, x3)]
 
     quarters = [slab2, slab3] + [lax.ppermute(part, "c", [(0, 1), (1, 0)]) for part in (slab2, slab3)]
 
@@ -266,11 +266,11 @@
     (out,) = call(
         late_kernel,
         [jax.ShapeDtypeStruct((ROWS_DEV, width), jnp.bfloat16)],
-        [VMEM] * 7,
+        [VMEM] * 8,
         [pltpu.VMEM((1024, TILE), jnp.bfloat16)] * 2,
         TOKENS * ROWS_DEV * width,
         4 * ROWS_DEV * width,
-        (slab, sums, acc, pivot, square, x4, y4),
+        (slab, sums, acc, pivot, square, *x4, y4),
     )
     return out
 

time: 147 us -> 148 us (level)
  starting transfers between devices: 54.5 us -> 57.9 us
  waiting for transfers between devices: 35.8 us -> 32.9 us
  Pallas kernels: 14.8 us -> 16.4 us
    ppermute x8 -> x9, starting transfers between devices: 39.5 us -> 42.9 us  [exchange(): return lax.ppermute(values, (axis, 'c'), perm)]
    concatenate x2 -> x0, other arithmetic: 1.61 us -> none  [the longest x1 1.53 us: per_device(): x4 = exchange(jnp.concatenate([three, x3], axis=0), 'x', 1)]
    pallas_call x3, Pallas kernels: 14.8 us -> 16.4 us  [call(): pl.pallas_call(kernel, out_shape=outs, in_specs=in_specs, out_specs=[pl.B...]
    ppermute x3, waiting for transfers between devices: 15.6 us -> 14.1 us  [z_permute(): return lax.ppermute(values, ('z', 'c'), perm)]
    ppermute x8 -> x9, waiting for transfers between devices: 13.7 us -> 12.2 us  [exchange(): return lax.ppermute(values, (axis, 'c'), perm)]
  transfers between devices with their start and end apart: 14 -> 15, of which waited for: 6 -> 7; matrix products, arithmetic and copies ran while one was open for 4% -> 5% of each run, Pallas kernels for 6% -> 7%
where the time goes in v6:
time: 148 us
  starting transfers between devices  57.9 us (39%)
  waiting for transfers between devices  32.9 us (22%)
  blocking collectives  28.7 us (19%)
  Pallas kernels  16.4 us (11%)
  local copies, waits for them, and re-layouts  6.55 us (4%)
  other arithmetic  4.89 us (3%)
    ppermute x9, starting transfers between devices, exchange(): return lax.ppermute(values, (axis, 'c'), perm)  42.9 us
    all_to_all x1, blocking collectives, per_device(): lax.all_to_all(with_slab.reshape(tok, n_col * (width + ROWS_DEV)), ('yl',...  28.7 us
    pallas_call x3, Pallas kernels, call(): pl.pallas_call(kernel, out_shape=outs, in_specs=in_specs, out_specs=[pl.B...  16.4 us
    ppermute x3, waiting for transfers between devices, z_permute(): return lax.ppermute(values, ('z', 'c'), perm)  14.1 us
    ppermute x9, waiting for transfers between devices, exchange(): return lax.ppermute(values, (axis, 'c'), perm)  12.2 us
    ppermute x1, waiting for transfers between devices, swap_places(): return lax.ppermute(values, ALL, perm)  6.18 us
    ppermute x3, starting transfers between devices, z_permute(): return lax.ppermute(values, ('z', 'c'), perm)  5.75 us
    ppermute x1, starting transfers between devices, swap_places(): return lax.ppermute(values, ALL, perm)  4.89 us
  transfers between devices with their start and end apart: 15, of which 7 were waited for; matrix products, arithmetic and copies ran while one was open for 5% of the time, Pallas kernels for 7%

profile of v6, /device:TPU:6, one launch (start us, length us, event | category | flops | bytes accessed | tf_op | source)
XLA Modules:
  0.0 147.6 jit_solution(1042686137379429385)
XLA Ops:
  2.2 28.7 %all_to_all.16 = bf16[4,32,2304]{2,0,1:T(4,128)(2,1)S(1)} all-to-all(bf16[4,32,2304]{2,0,1:T(4,128)(2,1)S(1)} %pad_maximum_fusion.3), channel_id=1, replica_groups=mesh['x'=4,'yh'=4,'yl'=2,'z'=8,'c'=2] {'yl','z','c'}, dimensions={1} | all-to-all | bytes 1179648 | tf_op jit(solution)/shard_map/all_to_all | solution.py:219
  31.1 2.7 %collective-permute-start = (bf16[128,1792]{1,0:T(8,128)(2,1)S(1)}, bf16[128,1792]{1,0:T(8,128)(2,1)S(1)}, u32[]{:S(2)}, u32[]{:S(2)}) collective-permute-start(bf16[128,1792]{1,0:T(8,128)(2,1)S(1)} %slice.41.own), channel_id=1, source_target_pairs={{0,128},{1,385},{128,0},{129,257},{256,384},{257,129},{384,256},{3... | collective-permute-start | bytes 1376264 | tf_op jit(solution)/shard_map/ppermute | solution.py:27
  33.9 4.5 %collective-permute-start.1 = (bf16[128,1408]{1,0:T(8,128)(2,1)S(1)}, bf16[128,1408]{1,0:T(8,128)(2,1)S(1)}, u32[]{:S(2)}, u32[]{:S(2)}) collective-permute-start(bf16[128,1408]{1,0:T(8,128)(2,1)S(1)} %slice.42), channel_id=1, source_target_pairs={{0,32},{1,97},{32,0},{33,65},{64,96},{65,33},{96,64},{97,1},{2,34}... | collective-permute-start | bytes 1081352 | tf_op jit(solution)/shard_map/ppermute | solution.py:27
  38.4 4.9 %collective-permute-start.2 = (bf16[128,512]{1,0:T(8,128)(2,1)S(1)}, bf16[128,512]{1,0:T(8,128)(2,1)S(1)}, u32[]{:S(2)}, u32[]{:S(2)}) collective-permute-start(bf16[128,512]{1,0:T(8,128)(2,1)S(1)} %slice.43), channel_id=1, source_target_pairs={{0,0},{1,32},{2,64},{3,96},{4,128},{5,160},{6,192},{7,224},{8,256}... | collective-permute-start | bytes 393224 | tf_op jit(solution)/shard_map/ppermute | solution.py:32
  43.3 6.2 %collective-permute-done.2 = bf16[128,512]{1,0:T(8,128)(2,1)S(1)} collective-permute-done((bf16[128,512]{1,0:T(8,128)(2,1)S(1)}, bf16[128,512]{1,0:T(8,128)(2,1)S(1)}, u32[]{:S(2)}, u32[]{:S(2)}) %collective-permute-start.2) | collective-permute-done | bytes 131104 | tf_op jit(solution)/shard_map/ppermute | solution.py:32
  49.6 1.9 %collective-permute-start.3 = (bf16[256,1792]{1,0:T(8,128)(2,1)S(1)}, bf16[256,1792]{1,0:T(8,128)(2,1)S(1)}, u32[]{:S(2)}, u32[]{:S(2)}) collective-permute-start(bf16[256,1792]{1,0:T(8,128)(2,1)S(1)} %pad_maximum_fusion), channel_id=1, source_target_pairs={{0,384},{1,129},{128,256},{129,1},{256,128},{257,385},{384,0},{385... | collective-permute-start | bytes 2752520 | tf_op jit(solution)/shard_map/ppermute | solution.py:27
  51.6 15.0 %collective-permute-start.4 = (bf16[256,1408]{1,0:T(8,128)(2,1)S(1)}, bf16[256,1408]{1,0:T(8,128)(2,1)S(1)}, u32[]{:S(2)}, u32[]{:S(2)}) collective-permute-start(bf16[256,1408]{1,0:T(8,128)(2,1)S(1)} %pad_maximum_fusion.2), channel_id=1, source_target_pairs={{0,96},{1,33},{32,64},{33,1},{64,32},{65,97},{96,0},{97,65},{2,98}... | collective-permute-start | bytes 2162696 | tf_op jit(solution)/shard_map/ppermute | solution.py:27
  66.6 1.9 %collective-permute-start.5 = (bf16[128,512]{1,0:T(8,128)(2,1)S(1)}, bf16[128,512]{1,0:T(8,128)(2,1)S(1)}, u32[]{:S(2)}, u32[]{:S(2)}) collective-permute-start(bf16[128,512]{1,0:T(8,128)(2,1)S(1)} %collective-permute-done.2), channel_id=1, source_target_pairs={{0,6},{1,11},{2,12},{3,9},{4,10},{5,15},{6,0},{7,13},{8,14},{9,3},... | collective-permute-start | bytes 393224 | tf_op jit(solution)/shard_map/ppermute | solution.py:42
  68.5 8.2 %collective-permute-done.5 = bf16[128,512]{1,0:T(8,128)(2,1)S(1)} collective-permute-done((bf16[128,512]{1,0:T(8,128)(2,1)S(1)}, bf16[128,512]{1,0:T(8,128)(2,1)S(1)}, u32[]{:S(2)}, u32[]{:S(2)}) %collective-permute-start.5) | collective-permute-done | bytes 131104 | tf_op jit(solution)/shard_map/ppermute | solution.py:42
  76.7 1.9 %collective-permute-start.6 = (bf16[256,512]{1,0:T(8,128)(2,1)S(1)}, bf16[256,512]{1,0:T(8,128)(2,1)S(1)}, u32[]{:S(2)}, u32[]{:S(2)}) collective-permute-start(bf16[256,512]{1,0:T(8,128)(2,1)S(1)} %constant_dynamic-update-slice_fusion), channel_id=1, source_target_pairs={{0,14},{1,3},{2,4},{3,1},{4,2},{5,7},{6,8},{7,5},{8,6},{9,11},{10,... | collective-permute-start | bytes 786440 | tf_op jit(solution)/shard_map/ppermute | solution.py:42
  80.3 5.9 %collective-permute-done.6 = bf16[256,512]{1,0:T(8,128)(2,1)S(1)} collective-permute-done((bf16[256,512]{1,0:T(8,128)(2,1)S(1)}, bf16[256,512]{1,0:T(8,128)(2,1)S(1)}, u32[]{:S(2)}, u32[]{:S(2)}) %collective-permute-start.6) | collective-permute-done | bytes 262176 | tf_op jit(solution)/shard_map/ppermute | solution.py:42
  87.1 4.4 %collective-permute-start.7 = (bf16[384,1408]{1,0:T(8,128)(2,1)}, bf16[384,1408]{1,0:T(8,128)(2,1)}, u32[]{:S(2)}, u32[]{:S(2)}) collective-permute-start(bf16[384,1408]{1,0:T(8,128)(2,1)} %constant_dynamic-update-slice_fusion.2), channel_id=1, source_target_pairs={{0,128},{1,385},{128,0},{129,257},{256,384},{257,129},{384,256},{3... | collective-permute-start | bytes 3244040 | tf_op jit(solution)/shard_map/ppermute | solution.py:27
  94.9 1.9 %collective-permute-start.8 = (bf16[512,384]{1,0:T(8,128)(2,1)}, bf16[512,384]{1,0:T(8,128)(2,1)S(1)}, u32[]{:S(2)}, u32[]{:S(2)}) collective-permute-start(bf16[512,384]{1,0:T(8,128)(2,1)} %pad_maximum_fusion.4), channel_id=1, source_target_pairs={{0,32},{1,97},{32,0},{33,65},{64,96},{65,33},{96,64},{97,1},{2,34}... | collective-permute-start | bytes 1179656 | tf_op jit(solution)/shard_map/ppermute | solution.py:27
  97.7 4.7 %collective-permute-start.12 = (bf16[384,1408]{1,0:T(8,128)(2,1)}, bf16[384,1408]{1,0:T(8,128)(2,1)}, u32[]{:S(2)}, u32[]{:S(2)}) collective-permute-start(bf16[384,1408]{1,0:T(8,128)(2,1)} %constant_dynamic-update-slice_fusion.2), channel_id=1, source_target_pairs={{0,384},{1,129},{128,256},{129,1},{256,128},{257,385},{384,0},{385... | collective-permute-start | bytes 3244040 | tf_op jit(solution)/shard_map/ppermute | solution.py:27
  102.4 3.7 %collective-permute-done.8.y3 = bf16[512,384]{1,0:T(8,128)(2,1)S(1)} collective-permute-done((bf16[512,384]{1,0:T(8,128)(2,1)}, bf16[512,384]{1,0:T(8,128)(2,1)S(1)}, u32[]{:S(2)}, u32[]{:S(2)}) %collective-permute-start.8) | collective-permute-done | bytes 393248 | tf_op jit(solution)/shard_map/ppermute | solution.py:27
  106.1 3.6 %collective-permute-done.7.x3 = bf16[384,1408]{1,0:T(8,128)(2,1)} collective-permute-done((bf16[384,1408]{1,0:T(8,128)(2,1)}, bf16[384,1408]{1,0:T(8,128)(2,1)}, u32[]{:S(2)}, u32[]{:S(2)}) %collective-permute-start.7) | collective-permute-done | bytes 1081376 | tf_op jit(solution)/shard_map/ppermute | solution.py:27
  109.7 5.9 %collective-permute-start.13 = (bf16[384,1408]{1,0:T(8,128)(2,1)}, bf16[384,1408]{1,0:T(8,128)(2,1)}, u32[]{:S(2)}, u32[]{:S(2)}) collective-permute-start(bf16[384,1408]{1,0:T(8,128)(2,1)} %collective-permute-done.7.x3), channel_id=1, source_target_pairs={{0,384},{1,129},{128,256},{129,1},{256,128},{257,385},{384,0},{385... | collective-permute-start | bytes 3244040 | tf_op jit(solution)/shard_map/ppermute | solution.py:27
  116.2 2.0 %pad_maximum_fusion.1 = bf16[1024,384]{1,0:T(8,128)(2,1)} fusion(bf16[512,384]{1,0:T(8,128)(2,1)S(1)} %collective-permute-done.8.y3, bf16[512,384]{1,0:T(8,128)(2,1)} %pad_maximum_fusion.4), kind=kLoop, calls=%fused_computation.3 | loop fusion | flops 1572864 | bytes 1572864 | tf_op jit(solution)/shard_map/concatenate | solution.py:239
  120.2 1.9 %collective-permute-start.10 = (bf16[512,512]{1,0:T(8,128)(2,1)}, bf16[512,512]{1,0:T(8,128)(2,1)}, u32[]{:S(2)}, u32[]{:S(2)}) collective-permute-start(bf16[512,512]{1,0:T(8,128)(2,1)} %constant_dynamic-update-slice_fusion.4.mine2_ref), channel_id=1, source_target_pairs={{0,1},{1,0},{2,3},{3,2},{4,5},{5,4},{6,7},{7,6},{8,9},{9,8},{10,11... | collective-permute-start | bytes 1572872 | tf_op jit(solution)/shard_map/ppermute | solution.py:243
  122.1 2.4 %collective-permute-start.11 = (bf16[512,512]{1,0:T(8,128)(2,1)}, bf16[512,512]{1,0:T(8,128)(2,1)}, u32[]{:S(2)}, u32[]{:S(2)}) collective-permute-start(bf16[512,512]{1,0:T(8,128)(2,1)} %collective-permute-done.9.mine3_ref), channel_id=1, source_target_pairs={{0,1},{1,0},{2,3},{3,2},{4,5},{5,4},{6,7},{7,6},{8,9},{9,8},{10,11... | collective-permute-start | bytes 1572872 | tf_op jit(solution)/shard_map/ppermute | solution.py:243
  126.4 5.0 %shard_map.28 = (bf16[512,2048]{1,0:T(8,128)(2,1)S(1)}, f32[512,128]{1,0:T(8,128)S(1)}) custom-call(s32[16]{0:T(128)S(1)} %compare_select_fusion.3.place_ref, bf16[512,512]{1,0:T(8,128)(2,1)} %constant_dynamic-update-slice_fusion.4.mine2_ref, bf16[512,512]{1,0:T(8,128)(2,1)} %collective-permute-done.9.mine3_ref, ...), custom_call_target="tpu_custom_call" | custom-call | flops 131072 | bytes 65536 | tf_op jit(solution)/shard_map/pallas_call | solution.py:90
  131.4 5.4 %shard_map.29 = (f32[512,1792]{1,0:T(8,128)S(1)}, f32[8,1792]{1,0:T(8,128)S(1)}, f32[8,1792]{1,0:T(8,128)S(1)}) custom-call(bf16[512,2048]{1,0:T(8,128)(2,1)S(1)} %get-tuple-element.31.slab_ref, bf16[128,1792]{1,0:T(8,128)(2,1)S(1)} %slice.41.own, bf16[128,1792]{1,0:T(8,128)(2,1)S(1)} %copy-done.1, bf16[256,1792]{1,0:T(8,128)(2,1)S(1)} %collective-permute-done.3.x2, ...), custom_call_target="tpu_custom_call" | custom-call | flops 29360128 | bytes 57344 | tf_op jit(solution)/shard_map/pallas_call | solution.py:90
  136.8 4.9 %collective-permute-done.14.y4 = bf16[1024,384]{1,0:T(8,128)(2,1)} collective-permute-done((bf16[1024,384]{1,0:T(8,128)(2,1)}, bf16[1024,384]{1,0:T(8,128)(2,1)}, u32[]{:S(2)}, u32[]{:S(2)}) %collective-permute-start.14) | collective-permute-done | bytes 786464 | tf_op jit(solution)/shard_map/ppermute | solution.py:27
  141.7 6.0 %shard_map.30 = bf16[512,1792]{1,0:T(8,128)(2,1)} custom-call(bf16[512,2048]{1,0:T(8,128)(2,1)S(1)} %get-tuple-element.31.slab_ref, f32[512,128]{1,0:T(8,128)S(1)} %get-tuple-element.32.sums_ref, f32[512,1792]{1,0:T(8,128)S(1)} %get-tuple-element.36.acc_ref, f32[8,1792]{1,0:T(8,128)S(1)} %get-tuple-element.37.pivot_ref, ...), custom_call_target="tpu_custom_call" | custom-call | flops 29360128 | bytes 57344 | tf_op jit(solution)/shard_map/pallas_call | solution.py:90
  (49 shorter events, 13.7 us)
Async XLA Ops:
  31.1 18.5 %copy-start.2 = (bf16[128,2304]{1,0:T(8,128)(2,1)}, bf16[128,2304]{1,0:T(8,128)(2,1)S(1)}, u32[]{:S(2)}) copy-start(bf16[128,2304]{1,0:T(8,128)(2,1)S(1)} %all_to_all.14) | copy-start | bytes 1769476
  31.1 18.4 %collective-permute-start = (bf16[128,1792]{1,0:T(8,128)(2,1)S(1)}, bf16[128,1792]{1,0:T(8,128)(2,1)S(1)}, u32[]{:S(2)}, u32[]{:S(2)}) collective-permute-start(bf16[128,1792]{1,0:T(8,128)(2,1)S(1)} %slice.41.own), channel_id=1, source_target_pairs={{0,128},{1,385},{128,0},{129,257},{256,384},{257,129},{384,256},{3... | collective-permute-start | bytes 1376264 | tf_op jit(solution)/shard_map/ppermute | solution.py:27
  33.9 15.6 %collective-permute-start.1 = (bf16[128,1408]{1,0:T(8,128)(2,1)S(1)}, bf16[128,1408]{1,0:T(8,128)(2,1)S(1)}, u32[]{:S(2)}, u32[]{:S(2)}) collective-permute-start(bf16[128,1408]{1,0:T(8,128)(2,1)S(1)} %slice.42), channel_id=1, source_target_pairs={{0,32},{1,97},{32,0},{33,65},{64,96},{65,33},{96,64},{97,1},{2,34}... | collective-permute-start | bytes 1081352 | tf_op jit(solution)/shard_map/ppermute | solution.py:27
  38.4 11.1 %collective-permute-start.2 = (bf16[128,512]{1,0:T(8,128)(2,1)S(1)}, bf16[128,512]{1,0:T(8,128)(2,1)S(1)}, u32[]{:S(2)}, u32[]{:S(2)}) collective-permute-start(bf16[128,512]{1,0:T(8,128)(2,1)S(1)} %slice.43), channel_id=1, source_target_pairs={{0,0},{1,32},{2,64},{3,96},{4,128},{5,160},{6,192},{7,224},{8,256}... | collective-permute-start | bytes 393224 | tf_op jit(solution)/shard_map/ppermute | solution.py:32
  49.5 19.0 %copy-start = (bf16[128,1792]{1,0:T(8,128)(2,1)}, bf16[128,1792]{1,0:T(8,128)(2,1)S(1)}, u32[]{:S(2)}) copy-start(bf16[128,1792]{1,0:T(8,128)(2,1)S(1)} %collective-permute-done.x1) | copy-start | bytes 1376260
  49.6 29.8 %collective-permute-start.3 = (bf16[256,1792]{1,0:T(8,128)(2,1)S(1)}, bf16[256,1792]{1,0:T(8,128)(2,1)S(1)}, u32[]{:S(2)}, u32[]{:S(2)}) collective-permute-start(bf16[256,1792]{1,0:T(8,128)(2,1)S(1)} %pad_maximum_fusion), channel_id=1, source_target_pairs={{0,384},{1,129},{128,256},{129,1},{256,128},{257,385},{384,0},{385... | collective-permute-start | bytes 2752520 | tf_op jit(solution)/shard_map/ppermute | solution.py:27
  51.5 27.9 %slice-start.1 = ((bf16[128,2304]{1,0:T(8,128)(2,1)}), bf16[128,384]{1,0:T(8,128)(2,1)S(1)}, s32[]{:S(2)}) async-start(bf16[128,2304]{1,0:T(8,128)(2,1)} %copy-done.2), calls=%async_computation.2 | async-start | bytes 196608 | tf_op jit(solution)/shard_map/slice | solution.py:231
  51.6 34.6 %collective-permute-start.4 = (bf16[256,1408]{1,0:T(8,128)(2,1)S(1)}, bf16[256,1408]{1,0:T(8,128)(2,1)S(1)}, u32[]{:S(2)}, u32[]{:S(2)}) collective-permute-start(bf16[256,1408]{1,0:T(8,128)(2,1)S(1)} %pad_maximum_fusion.2), channel_id=1, source_target_pairs={{0,96},{1,33},{32,64},{33,1},{64,32},{65,97},{96,0},{97,65},{2,98}... | collective-permute-start | bytes 2162696 | tf_op jit(solution)/shard_map/ppermute | solution.py:27
  66.6 10.2 %collective-permute-start.5 = (bf16[128,512]{1,0:T(8,128)(2,1)S(1)}, bf16[128,512]{1,0:T(8,128)(2,1)S(1)}, u32[]{:S(2)}, u32[]{:S(2)}) collective-permute-start(bf16[128,512]{1,0:T(8,128)(2,1)S(1)} %collective-permute-done.2), channel_id=1, source_target_pairs={{0,6},{1,11},{2,12},{3,9},{4,10},{5,15},{6,0},{7,13},{8,14},{9,3},... | collective-permute-start | bytes 393224 | tf_op jit(solution)/shard_map/ppermute | solution.py:42
  68.5 11.0 %slice-start = ((bf16[128,1792]{1,0:T(8,128)(2,1)}), bf16[128,384]{1,0:T(8,128)(2,1)S(1)}, s32[]{:S(2)}) async-start(bf16[128,1792]{1,0:T(8,128)(2,1)} %copy-done), calls=%async_computation.1 | async-start | bytes 196608 | tf_op jit(solution)/shard_map/slice | solution.py:231
  76.7 9.5 %collective-permute-start.6 = (bf16[256,512]{1,0:T(8,128)(2,1)S(1)}, bf16[256,512]{1,0:T(8,128)(2,1)S(1)}, u32[]{:S(2)}, u32[]{:S(2)}) collective-permute-start(bf16[256,512]{1,0:T(8,128)(2,1)S(1)} %constant_dynamic-update-slice_fusion), channel_id=1, source_target_pairs={{0,14},{1,3},{2,4},{3,1},{4,2},{5,7},{6,8},{7,5},{8,6},{9,11},{10,... | collective-permute-start | bytes 786440 | tf_op jit(solution)/shard_map/ppermute | solution.py:42
  87.1 22.5 %collective-permute-start.7 = (bf16[384,1408]{1,0:T(8,128)(2,1)}, bf16[384,1408]{1,0:T(8,128)(2,1)}, u32[]{:S(2)}, u32[]{:S(2)}) collective-permute-start(bf16[384,1408]{1,0:T(8,128)(2,1)} %constant_dynamic-update-slice_fusion.2), channel_id=1, source_target_pairs={{0,128},{1,385},{128,0},{129,257},{256,384},{257,129},{384,256},{3... | collective-permute-start | bytes 3244040 | tf_op jit(solution)/shard_map/ppermute | solution.py:27
  93.0 13.1 %collective-permute-start.9 = (bf16[512,512]{1,0:T(8,128)(2,1)}, bf16[512,512]{1,0:T(8,128)(2,1)}, u32[]{:S(2)}, u32[]{:S(2)}) collective-permute-start(bf16[512,512]{1,0:T(8,128)(2,1)} %constant_dynamic-update-slice_fusion.4.mine2_ref), channel_id=1, source_target_pairs={{0,2},{1,15},{2,0},{3,5},{4,6},{5,3},{6,4},{7,9},{8,10},{9,7},{10,... | collective-permute-start | bytes 1572872 | tf_op jit(solution)/shard_map/ppermute | solution.py:42
  94.9 11.1 %collective-permute-start.8 = (bf16[512,384]{1,0:T(8,128)(2,1)}, bf16[512,384]{1,0:T(8,128)(2,1)S(1)}, u32[]{:S(2)}, u32[]{:S(2)}) collective-permute-start(bf16[512,384]{1,0:T(8,128)(2,1)} %pad_maximum_fusion.4), channel_id=1, source_target_pairs={{0,32},{1,97},{32,0},{33,65},{64,96},{65,33},{96,64},{97,1},{2,34}... | collective-permute-start | bytes 1179656 | tf_op jit(solution)/shard_map/ppermute | solution.py:27
  97.7 39.1 %collective-permute-start.12 = (bf16[384,1408]{1,0:T(8,128)(2,1)}, bf16[384,1408]{1,0:T(8,128)(2,1)}, u32[]{:S(2)}, u32[]{:S(2)}) collective-permute-start(bf16[384,1408]{1,0:T(8,128)(2,1)} %constant_dynamic-update-slice_fusion.2), channel_id=1, source_target_pairs={{0,384},{1,129},{128,256},{129,1},{256,128},{257,385},{384,0},{385... | collective-permute-start | bytes 3244040 | tf_op jit(solution)/shard_map/ppermute | solution.py:27
  109.7 32.0 %collective-permute-start.13 = (bf16[384,1408]{1,0:T(8,128)(2,1)}, bf16[384,1408]{1,0:T(8,128)(2,1)}, u32[]{:S(2)}, u32[]{:S(2)}) collective-permute-start(bf16[384,1408]{1,0:T(8,128)(2,1)} %collective-permute-done.7.x3), channel_id=1, source_target_pairs={{0,384},{1,129},{128,256},{129,1},{256,128},{257,385},{384,0},{385... | collective-permute-start | bytes 3244040 | tf_op jit(solution)/shard_map/ppermute | solution.py:27
  118.2 23.5 %collective-permute-start.14 = (bf16[1024,384]{1,0:T(8,128)(2,1)}, bf16[1024,384]{1,0:T(8,128)(2,1)}, u32[]{:S(2)}, u32[]{:S(2)}) collective-permute-start(bf16[1024,384]{1,0:T(8,128)(2,1)} %pad_maximum_fusion.1), channel_id=1, source_target_pairs={{0,96},{1,33},{32,64},{33,1},{64,32},{65,97},{96,0},{97,65},{2,98}... | collective-permute-start | bytes 2359304 | tf_op jit(solution)/shard_map/ppermute | solution.py:27
  120.2 5.8 %collective-permute-start.10 = (bf16[512,512]{1,0:T(8,128)(2,1)}, bf16[512,512]{1,0:T(8,128)(2,1)}, u32[]{:S(2)}, u32[]{:S(2)}) collective-permute-start(bf16[512,512]{1,0:T(8,128)(2,1)} %constant_dynamic-update-slice_fusion.4.mine2_ref), channel_id=1, source_target_pairs={{0,1},{1,0},{2,3},{3,2},{4,5},{5,4},{6,7},{7,6},{8,9},{9,8},{10,11... | collective-permute-start | bytes 1572872 | tf_op jit(solution)/shard_map/ppermute | solution.py:243
  122.1 4.3 %collective-permute-start.11 = (bf16[512,512]{1,0:T(8,128)(2,1)}, bf16[512,512]{1,0:T(8,128)(2,1)}, u32[]{:S(2)}, u32[]{:S(2)}) collective-permute-start(bf16[512,512]{1,0:T(8,128)(2,1)} %collective-permute-done.9.mine3_ref), channel_id=1, source_target_pairs={{0,1},{1,0},{2,3},{3,2},{4,5},{5,4},{6,7},{7,6},{8,9},{9,8},{10,11... | collective-permute-start | bytes 1572872 | tf_op jit(solution)/shard_map/ppermute | solution.py:243
  125.2 6.2 %copy-start.1 = (bf16[128,1792]{1,0:T(8,128)(2,1)S(1)}, bf16[128,1792]{1,0:T(8,128)(2,1)}, u32[]{:S(2)}) copy-start(bf16[128,1792]{1,0:T(8,128)(2,1)} %copy-done) | copy-start | bytes 1376260

commit v7 on v4

--- a/solution.py
+++ b/solution.py
@@ -229,7 +229,7 @@
     slab1 = jnp.concatenate([slab0, z_permute(slab0, 0)], axis=0)
     slab2 = z_permute(slab1, 1)
     rest = jnp.concatenate([own[:, FIRST:], x1[:, FIRST:], x2[:, FIRST:]], axis=0)
-    x2, y2, rest, slab1, slab2 = together((x2, y2, rest, slab1, slab2))
+    x2, y2, rest, slab1 = together((x2, y2, rest, slab1))
     three = jnp.concatenate([y1, y2], axis=0)
     y3 = exchange(rest, "yh", 0)
     x3 = exchange(three, "x", 0)

time: 147 us -> 155 us (1.054)
  the two profiles are of different devices: /device:TPU:6 before, /device:TPU:4 now
where the time goes in v7:
time: 155 us
  starting transfers between devices  51 us (33%)
  waiting for transfers between devices  47.5 us (31%)
  blocking collectives  28.7 us (19%)
  Pallas kernels  14.8 us (10%)
  local copies, waits for them, and re-layouts  6.36 us (4%)
  other arithmetic  5.78 us (4%)
    ppermute x8, starting transfers between devices, exchange(): return lax.ppermute(values, (axis, 'c'), perm)  36.3 us
    all_to_all x1, blocking collectives, per_device(): lax.all_to_all(with_slab.reshape(tok, n_col * (width + ROWS_DEV)), ('yl',...  28.7 us
    ppermute x8, waiting for transfers between devices, exchange(): return lax.ppermute(values, (axis, 'c'), perm)  20 us
    ppermute x3, waiting for transfers between devices, z_permute(): return lax.ppermute(values, ('z', 'c'), perm)  16.6 us
    pallas_call x3, Pallas kernels, call(): pl.pallas_call(kernel, out_shape=outs, in_specs=in_specs, out_specs=[pl.B...  14.8 us
    ppermute x1, waiting for transfers between devices, swap_places(): return lax.ppermute(values, ALL, perm)  10.6 us
    ppermute x3, starting transfers between devices, z_permute(): return lax.ppermute(values, ('z', 'c'), perm)  5.76 us
    ppermute x1, starting transfers between devices, swap_places(): return lax.ppermute(values, ALL, perm)  4.57 us
  transfers between devices with their start and end apart: 14, of which 7 were waited for; matrix products, arithmetic and copies ran while one was open for 3% of the time, Pallas kernels for 6%

profile of v7, /device:TPU:4, one launch (start us, length us, event | category | flops | bytes accessed | tf_op | source)
XLA Modules:
  0.0 154.6 jit_solution(15700797904404396390)
XLA Ops:
  2.2 28.7 %all_to_all.16 = bf16[4,32,2304]{2,0,1:T(4,128)(2,1)S(1)} all-to-all(bf16[4,32,2304]{2,0,1:T(4,128)(2,1)S(1)} %pad_maximum_fusion.5), channel_id=1, replica_groups=mesh['x'=4,'yh'=4,'yl'=2,'z'=8,'c'=2] {'yl','z','c'}, dimensions={1} | all-to-all | bytes 1179648 | tf_op jit(solution)/shard_map/all_to_all | solution.py:219
  31.1 3.1 %collective-permute-start = (bf16[128,1792]{1,0:T(8,128)(2,1)S(1)}, bf16[128,1792]{1,0:T(8,128)(2,1)S(1)}, u32[]{:S(2)}, u32[]{:S(2)}) collective-permute-start(bf16[128,1792]{1,0:T(8,128)(2,1)S(1)} %slice.41.own), channel_id=1, source_target_pairs={{0,128},{1,385},{128,0},{129,257},{256,384},{257,129},{384,256},{3... | collective-permute-start | bytes 1376264 | tf_op jit(solution)/shard_map/ppermute | solution.py:27
  34.3 4.5 %collective-permute-start.1 = (bf16[128,1408]{1,0:T(8,128)(2,1)S(1)}, bf16[128,1408]{1,0:T(8,128)(2,1)S(1)}, u32[]{:S(2)}, u32[]{:S(2)}) collective-permute-start(bf16[128,1408]{1,0:T(8,128)(2,1)S(1)} %slice.42), channel_id=1, source_target_pairs={{0,32},{1,97},{32,0},{33,65},{64,96},{65,33},{96,64},{97,1},{2,34}... | collective-permute-start | bytes 1081352 | tf_op jit(solution)/shard_map/ppermute | solution.py:27
  38.8 4.6 %collective-permute-start.2 = (bf16[128,512]{1,0:T(8,128)(2,1)S(1)}, bf16[128,512]{1,0:T(8,128)(2,1)S(1)}, u32[]{:S(2)}, u32[]{:S(2)}) collective-permute-start(bf16[128,512]{1,0:T(8,128)(2,1)S(1)} %slice.43), channel_id=1, source_target_pairs={{0,0},{1,32},{2,64},{3,96},{4,128},{5,160},{6,192},{7,224},{8,256}... | collective-permute-start | bytes 393224 | tf_op jit(solution)/shard_map/ppermute | solution.py:32
  43.4 10.6 %collective-permute-done.2 = bf16[128,512]{1,0:T(8,128)(2,1)S(1)} collective-permute-done((bf16[128,512]{1,0:T(8,128)(2,1)S(1)}, bf16[128,512]{1,0:T(8,128)(2,1)S(1)}, u32[]{:S(2)}, u32[]{:S(2)}) %collective-permute-start.2) | collective-permute-done | bytes 131104 | tf_op jit(solution)/shard_map/ppermute | solution.py:32
  56.0 12.5 %collective-permute-start.4 = (bf16[256,1408]{1,0:T(8,128)(2,1)S(1)}, bf16[256,1408]{1,0:T(8,128)(2,1)S(1)}, u32[]{:S(2)}, u32[]{:S(2)}) collective-permute-start(bf16[256,1408]{1,0:T(8,128)(2,1)S(1)} %pad_maximum_fusion.4), channel_id=1, source_target_pairs={{0,96},{1,33},{32,64},{33,1},{64,32},{65,97},{96,0},{97,65},{2,98}... | collective-permute-start | bytes 2162696 | tf_op jit(solution)/shard_map/ppermute | solution.py:27
  68.5 1.9 %collective-permute-start.5 = (bf16[128,512]{1,0:T(8,128)(2,1)S(1)}, bf16[128,512]{1,0:T(8,128)(2,1)S(1)}, u32[]{:S(2)}, u32[]{:S(2)}) collective-permute-start(bf16[128,512]{1,0:T(8,128)(2,1)S(1)} %collective-permute-done.2), channel_id=1, source_target_pairs={{0,6},{1,11},{2,12},{3,9},{4,10},{5,15},{6,0},{7,13},{8,14},{9,3},... | collective-permute-start | bytes 393224 | tf_op jit(solution)/shard_map/ppermute | solution.py:42
  70.4 7.8 %collective-permute-done.5 = bf16[128,512]{1,0:T(8,128)(2,1)S(1)} collective-permute-done((bf16[128,512]{1,0:T(8,128)(2,1)S(1)}, bf16[128,512]{1,0:T(8,128)(2,1)S(1)}, u32[]{:S(2)}, u32[]{:S(2)}) %collective-permute-start.5) | collective-permute-done | bytes 131104 | tf_op jit(solution)/shard_map/ppermute | solution.py:42
  78.4 4.1 %collective-permute-done.4.y2 = bf16[256,1408]{1,0:T(8,128)(2,1)S(1)} collective-permute-done((bf16[256,1408]{1,0:T(8,128)(2,1)S(1)}, bf16[256,1408]{1,0:T(8,128)(2,1)S(1)}, u32[]{:S(2)}, u32[]{:S(2)}) %collective-permute-start.4) | collective-permute-done | bytes 720928 | tf_op jit(solution)/shard_map/ppermute | solution.py:27
  82.6 3.5 %collective-permute-start.6 = (bf16[384,1408]{1,0:T(8,128)(2,1)S(1)}, bf16[384,1408]{1,0:T(8,128)(2,1)S(1)}, u32[]{:S(2)}, u32[]{:S(2)}) collective-permute-start(bf16[384,1408]{1,0:T(8,128)(2,1)S(1)} %pad_maximum_fusion.1), channel_id=1, source_target_pairs={{0,128},{1,385},{128,0},{129,257},{256,384},{257,129},{384,256},{3... | collective-permute-start | bytes 3244040 | tf_op jit(solution)/shard_map/ppermute | solution.py:27
  86.2 1.9 %collective-permute-start.8 = (bf16[256,512]{1,0:T(8,128)(2,1)S(1)}, bf16[256,512]{1,0:T(8,128)(2,1)S(1)}, u32[]{:S(2)}, u32[]{:S(2)}) collective-permute-start(bf16[256,512]{1,0:T(8,128)(2,1)S(1)} %constant_dynamic-update-slice_fusion), channel_id=1, source_target_pairs={{0,14},{1,3},{2,4},{3,1},{4,2},{5,7},{6,8},{7,5},{8,6},{9,11},{10,... | collective-permute-start | bytes 786440 | tf_op jit(solution)/shard_map/ppermute | solution.py:42
  88.1 8.8 %collective-permute-done.8 = bf16[256,512]{1,0:T(8,128)(2,1)S(1)} collective-permute-done((bf16[256,512]{1,0:T(8,128)(2,1)S(1)}, bf16[256,512]{1,0:T(8,128)(2,1)S(1)}, u32[]{:S(2)}, u32[]{:S(2)}) %collective-permute-start.8) | collective-permute-done | bytes 262176 | tf_op jit(solution)/shard_map/ppermute | solution.py:42
  96.9 1.9 %collective-permute-start.9 = (bf16[512,512]{1,0:T(8,128)(2,1)S(1)}, bf16[512,512]{1,0:T(8,128)(2,1)S(1)}, u32[]{:S(2)}, u32[]{:S(2)}) collective-permute-start(bf16[512,512]{1,0:T(8,128)(2,1)S(1)} %constant_dynamic-update-slice_fusion.2.mine2_ref), channel_id=1, source_target_pairs={{0,2},{1,15},{2,0},{3,5},{4,6},{5,3},{6,4},{7,9},{8,10},{9,7},{10,... | collective-permute-start | bytes 1572872 | tf_op jit(solution)/shard_map/ppermute | solution.py:42
  98.8 4.1 %collective-permute-start.7 = (bf16[512,384]{1,0:T(8,128)(2,1)S(1)}, bf16[512,384]{1,0:T(8,128)(2,1)S(1)}, u32[]{:S(2)}, u32[]{:S(2)}) collective-permute-start(bf16[512,384]{1,0:T(8,128)(2,1)S(1)} %pad_maximum_fusion.6), channel_id=1, source_target_pairs={{0,32},{1,97},{32,0},{33,65},{64,96},{65,33},{96,64},{97,1},{2,34}... | collective-permute-start | bytes 1179656 | tf_op jit(solution)/shard_map/ppermute | solution.py:27
  103.0 10.6 %collective-permute-done.7.y3 = bf16[512,384]{1,0:T(8,128)(2,1)S(1)} collective-permute-done((bf16[512,384]{1,0:T(8,128)(2,1)S(1)}, bf16[512,384]{1,0:T(8,128)(2,1)S(1)}, u32[]{:S(2)}, u32[]{:S(2)}) %collective-permute-start.7) | collective-permute-done | bytes 393248 | tf_op jit(solution)/shard_map/ppermute | solution.py:27
  115.9 4.7 %collective-permute-start.12 = (bf16[768,1408]{1,0:T(8,128)(2,1)}, bf16[768,1408]{1,0:T(8,128)(2,1)}, u32[]{:S(2)}, u32[]{:S(2)}) collective-permute-start(bf16[768,1408]{1,0:T(8,128)(2,1)} %pad_maximum_fusion), channel_id=1, source_target_pairs={{0,384},{1,129},{128,256},{129,1},{256,128},{257,385},{384,0},{385... | collective-permute-start | bytes 6488072 | tf_op jit(solution)/shard_map/ppermute | solution.py:27
  122.2 2.0 %pad_maximum_fusion.3 = bf16[1024,384]{1,0:T(8,128)(2,1)} fusion(bf16[512,384]{1,0:T(8,128)(2,1)S(1)} %collective-permute-done.7.y3, bf16[512,384]{1,0:T(8,128)(2,1)} %copy-done.7), kind=kLoop, calls=%fused_computation.5 | loop fusion | flops 1572864 | bytes 1572864 | tf_op jit(solution)/shard_map/concatenate | solution.py:239
  124.2 2.0 %collective-permute-start.13 = (bf16[1024,384]{1,0:T(8,128)(2,1)}, bf16[1024,384]{1,0:T(8,128)(2,1)}, u32[]{:S(2)}, u32[]{:S(2)}) collective-permute-start(bf16[1024,384]{1,0:T(8,128)(2,1)} %pad_maximum_fusion.3), channel_id=1, source_target_pairs={{0,96},{1,33},{32,64},{33,1},{64,32},{65,97},{96,0},{97,65},{2,98}... | collective-permute-start | bytes 2359304 | tf_op jit(solution)/shard_map/ppermute | solution.py:27
  126.1 1.9 %collective-permute-start.10 = (bf16[512,512]{1,0:T(8,128)(2,1)}, bf16[512,512]{1,0:T(8,128)(2,1)}, u32[]{:S(2)}, u32[]{:S(2)}) collective-permute-start(bf16[512,512]{1,0:T(8,128)(2,1)} %copy-done.2), channel_id=1, source_target_pairs={{0,1},{1,0},{2,3},{3,2},{4,5},{5,4},{6,7},{7,6},{8,9},{9,8},{10,11... | collective-permute-start | bytes 1572872 | tf_op jit(solution)/shard_map/ppermute | solution.py:243
  128.1 2.4 %collective-permute-start.11 = (bf16[512,512]{1,0:T(8,128)(2,1)}, bf16[512,512]{1,0:T(8,128)(2,1)}, u32[]{:S(2)}, u32[]{:S(2)}) collective-permute-start(bf16[512,512]{1,0:T(8,128)(2,1)} %copy-done.4), channel_id=1, source_target_pairs={{0,1},{1,0},{2,3},{3,2},{4,5},{5,4},{6,7},{7,6},{8,9},{9,8},{10,11... | collective-permute-start | bytes 1572872 | tf_op jit(solution)/shard_map/ppermute | solution.py:243
  134.4 4.7 %shard_map.28 = (bf16[512,2048]{1,0:T(8,128)(2,1)S(1)}, f32[512,128]{1,0:T(8,128)S(1)}) custom-call(s32[16]{0:T(128)S(1)} %compare_select_fusion.3.place_ref, bf16[512,512]{1,0:T(8,128)(2,1)S(1)} %copy-done.3, bf16[512,512]{1,0:T(8,128)(2,1)S(1)} %copy-done.5, bf16[512,512]{1,0:T(8,128)(2,1)} %collective-permute-done.10.other2_ref, ...), custom_call_target="tpu_custom_call" | custom-call | flops 131072 | bytes 65536 | tf_op jit(solution)/shard_map/pallas_call | solution.py:90
  139.1 4.2 %shard_map.29 = (f32[512,1792]{1,0:T(8,128)S(1)}, f32[8,1792]{1,0:T(8,128)S(1)}, f32[8,1792]{1,0:T(8,128)S(1)}) custom-call(bf16[512,2048]{1,0:T(8,128)(2,1)S(1)} %get-tuple-element.29.slab_ref, bf16[128,1792]{1,0:T(8,128)(2,1)S(1)} %slice.41.own, bf16[128,1792]{1,0:T(8,128)(2,1)S(1)} %collective-permute-done.x1, bf16[256,1792]{1,0:T(8,128)(2,1)S(1)} %copy-done.1, ...), custom_call_target="tpu_custom_call" | custom-call | flops 29360128 | bytes 57344 | tf_op jit(solution)/shard_map/pallas_call | solution.py:90
  143.3 5.3 %collective-permute-done.13.y4 = bf16[1024,384]{1,0:T(8,128)(2,1)} collective-permute-done((bf16[1024,384]{1,0:T(8,128)(2,1)}, bf16[1024,384]{1,0:T(8,128)(2,1)}, u32[]{:S(2)}, u32[]{:S(2)}) %collective-permute-start.13) | collective-permute-done | bytes 786464 | tf_op jit(solution)/shard_map/ppermute | solution.py:27
  148.7 6.0 %shard_map.30 = bf16[512,1792]{1,0:T(8,128)(2,1)} custom-call(bf16[512,2048]{1,0:T(8,128)(2,1)S(1)} %get-tuple-element.29.slab_ref, f32[512,128]{1,0:T(8,128)S(1)} %get-tuple-element.30.sums_ref, f32[512,1792]{1,0:T(8,128)S(1)} %get-tuple-element.34.acc_ref, f32[8,1792]{1,0:T(8,128)S(1)} %get-tuple-element.35.pivot_ref, ...), custom_call_target="tpu_custom_call" | custom-call | flops 29360128 | bytes 57344 | tf_op jit(solution)/shard_map/pallas_call | solution.py:90
  (56 shorter events, 12.4 us)
Async XLA Ops:
  31.1 22.9 %copy-start.6 = (bf16[128,2304]{1,0:T(8,128)(2,1)}, bf16[128,2304]{1,0:T(8,128)(2,1)S(1)}, u32[]{:S(2)}) copy-start(bf16[128,2304]{1,0:T(8,128)(2,1)S(1)} %all_to_all.14) | copy-start | bytes 1769476
  31.1 22.8 %collective-permute-start = (bf16[128,1792]{1,0:T(8,128)(2,1)S(1)}, bf16[128,1792]{1,0:T(8,128)(2,1)S(1)}, u32[]{:S(2)}, u32[]{:S(2)}) collective-permute-start(bf16[128,1792]{1,0:T(8,128)(2,1)S(1)} %slice.41.own), channel_id=1, source_target_pairs={{0,128},{1,385},{128,0},{129,257},{256,384},{257,129},{384,256},{3... | collective-permute-start | bytes 1376264 | tf_op jit(solution)/shard_map/ppermute | solution.py:27
  34.3 19.7 %collective-permute-start.1 = (bf16[128,1408]{1,0:T(8,128)(2,1)S(1)}, bf16[128,1408]{1,0:T(8,128)(2,1)S(1)}, u32[]{:S(2)}, u32[]{:S(2)}) collective-permute-start(bf16[128,1408]{1,0:T(8,128)(2,1)S(1)} %slice.42), channel_id=1, source_target_pairs={{0,32},{1,97},{32,0},{33,65},{64,96},{65,33},{96,64},{97,1},{2,34}... | collective-permute-start | bytes 1081352 | tf_op jit(solution)/shard_map/ppermute | solution.py:27
  38.8 15.1 %collective-permute-start.2 = (bf16[128,512]{1,0:T(8,128)(2,1)S(1)}, bf16[128,512]{1,0:T(8,128)(2,1)S(1)}, u32[]{:S(2)}, u32[]{:S(2)}) collective-permute-start(bf16[128,512]{1,0:T(8,128)(2,1)S(1)} %slice.43), channel_id=1, source_target_pairs={{0,0},{1,32},{2,64},{3,96},{4,128},{5,160},{6,192},{7,224},{8,256}... | collective-permute-start | bytes 393224 | tf_op jit(solution)/shard_map/ppermute | solution.py:32
  54.0 24.3 %collective-permute-start.3 = (bf16[256,1792]{1,0:T(8,128)(2,1)S(1)}, bf16[256,1792]{1,0:T(8,128)(2,1)S(1)}, u32[]{:S(2)}, u32[]{:S(2)}) collective-permute-start(bf16[256,1792]{1,0:T(8,128)(2,1)S(1)} %pad_maximum_fusion.2), channel_id=1, source_target_pairs={{0,384},{1,129},{128,256},{129,1},{256,128},{257,385},{384,0},{385... | collective-permute-start | bytes 2752520 | tf_op jit(solution)/shard_map/ppermute | solution.py:27
  55.9 22.4 %slice-start = ((bf16[128,2304]{1,0:T(8,128)(2,1)}), bf16[128,384]{1,0:T(8,128)(2,1)S(1)}, s32[]{:S(2)}) async-start(bf16[128,2304]{1,0:T(8,128)(2,1)} %copy-done.6), calls=%async_computation.1 | async-start | bytes 196608 | tf_op jit(solution)/shard_map/slice | solution.py:231
  56.0 26.5 %collective-permute-start.4 = (bf16[256,1408]{1,0:T(8,128)(2,1)S(1)}, bf16[256,1408]{1,0:T(8,128)(2,1)S(1)}, u32[]{:S(2)}, u32[]{:S(2)}) collective-permute-start(bf16[256,1408]{1,0:T(8,128)(2,1)S(1)} %pad_maximum_fusion.4), channel_id=1, source_target_pairs={{0,96},{1,33},{32,64},{33,1},{64,32},{65,97},{96,0},{97,65},{2,98}... | collective-permute-start | bytes 2162696 | tf_op jit(solution)/shard_map/ppermute | solution.py:27
  68.5 9.8 %collective-permute-start.5 = (bf16[128,512]{1,0:T(8,128)(2,1)S(1)}, bf16[128,512]{1,0:T(8,128)(2,1)S(1)}, u32[]{:S(2)}, u32[]{:S(2)}) collective-permute-start(bf16[128,512]{1,0:T(8,128)(2,1)S(1)} %collective-permute-done.2), channel_id=1, source_target_pairs={{0,6},{1,11},{2,12},{3,9},{4,10},{5,15},{6,0},{7,13},{8,14},{9,3},... | collective-permute-start | bytes 393224 | tf_op jit(solution)/shard_map/ppermute | solution.py:42
  78.3 4.2 %copy-start = (bf16[256,1792]{1,0:T(8,128)(2,1)}, bf16[256,1792]{1,0:T(8,128)(2,1)S(1)}, u32[]{:S(2)}) copy-start(bf16[256,1792]{1,0:T(8,128)(2,1)S(1)} %collective-permute-done.3.x2) | copy-start | bytes 2752516
  78.4 35.1 %copy-start.7 = (bf16[512,384]{1,0:T(8,128)(2,1)}, bf16[512,384]{1,0:T(8,128)(2,1)S(1)}, u32[]{:S(2)}) copy-start(bf16[512,384]{1,0:T(8,128)(2,1)S(1)} %pad_maximum_fusion.6) | copy-start | bytes 1179652
  82.6 31.7 %collective-permute-start.6 = (bf16[384,1408]{1,0:T(8,128)(2,1)S(1)}, bf16[384,1408]{1,0:T(8,128)(2,1)S(1)}, u32[]{:S(2)}, u32[]{:S(2)}) collective-permute-start(bf16[384,1408]{1,0:T(8,128)(2,1)S(1)} %pad_maximum_fusion.1), channel_id=1, source_target_pairs={{0,128},{1,385},{128,0},{129,257},{256,384},{257,129},{384,256},{3... | collective-permute-start | bytes 3244040 | tf_op jit(solution)/shard_map/ppermute | solution.py:27
  86.2 10.7 %collective-permute-start.8 = (bf16[256,512]{1,0:T(8,128)(2,1)S(1)}, bf16[256,512]{1,0:T(8,128)(2,1)S(1)}, u32[]{:S(2)}, u32[]{:S(2)}) collective-permute-start(bf16[256,512]{1,0:T(8,128)(2,1)S(1)} %constant_dynamic-update-slice_fusion), channel_id=1, source_target_pairs={{0,14},{1,3},{2,4},{3,1},{4,2},{5,7},{6,8},{7,5},{8,6},{9,11},{10,... | collective-permute-start | bytes 786440 | tf_op jit(solution)/shard_map/ppermute | solution.py:42
  96.9 16.6 %copy-start.2 = (bf16[512,512]{1,0:T(8,128)(2,1)}, bf16[512,512]{1,0:T(8,128)(2,1)S(1)}, u32[]{:S(2)}) copy-start(bf16[512,512]{1,0:T(8,128)(2,1)S(1)} %constant_dynamic-update-slice_fusion.2.mine2_ref) | copy-start | bytes 1572868
  96.9 16.6 %collective-permute-start.9 = (bf16[512,512]{1,0:T(8,128)(2,1)S(1)}, bf16[512,512]{1,0:T(8,128)(2,1)S(1)}, u32[]{:S(2)}, u32[]{:S(2)}) collective-permute-start(bf16[512,512]{1,0:T(8,128)(2,1)S(1)} %constant_dynamic-update-slice_fusion.2.mine2_ref), channel_id=1, source_target_pairs={{0,2},{1,15},{2,0},{3,5},{4,6},{5,3},{6,4},{7,9},{8,10},{9,7},{10,... | collective-permute-start | bytes 1572872 | tf_op jit(solution)/shard_map/ppermute | solution.py:42
  98.8 14.7 %collective-permute-start.7 = (bf16[512,384]{1,0:T(8,128)(2,1)S(1)}, bf16[512,384]{1,0:T(8,128)(2,1)S(1)}, u32[]{:S(2)}, u32[]{:S(2)}) collective-permute-start(bf16[512,384]{1,0:T(8,128)(2,1)S(1)} %pad_maximum_fusion.6), channel_id=1, source_target_pairs={{0,32},{1,97},{32,0},{33,65},{64,96},{65,33},{96,64},{97,1},{2,34}... | collective-permute-start | bytes 1179656 | tf_op jit(solution)/shard_map/ppermute | solution.py:27
  113.5 0.8 copy-start.4
  115.9 32.8 %collective-permute-start.12 = (bf16[768,1408]{1,0:T(8,128)(2,1)}, bf16[768,1408]{1,0:T(8,128)(2,1)}, u32[]{:S(2)}, u32[]{:S(2)}) collective-permute-start(bf16[768,1408]{1,0:T(8,128)(2,1)} %pad_maximum_fusion), channel_id=1, source_target_pairs={{0,384},{1,129},{128,256},{129,1},{256,128},{257,385},{384,0},{385... | collective-permute-start | bytes 6488072 | tf_op jit(solution)/shard_map/ppermute | solution.py:27
  124.2 24.5 %collective-permute-start.13 = (bf16[1024,384]{1,0:T(8,128)(2,1)}, bf16[1024,384]{1,0:T(8,128)(2,1)}, u32[]{:S(2)}, u32[]{:S(2)}) collective-permute-start(bf16[1024,384]{1,0:T(8,128)(2,1)} %pad_maximum_fusion.3), channel_id=1, source_target_pairs={{0,96},{1,33},{32,64},{33,1},{64,32},{65,97},{96,0},{97,65},{2,98}... | collective-permute-start | bytes 2359304 | tf_op jit(solution)/shard_map/ppermute | solution.py:27
  126.1 5.8 %collective-permute-start.10 = (bf16[512,512]{1,0:T(8,128)(2,1)}, bf16[512,512]{1,0:T(8,128)(2,1)}, u32[]{:S(2)}, u32[]{:S(2)}) collective-permute-start(bf16[512,512]{1,0:T(8,128)(2,1)} %copy-done.2), channel_id=1, source_target_pairs={{0,1},{1,0},{2,3},{3,2},{4,5},{5,4},{6,7},{7,6},{8,9},{9,8},{10,11... | collective-permute-start | bytes 1572872 | tf_op jit(solution)/shard_map/ppermute | solution.py:243
  128.1 4.3 %collective-permute-start.11 = (bf16[512,512]{1,0:T(8,128)(2,1)}, bf16[512,512]{1,0:T(8,128)(2,1)}, u32[]{:S(2)}, u32[]{:S(2)}) collective-permute-start(bf16[512,512]{1,0:T(8,128)(2,1)} %copy-done.4), channel_id=1, source_target_pairs={{0,1},{1,0},{2,3},{3,2},{4,5},{5,4},{6,7},{7,6},{8,9},{9,8},{10,11... | collective-permute-start | bytes 1572872 | tf_op jit(solution)/shard_map/ppermute | solution.py:243
  131.9 7.2 %copy-start.1 = (bf16[256,1792]{1,0:T(8,128)(2,1)S(1)}, bf16[256,1792]{1,0:T(8,128)(2,1)}, u32[]{:S(2)}) copy-start(bf16[256,1792]{1,0:T(8,128)(2,1)} %copy-done) | copy-start | bytes 2752516
  132.3 1.0 copy-start.3
  133.4 1.0 copy-start.5
